TPU v7x, 32 devices: a whole 2x2x4 slice. The times are simulated.
32 devices in a mesh: rep: 2 (over y), grp: 16 (over z, x, core).
Axes of the slice: x: 2, y: 2, z: 4, core: 2. Of those that a mesh axis runs over, the one named last changes fastest.
Arguments:
- tokens: bfloat16 [2, 256, 7168], P(None, ('rep', 'grp')), parts along dimension 1, may hold values from -6 to 6
- expert_ids: int32 [2, 256, 4], P(None, ('rep', 'grp')), parts along dimension 1, may hold values from 0 to 15, as said below
- gate_weights: bfloat16 [2, 256, 4], P(None, ('rep', 'grp')), parts along dimension 1, may hold values from 0.099609375 to 1
- w_gate: bfloat16 [16, 7168, 2048], P('grp'), may hold values from -0.0625 to 0.0625
- w_up: bfloat16 [16, 7168, 2048], P('grp'), may hold values from -0.0625 to 0.0625
- w_down: bfloat16 [16, 2048, 7168], P('grp'), may hold values from -0.125 to 0.125
Outputs:
- mixed: bfloat16 [2, 256, 7168], P(None, ('rep', 'grp')), parts along dimension 1
There are 2 independent parts, one for each index of `rep`. A program takes and returns all parts, laid end to end along the dimension named above; an argument that names none is the same for every part. Nothing has to cross between parts.
Inputs may be any that keep to these rules, and one draw needn't show every extreme that they name: `expert_ids`: A row's 4 ids are distinct and lie in two to four groups. In each micro-batch, at most 4 of one device's 8 rows route to any one group, and on every device some group receives exactly 4 of them.
All inputs are finite; a program needn't handle non-finite values.
Results may differ from a plain program's by a relative error of at most 0.006.
Values may be sent and summed in bfloat16 or wider, within the bound.
No kernel may reach another device: no remote copies, remote signals or barrier semaphores. Data moves between devices by JAX's collectives and lax.ppermute only.
A program may use at most 192 MiB of HBM per device.

v0:
```python
import jax
import jax.numpy as jnp
from jax import lax
from jax.sharding import PartitionSpec as P

GROUPS = 8
EXP_GRP = 2


def passed_along(shard, axis, by):
    size = lax.axis_size(axis)
    return lax.ppermute(shard, axis, [(i, (i + by) % size) for i in range(size)])


def swapped(shard, axis, bit):
    return lax.ppermute(shard, axis, [(i, i ^ 1 << bit) for i in range(lax.axis_size(axis))])


def body(tokens, expert_ids, gate_weights, w_gate, w_up, w_down):
    devices = lax.axis_size("grp")
    gsize = devices // GROUPS
    in_bits = gsize.bit_length() - 1
    rank = lax.axis_index("grp")
    group_me = rank // gsize
    my_expert = rank % gsize // (gsize // EXP_GRP)
    select = (jnp.arange(EXP_GRP, dtype=jnp.int32) == my_expert).astype(jnp.float32)
    rows = tokens.shape[1]
    cap = rows // 2
    width = tokens.shape[2]
    positions = jnp.arange(GROUPS, dtype=jnp.int32)
    targets = (group_me + positions) % GROUPS
    expert_grid = targets[:, None] * EXP_GRP + jnp.arange(EXP_GRP, dtype=jnp.int32)[None, :]
    slot_grid = jnp.arange(cap, dtype=jnp.int32)
    outputs = []
    for batch in range(tokens.shape[0]):
        x_rows = tokens[batch]
        ids = expert_ids[batch]
        weights = gate_weights[batch]
        owner = ids // EXP_GRP
        routed = jnp.any(owner[:, None, :] == targets[None, :, None], axis=-1)
        routed_int = routed.astype(jnp.int32)
        slots = jnp.cumsum(routed_int, axis=0) - routed_int
        dispatch = jnp.logical_and(routed[:, :, None], slots[:, :, None] == slot_grid).astype(
            jnp.bfloat16
        )
        local_weight = jnp.sum(
            jnp.where(
                ids[:, None, None, :] == expert_grid[None, :, :, None],
                weights[:, None, None, :],
                jnp.zeros((), jnp.bfloat16),
            ),
            axis=-1,
        )
        bucket = jnp.einsum(
            "rtc,rd->tcd", dispatch, x_rows, preferred_element_type=jnp.float32
        ).astype(jnp.bfloat16)
        bucket_weight = jnp.einsum(
            "rtc,rte->tce", dispatch, local_weight, preferred_element_type=jnp.float32
        ).astype(jnp.bfloat16)
        rows_list = [bucket[0]]
        weight_list = [bucket_weight[0]]
        for offset in range(1, GROUPS):
            got_rows, got_weight = passed_along(
                (bucket[offset], bucket_weight[offset]), "grp", offset * gsize
            )
            rows_list.append(got_rows)
            weight_list.append(got_weight)
        arrived = jnp.stack(rows_list)
        arrived_weight = jnp.stack(weight_list)
        all_rows = arrived.reshape(GROUPS * cap, width)
        all_weight = arrived_weight.reshape(GROUPS * cap, EXP_GRP)
        for bit in range(in_bits):
            other_rows, other_weight = swapped((all_rows, all_weight), "grp", bit)
            lower = rank // (1 << bit) % 2 == 0
            all_rows = jnp.where(
                lower,
                jnp.concatenate([all_rows, other_rows]),
                jnp.concatenate([other_rows, all_rows]),
            )
            all_weight = jnp.where(
                lower,
                jnp.concatenate([all_weight, other_weight]),
                jnp.concatenate([other_weight, all_weight]),
            )
        column = jnp.sum(all_weight.astype(jnp.float32) * select[None, :], axis=1, keepdims=True)
        gate = jnp.dot(all_rows, w_gate[0], preferred_element_type=jnp.float32)
        up_val = jnp.dot(all_rows, w_up[0], preferred_element_type=jnp.float32)
        hidden = (jax.nn.silu(gate) * up_val * column).astype(jnp.bfloat16)
        partial_sum = jnp.dot(hidden, w_down[0], preferred_element_type=jnp.float32)
        for bit in reversed(range(in_bits)):
            half = partial_sum.shape[0] // 2
            lower = rank // (1 << bit) % 2 == 0
            kept = jnp.where(lower, partial_sum[:half], partial_sum[half:])
            away = jnp.where(lower, partial_sum[half:], partial_sum[:half]).astype(jnp.bfloat16)
            got = swapped(away, "grp", bit)
            kept_rounded = lax.optimization_barrier(kept.astype(jnp.bfloat16))
            partial_sum = kept_rounded.astype(jnp.float32) + got.astype(jnp.float32)
        group_out = partial_sum.astype(jnp.bfloat16).reshape(GROUPS, cap, width)
        back_list = [group_out[0]]
        for offset in range(1, GROUPS):
            back_list.append(passed_along(group_out[offset], "grp", devices - offset * gsize))
        returned = jnp.stack(back_list)
        mixed = jnp.einsum("rtc,tcd->rd", dispatch, returned, preferred_element_type=jnp.float32)
        outputs.append(mixed.astype(jnp.bfloat16))
    return jnp.stack(outputs)


def solution(mesh):
    return jax.shard_map(
        body,
        mesh=mesh,
        in_specs=(
            P(None, ("rep", "grp"), None),
            P(None, ("rep", "grp"), None),
            P(None, ("rep", "grp"), None),
            P("grp", None, None),
            P("grp", None, None),
            P("grp", None, None),
        ),
        out_specs=P(None, ("rep", "grp"), None),
        check_vma=False,
    )
```

profile of v0, /device:TPU:12, one launch (start us, length us, event | category | flops | bytes accessed | tf_op | source)
XLA Modules:
  0.0 196.3 jit_solution(17935867089002220094)
XLA Ops:
  7.5 2.7 %collective-permute-start.3 = (bf16[4,7168]{1,0:T(4,128)(2,1)S(1)}, bf16[4,7168]{1,0:T(4,128)(2,1)S(1)}, u32[]{:S(2)}, u32[]{:S(2)}) collective-permute-start(bf16[4,7168]{1,0:T(4,128)(2,1)S(1)} %bitcast.227), channel_id=1, source_target_pairs={{0,8},{1,9},{2,10},{3,11},{4,12},{5,13},{6,14},{7,15},{8,0},{9,1},... | collective-permute-start | bytes 172040 | tf_op jit(solution)/shard_map/ppermute | solution.py:12
  13.1 2.0 %collective-permute-done.8 = bf16[4,2]{0,1:T(2,128)(2,1)S(1)} collective-permute-done((bf16[4,2]{0,1:T(2,128)(2,1)S(1)}, bf16[4,2]{0,1:T(2,128)(2,1)S(1)}, u32[]{:S(2)}, u32[]{:S(2)}) %collective-permute-start.8) | collective-permute-done | bytes 48 | tf_op jit(solution)/shard_map/ppermute | solution.py:12
  15.9 3.0 %collective-permute-done.9 = bf16[4,2]{0,1:T(2,128)(2,1)S(1)} collective-permute-done((bf16[4,2]{0,1:T(2,128)(2,1)S(1)}, bf16[4,2]{0,1:T(2,128)(2,1)S(1)}, u32[]{:S(2)}, u32[]{:S(2)}) %collective-permute-start.9) | collective-permute-done | bytes 48 | tf_op jit(solution)/shard_map/ppermute | solution.py:12
  19.4 4.8 %collective-permute-done.10 = bf16[4,2]{0,1:T(2,128)(2,1)S(1)} collective-permute-done((bf16[4,2]{0,1:T(2,128)(2,1)S(1)}, bf16[4,2]{0,1:T(2,128)(2,1)S(1)}, u32[]{:S(2)}, u32[]{:S(2)}) %collective-permute-start.10) | collective-permute-done | bytes 48 | tf_op jit(solution)/shard_map/ppermute | solution.py:12
  24.2 2.1 %collective-permute-start.11 = (bf16[4,2]{0,1:T(2,128)(2,1)S(1)}, bf16[4,2]{0,1:T(2,128)(2,1)S(1)}, u32[]{:S(2)}, u32[]{:S(2)}) collective-permute-start(bf16[4,2]{0,1:T(2,128)(2,1)S(1)} %get-tuple-element.56), channel_id=1, source_target_pairs={{0,8},{1,9},{2,10},{3,11},{4,12},{5,13},{6,14},{7,15},{8,0},{9,1},... | collective-permute-start | bytes 56 | tf_op jit(solution)/shard_map/ppermute | solution.py:12
  26.4 2.3 %collective-permute-done.11 = bf16[4,2]{0,1:T(2,128)(2,1)S(1)} collective-permute-done((bf16[4,2]{0,1:T(2,128)(2,1)S(1)}, bf16[4,2]{0,1:T(2,128)(2,1)S(1)}, u32[]{:S(2)}, u32[]{:S(2)}) %collective-permute-start.11) | collective-permute-done | bytes 48 | tf_op jit(solution)/shard_map/ppermute | solution.py:12
  29.6 3.5 %collective-permute-done.12 = bf16[4,2]{0,1:T(2,128)(2,1)S(1)} collective-permute-done((bf16[4,2]{0,1:T(2,128)(2,1)S(1)}, bf16[4,2]{0,1:T(2,128)(2,1)S(1)}, u32[]{:S(2)}, u32[]{:S(2)}) %collective-permute-start.12) | collective-permute-done | bytes 48 | tf_op jit(solution)/shard_map/ppermute | solution.py:12
  33.1 3.8 %collective-permute-start.13 = (bf16[4,2]{0,1:T(2,128)(2,1)S(1)}, bf16[4,2]{0,1:T(2,128)(2,1)S(1)}, u32[]{:S(2)}, u32[]{:S(2)}) collective-permute-start(bf16[4,2]{0,1:T(2,128)(2,1)S(1)} %get-tuple-element.54), channel_id=1, source_target_pairs={{0,12},{1,13},{2,14},{3,15},{4,0},{5,1},{6,2},{7,3},{8,4},{9,5},{1... | collective-permute-start | bytes 56 | tf_op jit(solution)/shard_map/ppermute | solution.py:12
  38.2 2.2 %collective-permute-start.14 = (bf16[4,2]{0,1:T(2,128)(2,1)S(1)}, bf16[4,2]{0,1:T(2,128)(2,1)S(1)}, u32[]{:S(2)}, u32[]{:S(2)}) collective-permute-start(bf16[4,2]{0,1:T(2,128)(2,1)S(1)} %get-tuple-element.53), channel_id=1, source_target_pairs={{0,14},{1,15},{2,0},{3,1},{4,2},{5,3},{6,4},{7,5},{8,6},{9,7},{10,... | collective-permute-start | bytes 56 | tf_op jit(solution)/shard_map/ppermute | solution.py:12
  43.5 2.9 %collective-permute-done.32 = bf16[4,2]{0,1:T(2,128)(2,1)S(1)} collective-permute-done((bf16[4,2]{0,1:T(2,128)(2,1)S(1)}, bf16[4,2]{0,1:T(2,128)(2,1)S(1)}, u32[]{:S(2)}, u32[]{:S(2)}) %collective-permute-start.32) | collective-permute-done | bytes 48 | tf_op jit(solution)/shard_map/ppermute | solution.py:12
  47.2 4.5 %collective-permute-done.33 = bf16[4,2]{0,1:T(2,128)(2,1)S(1)} collective-permute-done((bf16[4,2]{0,1:T(2,128)(2,1)S(1)}, bf16[4,2]{0,1:T(2,128)(2,1)S(1)}, u32[]{:S(2)}, u32[]{:S(2)}) %collective-permute-start.33) | collective-permute-done | bytes 48 | tf_op jit(solution)/shard_map/ppermute | solution.py:12
  52.5 4.6 %collective-permute-done.34 = bf16[4,2]{0,1:T(2,128)(2,1)S(1)} collective-permute-done((bf16[4,2]{0,1:T(2,128)(2,1)S(1)}, bf16[4,2]{0,1:T(2,128)(2,1)S(1)}, u32[]{:S(2)}, u32[]{:S(2)}) %collective-permute-start.34) | collective-permute-done | bytes 48 | tf_op jit(solution)/shard_map/ppermute | solution.py:12
  57.1 2.1 %collective-permute-start.35 = (bf16[4,2]{0,1:T(2,128)(2,1)S(1)}, bf16[4,2]{0,1:T(2,128)(2,1)S(1)}, u32[]{:S(2)}, u32[]{:S(2)}) collective-permute-start(bf16[4,2]{0,1:T(2,128)(2,1)S(1)} %get-tuple-element.48), channel_id=1, source_target_pairs={{0,8},{1,9},{2,10},{3,11},{4,12},{5,13},{6,14},{7,15},{8,0},{9,1},... | collective-permute-start | bytes 56 | tf_op jit(solution)/shard_map/ppermute | solution.py:12
  59.3 2.3 %collective-permute-done.35 = bf16[4,2]{0,1:T(2,128)(2,1)S(1)} collective-permute-done((bf16[4,2]{0,1:T(2,128)(2,1)S(1)}, bf16[4,2]{0,1:T(2,128)(2,1)S(1)}, u32[]{:S(2)}, u32[]{:S(2)}) %collective-permute-start.35) | collective-permute-done | bytes 48 | tf_op jit(solution)/shard_map/ppermute | solution.py:12
  62.9 3.1 %collective-permute-done.36 = bf16[4,2]{0,1:T(2,128)(2,1)S(1)} collective-permute-done((bf16[4,2]{0,1:T(2,128)(2,1)S(1)}, bf16[4,2]{0,1:T(2,128)(2,1)S(1)}, u32[]{:S(2)}, u32[]{:S(2)}) %collective-permute-start.36) | collective-permute-done | bytes 48 | tf_op jit(solution)/shard_map/ppermute | solution.py:12
  66.0 2.3 %collective-permute-start.4 = (bf16[4,7168]{1,0:T(4,128)(2,1)S(1)}, bf16[4,7168]{1,0:T(4,128)(2,1)S(1)}, u32[]{:S(2)}, u32[]{:S(2)}) collective-permute-start(bf16[4,7168]{1,0:T(4,128)(2,1)S(1)} %bitcast.235), channel_id=1, source_target_pairs={{0,10},{1,11},{2,12},{3,13},{4,14},{5,15},{6,0},{7,1},{8,2},{9,3},... | collective-permute-start | bytes 172040 | tf_op jit(solution)/shard_map/ppermute | solution.py:12
  68.3 2.5 %collective-permute-start.5 = (bf16[4,7168]{1,0:T(4,128)(2,1)S(1)}, bf16[4,7168]{1,0:T(4,128)(2,1)S(1)}, u32[]{:S(2)}, u32[]{:S(2)}) collective-permute-start(bf16[4,7168]{1,0:T(4,128)(2,1)S(1)} %bitcast.234), channel_id=1, source_target_pairs={{0,12},{1,13},{2,14},{3,15},{4,0},{5,1},{6,2},{7,3},{8,4},{9,5},{1... | collective-permute-start | bytes 172040 | tf_op jit(solution)/shard_map/ppermute | solution.py:12
  72.8 3.3 %collective-permute-start.38 = (bf16[4,2]{0,1:T(2,128)(2,1)S(1)}, bf16[4,2]{0,1:T(2,128)(2,1)S(1)}, u32[]{:S(2)}, u32[]{:S(2)}) collective-permute-start(bf16[4,2]{0,1:T(2,128)(2,1)S(1)} %get-tuple-element.45), channel_id=1, source_target_pairs={{0,14},{1,15},{2,0},{3,1},{4,2},{5,3},{6,4},{7,5},{8,6},{9,7},{10,... | collective-permute-start | bytes 56 | tf_op jit(solution)/shard_map/ppermute | solution.py:12
  77.3 3.2 %collective-permute-start.26 = (bf16[4,7168]{1,0:T(4,128)(2,1)S(1)}, bf16[4,7168]{1,0:T(4,128)(2,1)S(1)}, u32[]{:S(2)}, u32[]{:S(2)}) collective-permute-start(bf16[4,7168]{1,0:T(4,128)(2,1)S(1)} %bitcast.222), channel_id=1, source_target_pairs={{0,6},{1,7},{2,8},{3,9},{4,10},{5,11},{6,12},{7,13},{8,14},{9,15},... | collective-permute-start | bytes 172040 | tf_op jit(solution)/shard_map/ppermute | solution.py:12
  87.0 2.9 %collective-permute-start.28 = (bf16[4,7168]{1,0:T(4,128)(2,1)S(1)}, bf16[4,7168]{1,0:T(4,128)(2,1)S(1)}, u32[]{:S(2)}, u32[]{:S(2)}) collective-permute-start(bf16[4,7168]{1,0:T(4,128)(2,1)S(1)} %bitcast.220), channel_id=1, source_target_pairs={{0,10},{1,11},{2,12},{3,13},{4,14},{5,15},{6,0},{7,1},{8,2},{9,3},... | collective-permute-start | bytes 172040 | tf_op jit(solution)/shard_map/ppermute | solution.py:12
  91.9 2.9 %collective-permute-done.28 = bf16[4,7168]{1,0:T(4,128)(2,1)S(1)} collective-permute-done((bf16[4,7168]{1,0:T(4,128)(2,1)S(1)}, bf16[4,7168]{1,0:T(4,128)(2,1)S(1)}, u32[]{:S(2)}, u32[]{:S(2)}) %collective-permute-start.28) | collective-permute-done | bytes 57376 | tf_op jit(solution)/shard_map/ppermute | solution.py:12
  97.3 12.0 %fusion.6 = f32[64,2048]{1,0:T(8,128)S(1)} fusion(bf16[1,7168,2048]{2,1,0:T(8,128)(2,1)} %param.10, bf16[32,7168]{1,0:T(8,128)(2,1)S(1)} %collective-permute-done.7, bf16[32,7168]{1,0:T(8,128)(2,1)S(1)} %reshape.191, pred[]{:T(512)S(6)} %eq.104), kind=kOutput, calls=%fused_computation.6 | convolution fusion | flops 1883176960 | bytes 30801920 | tf_op jit(solution)/shard_map/dot_general | solution.py:87
  109.3 20.8 %fusion.2 = bf16[64,7168]{1,0:T(8,128)(2,1)S(1)} fusion(bf16[1,2048,7168]{2,1,0:T(8,128)(2,1)} %param.11, f32[64,2048]{1,0:T(8,128)S(1)} %fusion.6, bf16[1,7168,2048]{2,1,0:T(8,128)(2,1)} %param.9, f32[64]{0:T(128)S(1)} %get-tuple-element.7, bf16[32,7168]{1,0:T(8,128)(2,1)S(1)} %collective-permute-done.7, bf16[32,7168]{1,0:T(8,128)(2,1)S(1)} %reshape.191, ...), kind=kOutput, calls=%fused_computation.2 | convolution fusion | flops 3763142656 | bytes 61079808 | tf_op jit(solution)/shard_map/dot_general | solution.py:89
  130.8 12.0 %fusion.4 = f32[64,2048]{1,0:T(8,128)S(1)} fusion(bf16[1,7168,2048]{2,1,0:T(8,128)(2,1)} %param.10, bf16[32,7168]{1,0:T(8,128)(2,1)S(1)} %collective-permute-done.31, bf16[32,7168]{1,0:T(8,128)(2,1)S(1)} %reshape.193, pred[]{:T(512)S(6)} %eq.104), kind=kOutput, calls=%fused_computation.4 | convolution fusion | flops 1883176960 | bytes 30801920 | tf_op jit(solution)/shard_map/dot_general | solution.py:87
  142.8 20.8 %fusion = bf16[64,7168]{1,0:T(8,128)(2,1)S(1)} fusion(bf16[1,2048,7168]{2,1,0:T(8,128)(2,1)} %param.11, f32[64,2048]{1,0:T(8,128)S(1)} %fusion.4, bf16[1,7168,2048]{2,1,0:T(8,128)(2,1)} %param.9, f32[64]{0:T(128)S(1)} %get-tuple-element.8, bf16[32,7168]{1,0:T(8,128)(2,1)S(1)} %collective-permute-done.31, bf16[32,7168]{1,0:T(8,128)(2,1)S(1)} %reshape.193, ...), kind=kOutput, calls=%fused_computation | convolution fusion | flops 3763142656 | bytes 61079808 | tf_op jit(solution)/shard_map/dot_general | solution.py:89
  165.2 2.2 %collective-permute-start.17 = (bf16[4,7168]{1,0:T(4,128)(2,1)S(1)}, bf16[4,7168]{1,0:T(4,128)(2,1)S(1)}, u32[]{:S(2)}, u32[]{:S(2)}) collective-permute-start(bf16[4,7168]{1,0:T(4,128)(2,1)S(1)} %get-tuple-element.21), channel_id=1, source_target_pairs={{0,14},{1,15},{2,0},{3,1},{4,2},{5,3},{6,4},{7,5},{8,6},{9,7},{10,... | collective-permute-start | bytes 172040 | tf_op jit(solution)/shard_map/ppermute | solution.py:12
  167.7 3.5 %collective-permute-start.18 = (bf16[4,7168]{1,0:T(4,128)(2,1)S(1)}, bf16[4,7168]{1,0:T(4,128)(2,1)S(1)}, u32[]{:S(2)}, u32[]{:S(2)}) collective-permute-start(bf16[4,7168]{1,0:T(4,128)(2,1)S(1)} %get-tuple-element.20), channel_id=1, source_target_pairs={{0,12},{1,13},{2,14},{3,15},{4,0},{5,1},{6,2},{7,3},{8,4},{9,5},{1... | collective-permute-start | bytes 172040 | tf_op jit(solution)/shard_map/ppermute | solution.py:12
  171.2 3.3 %collective-permute-start.21 = (bf16[4,7168]{1,0:T(4,128)(2,1)S(1)}, bf16[4,7168]{1,0:T(4,128)(2,1)S(1)}, u32[]{:S(2)}, u32[]{:S(2)}) collective-permute-start(bf16[4,7168]{1,0:T(4,128)(2,1)S(1)} %get-tuple-element.17), channel_id=1, source_target_pairs={{0,6},{1,7},{2,8},{3,9},{4,10},{5,11},{6,12},{7,13},{8,14},{9,15},... | collective-permute-start | bytes 172040 | tf_op jit(solution)/shard_map/ppermute | solution.py:12
  177.6 3.6 %collective-permute-done.19 = bf16[4,7168]{1,0:T(4,128)(2,1)S(1)} collective-permute-done((bf16[4,7168]{1,0:T(4,128)(2,1)S(1)}, bf16[4,7168]{1,0:T(4,128)(2,1)S(1)}, u32[]{:S(2)}, u32[]{:S(2)}) %collective-permute-start.19) | collective-permute-done | bytes 57376 | tf_op jit(solution)/shard_map/ppermute | solution.py:12
  184.2 3.4 %collective-permute-start.44 = (bf16[4,7168]{1,0:T(4,128)(2,1)S(1)}, bf16[4,7168]{1,0:T(4,128)(2,1)S(1)}, u32[]{:S(2)}, u32[]{:S(2)}) collective-permute-start(bf16[4,7168]{1,0:T(4,128)(2,1)S(1)} %get-tuple-element.33), channel_id=1, source_target_pairs={{0,8},{1,9},{2,10},{3,11},{4,12},{5,13},{6,14},{7,15},{8,0},{9,1},... | collective-permute-start | bytes 172040 | tf_op jit(solution)/shard_map/ppermute | solution.py:12
  187.8 2.2 %collective-permute-start.46 = (bf16[4,7168]{1,0:T(4,128)(2,1)S(1)}, bf16[4,7168]{1,0:T(4,128)(2,1)S(1)}, u32[]{:S(2)}, u32[]{:S(2)}) collective-permute-start(bf16[4,7168]{1,0:T(4,128)(2,1)S(1)} %get-tuple-element.31), channel_id=1, source_target_pairs={{0,4},{1,5},{2,6},{3,7},{4,8},{5,9},{6,10},{7,11},{8,12},{9,13},{1... | collective-permute-start | bytes 172040 | tf_op jit(solution)/shard_map/ppermute | solution.py:12
  191.4 2.3 %collective-permute-done.45 = bf16[4,7168]{1,0:T(4,128)(2,1)S(1)} collective-permute-done((bf16[4,7168]{1,0:T(4,128)(2,1)S(1)}, bf16[4,7168]{1,0:T(4,128)(2,1)S(1)}, u32[]{:S(2)}, u32[]{:S(2)}) %collective-permute-start.45) | collective-permute-done | bytes 57376 | tf_op jit(solution)/shard_map/ppermute | solution.py:12
  (180 shorter events, 46.2 us)
Async XLA Ops:
  3.0 65.3 %collective-permute-start = (bf16[4,7168]{1,0:T(4,128)(2,1)S(1)}, bf16[4,7168]{1,0:T(4,128)(2,1)S(1)}, u32[]{:S(2)}, u32[]{:S(2)}) collective-permute-start(bf16[4,7168]{1,0:T(4,128)(2,1)S(1)} %bitcast.232), channel_id=1, source_target_pairs={{0,2},{1,3},{2,4},{3,5},{4,6},{5,7},{6,8},{7,9},{8,10},{9,11},{10,... | collective-permute-start | bytes 172040 | tf_op jit(solution)/shard_map/ppermute | solution.py:12
  4.6 66.1 %collective-permute-start.1 = (bf16[4,7168]{1,0:T(4,128)(2,1)S(1)}, bf16[4,7168]{1,0:T(4,128)(2,1)S(1)}, u32[]{:S(2)}, u32[]{:S(2)}) collective-permute-start(bf16[4,7168]{1,0:T(4,128)(2,1)S(1)} %bitcast.231), channel_id=1, source_target_pairs={{0,4},{1,5},{2,6},{3,7},{4,8},{5,9},{6,10},{7,11},{8,12},{9,13},{1... | collective-permute-start | bytes 172040 | tf_op jit(solution)/shard_map/ppermute | solution.py:12
  6.3 66.4 %collective-permute-start.2 = (bf16[4,7168]{1,0:T(4,128)(2,1)S(1)}, bf16[4,7168]{1,0:T(4,128)(2,1)S(1)}, u32[]{:S(2)}, u32[]{:S(2)}) collective-permute-start(bf16[4,7168]{1,0:T(4,128)(2,1)S(1)} %bitcast.229), channel_id=1, source_target_pairs={{0,6},{1,7},{2,8},{3,9},{4,10},{5,11},{6,12},{7,13},{8,14},{9,15},... | collective-permute-start | bytes 172040 | tf_op jit(solution)/shard_map/ppermute | solution.py:12
  7.5 65.3 %collective-permute-start.3 = (bf16[4,7168]{1,0:T(4,128)(2,1)S(1)}, bf16[4,7168]{1,0:T(4,128)(2,1)S(1)}, u32[]{:S(2)}, u32[]{:S(2)}) collective-permute-start(bf16[4,7168]{1,0:T(4,128)(2,1)S(1)} %bitcast.227), channel_id=1, source_target_pairs={{0,8},{1,9},{2,10},{3,11},{4,12},{5,13},{6,14},{7,15},{8,0},{9,1},... | collective-permute-start | bytes 172040 | tf_op jit(solution)/shard_map/ppermute | solution.py:12
  18.9 5.3 %collective-permute-start.10 = (bf16[4,2]{0,1:T(2,128)(2,1)S(1)}, bf16[4,2]{0,1:T(2,128)(2,1)S(1)}, u32[]{:S(2)}, u32[]{:S(2)}) collective-permute-start(bf16[4,2]{0,1:T(2,128)(2,1)S(1)} %get-tuple-element.57), channel_id=1, source_target_pairs={{0,6},{1,7},{2,8},{3,9},{4,10},{5,11},{6,12},{7,13},{8,14},{9,15},... | collective-permute-start | bytes 56 | tf_op jit(solution)/shard_map/ppermute | solution.py:12
  46.4 5.4 %collective-permute-start.33 = (bf16[4,2]{0,1:T(2,128)(2,1)S(1)}, bf16[4,2]{0,1:T(2,128)(2,1)S(1)}, u32[]{:S(2)}, u32[]{:S(2)}) collective-permute-start(bf16[4,2]{0,1:T(2,128)(2,1)S(1)} %get-tuple-element.50), channel_id=1, source_target_pairs={{0,4},{1,5},{2,6},{3,7},{4,8},{5,9},{6,10},{7,11},{8,12},{9,13},{1... | collective-permute-start | bytes 56 | tf_op jit(solution)/shard_map/ppermute | solution.py:12
  66.0 10.3 %collective-permute-start.4 = (bf16[4,7168]{1,0:T(4,128)(2,1)S(1)}, bf16[4,7168]{1,0:T(4,128)(2,1)S(1)}, u32[]{:S(2)}, u32[]{:S(2)}) collective-permute-start(bf16[4,7168]{1,0:T(4,128)(2,1)S(1)} %bitcast.235), channel_id=1, source_target_pairs={{0,10},{1,11},{2,12},{3,13},{4,14},{5,15},{6,0},{7,1},{8,2},{9,3},... | collective-permute-start | bytes 172040 | tf_op jit(solution)/shard_map/ppermute | solution.py:12
  68.3 8.2 %collective-permute-start.5 = (bf16[4,7168]{1,0:T(4,128)(2,1)S(1)}, bf16[4,7168]{1,0:T(4,128)(2,1)S(1)}, u32[]{:S(2)}, u32[]{:S(2)}) collective-permute-start(bf16[4,7168]{1,0:T(4,128)(2,1)S(1)} %bitcast.234), channel_id=1, source_target_pairs={{0,12},{1,13},{2,14},{3,15},{4,0},{5,1},{6,2},{7,3},{8,4},{9,5},{1... | collective-permute-start | bytes 172040 | tf_op jit(solution)/shard_map/ppermute | solution.py:12
  70.7 6.6 %collective-permute-start.6 = (bf16[4,7168]{1,0:T(4,128)(2,1)S(1)}, bf16[4,7168]{1,0:T(4,128)(2,1)S(1)}, u32[]{:S(2)}, u32[]{:S(2)}) collective-permute-start(bf16[4,7168]{1,0:T(4,128)(2,1)S(1)} %bitcast.233), channel_id=1, source_target_pairs={{0,14},{1,15},{2,0},{3,1},{4,2},{5,3},{6,4},{7,5},{8,6},{9,7},{10,... | collective-permute-start | bytes 172040 | tf_op jit(solution)/shard_map/ppermute | solution.py:12
  72.7 9.8 %collective-permute-start.37 = (bf16[4,2]{0,1:T(2,128)(2,1)S(1)}, bf16[4,2]{0,1:T(2,128)(2,1)S(1)}, u32[]{:S(2)}, u32[]{:S(2)}) collective-permute-start(bf16[4,2]{0,1:T(2,128)(2,1)S(1)} %get-tuple-element.46), channel_id=1, source_target_pairs={{0,12},{1,13},{2,14},{3,15},{4,0},{5,1},{6,2},{7,3},{8,4},{9,5},{1... | collective-permute-start | bytes 56 | tf_op jit(solution)/shard_map/ppermute | solution.py:12
  72.8 9.8 %collective-permute-start.38 = (bf16[4,2]{0,1:T(2,128)(2,1)S(1)}, bf16[4,2]{0,1:T(2,128)(2,1)S(1)}, u32[]{:S(2)}, u32[]{:S(2)}) collective-permute-start(bf16[4,2]{0,1:T(2,128)(2,1)S(1)} %get-tuple-element.45), channel_id=1, source_target_pairs={{0,14},{1,15},{2,0},{3,1},{4,2},{5,3},{6,4},{7,5},{8,6},{9,7},{10,... | collective-permute-start | bytes 56 | tf_op jit(solution)/shard_map/ppermute | solution.py:12
  76.3 10.7 %collective-permute-start.24 = (bf16[4,7168]{1,0:T(4,128)(2,1)S(1)}, bf16[4,7168]{1,0:T(4,128)(2,1)S(1)}, u32[]{:S(2)}, u32[]{:S(2)}) collective-permute-start(bf16[4,7168]{1,0:T(4,128)(2,1)S(1)} %bitcast.230), channel_id=1, source_target_pairs={{0,2},{1,3},{2,4},{3,5},{4,6},{5,7},{6,8},{7,9},{8,10},{9,11},{10,... | collective-permute-start | bytes 172040 | tf_op jit(solution)/shard_map/ppermute | solution.py:12
  76.4 13.5 %collective-permute-start.25 = (bf16[4,7168]{1,0:T(4,128)(2,1)S(1)}, bf16[4,7168]{1,0:T(4,128)(2,1)S(1)}, u32[]{:S(2)}, u32[]{:S(2)}) collective-permute-start(bf16[4,7168]{1,0:T(4,128)(2,1)S(1)} %bitcast.224), channel_id=1, source_target_pairs={{0,4},{1,5},{2,6},{3,7},{4,8},{5,9},{6,10},{7,11},{8,12},{9,13},{1... | collective-permute-start | bytes 172040 | tf_op jit(solution)/shard_map/ppermute | solution.py:12
  77.3 12.6 %collective-permute-start.26 = (bf16[4,7168]{1,0:T(4,128)(2,1)S(1)}, bf16[4,7168]{1,0:T(4,128)(2,1)S(1)}, u32[]{:S(2)}, u32[]{:S(2)}) collective-permute-start(bf16[4,7168]{1,0:T(4,128)(2,1)S(1)} %bitcast.222), channel_id=1, source_target_pairs={{0,6},{1,7},{2,8},{3,9},{4,10},{5,11},{6,12},{7,13},{8,14},{9,15},... | collective-permute-start | bytes 172040 | tf_op jit(solution)/shard_map/ppermute | solution.py:12
  82.5 14.8 %collective-permute-start.7 = (bf16[32,7168]{1,0:T(8,128)(2,1)S(1)}, bf16[32,7168]{1,0:T(8,128)(2,1)S(1)}, u32[]{:S(2)}, u32[]{:S(2)}) collective-permute-start(bf16[32,7168]{1,0:T(8,128)(2,1)S(1)} %reshape.191), channel_id=1, source_target_pairs={{0,1},{1,0},{2,3},{3,2},{4,5},{5,4},{6,7},{7,6},{8,9},{9,8},{10,11... | collective-permute-start | bytes 1376264 | tf_op jit(solution)/shard_map/ppermute | solution.py:16
  85.5 6.3 %collective-permute-start.27 = (bf16[4,7168]{1,0:T(4,128)(2,1)S(1)}, bf16[4,7168]{1,0:T(4,128)(2,1)S(1)}, u32[]{:S(2)}, u32[]{:S(2)}) collective-permute-start(bf16[4,7168]{1,0:T(4,128)(2,1)S(1)} %bitcast.221), channel_id=1, source_target_pairs={{0,8},{1,9},{2,10},{3,11},{4,12},{5,13},{6,14},{7,15},{8,0},{9,1},... | collective-permute-start | bytes 172040 | tf_op jit(solution)/shard_map/ppermute | solution.py:12
  87.0 7.9 %collective-permute-start.28 = (bf16[4,7168]{1,0:T(4,128)(2,1)S(1)}, bf16[4,7168]{1,0:T(4,128)(2,1)S(1)}, u32[]{:S(2)}, u32[]{:S(2)}) collective-permute-start(bf16[4,7168]{1,0:T(4,128)(2,1)S(1)} %bitcast.220), channel_id=1, source_target_pairs={{0,10},{1,11},{2,12},{3,13},{4,14},{5,15},{6,0},{7,1},{8,2},{9,3},... | collective-permute-start | bytes 172040 | tf_op jit(solution)/shard_map/ppermute | solution.py:12
  97.2 33.6 %collective-permute-start.31 = (bf16[32,7168]{1,0:T(8,128)(2,1)S(1)}, bf16[32,7168]{1,0:T(8,128)(2,1)S(1)}, u32[]{:S(2)}, u32[]{:S(2)}) collective-permute-start(bf16[32,7168]{1,0:T(8,128)(2,1)S(1)} %reshape.193), channel_id=1, source_target_pairs={{0,1},{1,0},{2,3},{3,2},{4,5},{5,4},{6,7},{7,6},{8,9},{9,8},{10,11... | collective-permute-start | bytes 1376264 | tf_op jit(solution)/shard_map/ppermute | solution.py:16
  130.3 33.6 %collective-permute-start.16 = (bf16[32,7168]{1,0:T(8,128)(2,1)S(1)}, bf16[32,7168]{1,0:T(8,128)(2,1)}, u32[]{:S(2)}, u32[]{:S(2)}) collective-permute-start(bf16[32,7168]{1,0:T(8,128)(2,1)S(1)} %get-tuple-element.12), channel_id=1, source_target_pairs={{0,1},{1,0},{2,3},{3,2},{4,5},{5,4},{6,7},{7,6},{8,9},{9,8},{10,11... | collective-permute-start | bytes 1376264 | tf_op jit(solution)/shard_map/ppermute | solution.py:16
  165.2 9.3 %collective-permute-start.17 = (bf16[4,7168]{1,0:T(4,128)(2,1)S(1)}, bf16[4,7168]{1,0:T(4,128)(2,1)S(1)}, u32[]{:S(2)}, u32[]{:S(2)}) collective-permute-start(bf16[4,7168]{1,0:T(4,128)(2,1)S(1)} %get-tuple-element.21), channel_id=1, source_target_pairs={{0,14},{1,15},{2,0},{3,1},{4,2},{5,3},{6,4},{7,5},{8,6},{9,7},{10,... | collective-permute-start | bytes 172040 | tf_op jit(solution)/shard_map/ppermute | solution.py:12
  167.7 8.0 %collective-permute-start.18 = (bf16[4,7168]{1,0:T(4,128)(2,1)S(1)}, bf16[4,7168]{1,0:T(4,128)(2,1)S(1)}, u32[]{:S(2)}, u32[]{:S(2)}) collective-permute-start(bf16[4,7168]{1,0:T(4,128)(2,1)S(1)} %get-tuple-element.20), channel_id=1, source_target_pairs={{0,12},{1,13},{2,14},{3,15},{4,0},{5,1},{6,2},{7,3},{8,4},{9,5},{1... | collective-permute-start | bytes 172040 | tf_op jit(solution)/shard_map/ppermute | solution.py:12
  171.2 10.0 %collective-permute-start.19 = (bf16[4,7168]{1,0:T(4,128)(2,1)S(1)}, bf16[4,7168]{1,0:T(4,128)(2,1)S(1)}, u32[]{:S(2)}, u32[]{:S(2)}) collective-permute-start(bf16[4,7168]{1,0:T(4,128)(2,1)S(1)} %get-tuple-element.19), channel_id=1, source_target_pairs={{0,10},{1,11},{2,12},{3,13},{4,14},{5,15},{6,0},{7,1},{8,2},{9,3},... | collective-permute-start | bytes 172040 | tf_op jit(solution)/shard_map/ppermute | solution.py:12
  171.2 10.0 %collective-permute-start.20 = (bf16[4,7168]{1,0:T(4,128)(2,1)S(1)}, bf16[4,7168]{1,0:T(4,128)(2,1)S(1)}, u32[]{:S(2)}, u32[]{:S(2)}) collective-permute-start(bf16[4,7168]{1,0:T(4,128)(2,1)S(1)} %get-tuple-element.18), channel_id=1, source_target_pairs={{0,8},{1,9},{2,10},{3,11},{4,12},{5,13},{6,14},{7,15},{8,0},{9,1},... | collective-permute-start | bytes 172040 | tf_op jit(solution)/shard_map/ppermute | solution.py:12
  171.2 11.9 %collective-permute-start.21 = (bf16[4,7168]{1,0:T(4,128)(2,1)S(1)}, bf16[4,7168]{1,0:T(4,128)(2,1)S(1)}, u32[]{:S(2)}, u32[]{:S(2)}) collective-permute-start(bf16[4,7168]{1,0:T(4,128)(2,1)S(1)} %get-tuple-element.17), channel_id=1, source_target_pairs={{0,6},{1,7},{2,8},{3,9},{4,10},{5,11},{6,12},{7,13},{8,14},{9,15},... | collective-permute-start | bytes 172040 | tf_op jit(solution)/shard_map/ppermute | solution.py:12
  174.5 9.6 %collective-permute-start.22 = (bf16[4,7168]{1,0:T(4,128)(2,1)S(1)}, bf16[4,7168]{1,0:T(4,128)(2,1)S(1)}, u32[]{:S(2)}, u32[]{:S(2)}) collective-permute-start(bf16[4,7168]{1,0:T(4,128)(2,1)S(1)} %get-tuple-element.16), channel_id=1, source_target_pairs={{0,4},{1,5},{2,6},{3,7},{4,8},{5,9},{6,10},{7,11},{8,12},{9,13},{1... | collective-permute-start | bytes 172040 | tf_op jit(solution)/shard_map/ppermute | solution.py:12
  175.7 12.0 %collective-permute-start.23 = (bf16[4,7168]{1,0:T(4,128)(2,1)S(1)}, bf16[4,7168]{1,0:T(4,128)(2,1)S(1)}, u32[]{:S(2)}, u32[]{:S(2)}) collective-permute-start(bf16[4,7168]{1,0:T(4,128)(2,1)S(1)} %get-tuple-element.15), channel_id=1, source_target_pairs={{0,2},{1,3},{2,4},{3,5},{4,6},{5,7},{6,8},{7,9},{8,10},{9,11},{10,... | collective-permute-start | bytes 172040 | tf_op jit(solution)/shard_map/ppermute | solution.py:12
  181.2 6.6 %collective-permute-start.41 = (bf16[4,7168]{1,0:T(4,128)(2,1)S(1)}, bf16[4,7168]{1,0:T(4,128)(2,1)S(1)}, u32[]{:S(2)}, u32[]{:S(2)}) collective-permute-start(bf16[4,7168]{1,0:T(4,128)(2,1)S(1)} %get-tuple-element.36), channel_id=1, source_target_pairs={{0,14},{1,15},{2,0},{3,1},{4,2},{5,3},{6,4},{7,5},{8,6},{9,7},{10,... | collective-permute-start | bytes 172040 | tf_op jit(solution)/shard_map/ppermute | solution.py:12
  181.2 8.8 %collective-permute-start.42 = (bf16[4,7168]{1,0:T(4,128)(2,1)S(1)}, bf16[4,7168]{1,0:T(4,128)(2,1)S(1)}, u32[]{:S(2)}, u32[]{:S(2)}) collective-permute-start(bf16[4,7168]{1,0:T(4,128)(2,1)S(1)} %get-tuple-element.35), channel_id=1, source_target_pairs={{0,12},{1,13},{2,14},{3,15},{4,0},{5,1},{6,2},{7,3},{8,4},{9,5},{1... | collective-permute-start | bytes 172040 | tf_op jit(solution)/shard_map/ppermute | solution.py:12
  183.1 7.8 %collective-permute-start.43 = (bf16[4,7168]{1,0:T(4,128)(2,1)S(1)}, bf16[4,7168]{1,0:T(4,128)(2,1)S(1)}, u32[]{:S(2)}, u32[]{:S(2)}) collective-permute-start(bf16[4,7168]{1,0:T(4,128)(2,1)S(1)} %get-tuple-element.34), channel_id=1, source_target_pairs={{0,10},{1,11},{2,12},{3,13},{4,14},{5,15},{6,0},{7,1},{8,2},{9,3},... | collective-permute-start | bytes 172040 | tf_op jit(solution)/shard_map/ppermute | solution.py:12
  184.2 7.2 %collective-permute-start.44 = (bf16[4,7168]{1,0:T(4,128)(2,1)S(1)}, bf16[4,7168]{1,0:T(4,128)(2,1)S(1)}, u32[]{:S(2)}, u32[]{:S(2)}) collective-permute-start(bf16[4,7168]{1,0:T(4,128)(2,1)S(1)} %get-tuple-element.33), channel_id=1, source_target_pairs={{0,8},{1,9},{2,10},{3,11},{4,12},{5,13},{6,14},{7,15},{8,0},{9,1},... | collective-permute-start | bytes 172040 | tf_op jit(solution)/shard_map/ppermute | solution.py:12
  187.6 6.0 %collective-permute-start.45 = (bf16[4,7168]{1,0:T(4,128)(2,1)S(1)}, bf16[4,7168]{1,0:T(4,128)(2,1)S(1)}, u32[]{:S(2)}, u32[]{:S(2)}) collective-permute-start(bf16[4,7168]{1,0:T(4,128)(2,1)S(1)} %get-tuple-element.32), channel_id=1, source_target_pairs={{0,6},{1,7},{2,8},{3,9},{4,10},{5,11},{6,12},{7,13},{8,14},{9,15},... | collective-permute-start | bytes 172040 | tf_op jit(solution)/shard_map/ppermute | solution.py:12
  187.8 6.0 %collective-permute-start.46 = (bf16[4,7168]{1,0:T(4,128)(2,1)S(1)}, bf16[4,7168]{1,0:T(4,128)(2,1)S(1)}, u32[]{:S(2)}, u32[]{:S(2)}) collective-permute-start(bf16[4,7168]{1,0:T(4,128)(2,1)S(1)} %get-tuple-element.31), channel_id=1, source_target_pairs={{0,4},{1,5},{2,6},{3,7},{4,8},{5,9},{6,10},{7,11},{8,12},{9,13},{1... | collective-permute-start | bytes 172040 | tf_op jit(solution)/shard_map/ppermute | solution.py:12
  (19 other events, 98.8 us)
where the time goes:
time: 199 us; the launch traced here: 196 us
  matrix products  68.4 us (34%)
  starting transfers between devices  67.2 us (34%)
  waiting for transfers between devices  48.4 us (24%)
  local copies, waits for them, and re-layouts  8.45 us (4%)
  other arithmetic  3.26 us (2%)
    ppermute x42, starting transfers between devices, passed_along(): lax.ppermute(shard, axis, [(i, (i + by) % size) for i in range(size)])  65.8 us
    ppermute x42, waiting for transfers between devices, passed_along(): lax.ppermute(shard, axis, [(i, (i + by) % size) for i in range(size)])  46.2 us
    dot_general x2, matrix products, body(): partial_sum = jnp.dot(hidden, w_down[0], preferred_element_type=jnp.float32)  41.7 us
    dot_general x2, matrix products, body(): up_val = jnp.dot(all_rows, w_up[0], preferred_element_type=jnp.float32)  24.1 us
    another operation x18, local copies, waits for them, and re-layouts, body(): arrived = jnp.stack(rows_list)  4.81 us
  transfers between devices with their start and end apart: 48, of which 20 were waited for; matrix products, arithmetic and copies ran while one was open for 39% of the time, Pallas kernels for 0%

commit v1 on v0

v1 whole, which is shorter than its diff:
```python
import jax
import jax.numpy as jnp
from jax import lax
from jax.sharding import PartitionSpec as P

GROUPS = 8
EXP_GRP = 2
EXTRA = 128
IN_CUTS = 1
OUT_CUTS = 1


def exchanged(shard, by, unit):
    size = lax.axis_size("grp")
    return lax.ppermute(
        shard, "grp", [(i, ((i // unit) ^ by) * unit + i % unit) for i in range(size)]
    )


def spans(width, cuts):
    step = width // cuts
    return [(k * step, step) for k in range(cuts)]


def body(tokens, expert_ids, gate_weights, w_gate, w_up, w_down):
    devices = lax.axis_size("grp")
    gsize = devices // GROUPS
    in_bits = gsize.bit_length() - 1
    rank = lax.axis_index("grp")
    group_me = rank // gsize
    my_expert = group_me * EXP_GRP + rank % gsize // (gsize // EXP_GRP)
    batches, rows, width = tokens.shape
    cap = rows // 2
    topk = expert_ids.shape[2]
    block = batches * cap

    targets = group_me ^ jnp.arange(GROUPS, dtype=jnp.int32)
    routed = jnp.any(
        (expert_ids // EXP_GRP)[:, :, None, :] == targets[None, None, :, None], axis=-1
    )
    routed_int = routed.astype(jnp.int32)
    slots = jnp.cumsum(routed_int, axis=1) - routed_int
    dispatch = jnp.logical_and(
        routed[..., None], slots[..., None] == jnp.arange(cap, dtype=jnp.int32)
    )
    same = jnp.eye(batches, dtype=bool)
    slot_rows = (
        jnp.logical_and(
            dispatch.transpose(2, 0, 3, 1)[:, :, :, None, :], same[None, :, None, :, None]
        )
        .astype(jnp.bfloat16)
        .reshape(GROUPS * block, batches * rows)
    )

    flat = tokens.reshape(batches * rows, width)
    extra = jnp.concatenate(
        [
            expert_ids.astype(jnp.bfloat16).reshape(batches * rows, topk),
            gate_weights.reshape(batches * rows, topk),
            jnp.zeros((batches * rows, EXTRA - 2 * topk), jnp.bfloat16),
        ],
        axis=1,
    )

    gate = up_val = column = None
    for k, (at, step) in enumerate(spans(width, IN_CUTS)):
        part = flat[:, at : at + step]
        if k == 0:
            part = jnp.concatenate([part, extra], axis=1)
        bucket = jnp.dot(slot_rows, part, preferred_element_type=jnp.float32).astype(jnp.bfloat16)
        arrived = [bucket[:block]]
        for by in range(1, GROUPS):
            arrived.append(exchanged(bucket[by * block : (by + 1) * block], by, gsize))
        all_rows = jnp.concatenate(arrived)
        for bit in range(in_bits):
            all_rows = jnp.concatenate([all_rows, exchanged(all_rows, 1 << bit, 1)])
        if k == 0:
            ids = all_rows[:, step : step + topk]
            weights = all_rows[:, step + topk : step + 2 * topk].astype(jnp.float32)
            chosen = ids == my_expert.astype(jnp.bfloat16)
            column = jnp.sum(jnp.where(chosen, weights, 0.0), axis=1, keepdims=True)
            all_rows = all_rows[:, :step]
        gate_k = jnp.dot(all_rows, w_gate[0, at : at + step], preferred_element_type=jnp.float32)
        up_k = jnp.dot(all_rows, w_up[0, at : at + step], preferred_element_type=jnp.float32)
        gate = gate_k if gate is None else gate + gate_k
        up_val = up_k if up_val is None else up_val + up_k
    hidden = (jax.nn.silu(gate) * up_val * column).astype(jnp.bfloat16)

    outputs = []
    for at, step in spans(width, OUT_CUTS):
        total = jnp.dot(hidden, w_down[0, :, at : at + step], preferred_element_type=jnp.float32)
        for bit in reversed(range(in_bits)):
            half = total.shape[0] // 2
            got = exchanged(total[half:].astype(jnp.bfloat16), 1 << bit, 1)
            total = total[:half] + got.astype(jnp.float32)
        result = total.astype(jnp.bfloat16)
        back = [result[:block]]
        for by in range(1, GROUPS):
            back.append(exchanged(result[by * block : (by + 1) * block], by, gsize))
        mixed = lax.dot_general(
            slot_rows,
            jnp.concatenate(back),
            (((0,), (0,)), ((), ())),
            preferred_element_type=jnp.float32,
        )
        outputs.append(mixed.astype(jnp.bfloat16))
    return jnp.concatenate(outputs, axis=1).reshape(batches, rows, width)


def solution(mesh):
    split = P(None, ("rep", "grp"), None)
    stacked = P("grp", None, None)
    return jax.shard_map(
        body,
        mesh=mesh,
        in_specs=(split, split, split, stacked, stacked, stacked),
        out_specs=split,
        check_vma=False,
    )
```

time: 199 us -> 105 us (0.53)
  the two profiles are of different devices: /device:TPU:12 before, /device:TPU:0 now
where the time goes in v1:
time: 105 us
  matrix products  34.9 us (33%)
  waiting for transfers between devices  31 us (30%)
  starting transfers between devices  26.4 us (25%)
  local copies, waits for them, and re-layouts  9.32 us (9%)
  other arithmetic  2.84 us (3%)
    ppermute x16, waiting for transfers between devices, exchanged(): lax.ppermute(shard, 'grp', [(i, (i // unit ^ by) * unit + i % unit) for i...  31 us
    ppermute x16, starting transfers between devices, exchanged(): lax.ppermute(shard, 'grp', [(i, (i // unit ^ by) * unit + i % unit) for i...  26.4 us
    dot_general x1, matrix products, body(): jnp.dot(hidden, w_down[0, :, at:at + step], preferred_element_type=jnp.fl...  22.1 us
    dot_general x1, matrix products, body(): jnp.dot(all_rows, w_up[0, at:at + step], preferred_element_type=jnp.float32)  11.4 us
    unnamed x13, local copies, waits for them, and re-layouts  4.71 us
  transfers between devices with their start and end apart: 16, of which 6 were waited for; matrix products, arithmetic and copies ran while one was open for 4% of the time, Pallas kernels for 0%

profile of v1, /device:TPU:0, one launch (start us, length us, event | category | flops | bytes accessed | tf_op | source)
XLA Modules:
  0.0 104.6 jit_solution(3624615003787384478)
XLA Ops:
  0.0 0.8 copy.26
  0.8 0.8 fusion.25
  2.2 1.0 concatenate.13
  3.6 0.7 slice_dynamic-update-slice_fusion.2
  4.3 2.9 %collective-permute-start = (bf16[8,7296]{1,0:T(8,128)(2,1)S(1)}, bf16[8,7296]{1,0:T(8,128)(2,1)S(1)}, u32[]{:S(2)}, u32[]{:S(2)}) collective-permute-start(bf16[8,7296]{1,0:T(8,128)(2,1)S(1)} %get-tuple-element.13), channel_id=1, source_target_pairs={{0,2},{1,3},{2,0},{3,1},{4,6},{5,7},{6,4},{7,5},{8,10},{9,11},{10,... | collective-permute-start | bytes 350216 | tf_op jit(solution)/shard_map/ppermute | solution.py:15
  7.3 3.6 %collective-permute-start.6 = (bf16[8,7296]{1,0:T(8,128)(2,1)S(1)}, bf16[8,7296]{1,0:T(8,128)(2,1)S(1)}, u32[]{:S(2)}, u32[]{:S(2)}) collective-permute-start(bf16[8,7296]{1,0:T(8,128)(2,1)S(1)} %get-tuple-element.7), channel_id=1, source_target_pairs={{0,14},{1,15},{2,12},{3,13},{4,10},{5,11},{6,8},{7,9},{8,6},{9,7},... | collective-permute-start | bytes 350216 | tf_op jit(solution)/shard_map/ppermute | solution.py:15
  10.9 1.9 %collective-permute-start.4 = (bf16[8,7296]{1,0:T(8,128)(2,1)S(1)}, bf16[8,7296]{1,0:T(8,128)(2,1)S(1)}, u32[]{:S(2)}, u32[]{:S(2)}) collective-permute-start(bf16[8,7296]{1,0:T(8,128)(2,1)S(1)} %get-tuple-element.9), channel_id=1, source_target_pairs={{0,10},{1,11},{2,8},{3,9},{4,14},{5,15},{6,12},{7,13},{8,2},{9,3},... | collective-permute-start | bytes 350216 | tf_op jit(solution)/shard_map/ppermute | solution.py:15
  12.8 2.1 %collective-permute-start.3 = (bf16[8,7296]{1,0:T(8,128)(2,1)S(1)}, bf16[8,7296]{1,0:T(8,128)(2,1)S(1)}, u32[]{:S(2)}, u32[]{:S(2)}) collective-permute-start(bf16[8,7296]{1,0:T(8,128)(2,1)S(1)} %get-tuple-element.10), channel_id=1, source_target_pairs={{0,8},{1,9},{2,10},{3,11},{4,12},{5,13},{6,14},{7,15},{8,0},{9,1},... | collective-permute-start | bytes 350216 | tf_op jit(solution)/shard_map/ppermute | solution.py:15
  14.9 1.2 %collective-permute-start.1 = (bf16[8,7296]{1,0:T(8,128)(2,1)S(1)}, bf16[8,7296]{1,0:T(8,128)(2,1)S(1)}, u32[]{:S(2)}, u32[]{:S(2)}) collective-permute-start(bf16[8,7296]{1,0:T(8,128)(2,1)S(1)} %get-tuple-element.12), channel_id=1, source_target_pairs={{0,4},{1,5},{2,6},{3,7},{4,0},{5,1},{6,2},{7,3},{8,12},{9,13},{10,... | collective-permute-start | bytes 350216 | tf_op jit(solution)/shard_map/ppermute | solution.py:15
  16.2 0.7 constant_dynamic-update-slice_fusion.6
  16.8 6.2 %collective-permute-done.1 = bf16[8,7296]{1,0:T(8,128)(2,1)S(1)} collective-permute-done((bf16[8,7296]{1,0:T(8,128)(2,1)S(1)}, bf16[8,7296]{1,0:T(8,128)(2,1)S(1)}, u32[]{:S(2)}, u32[]{:S(2)}) %collective-permute-start.1) | collective-permute-done | bytes 116768 | tf_op jit(solution)/shard_map/ppermute | solution.py:15
  23.1 3.4 %collective-permute-start.2 = (bf16[8,7296]{1,0:T(8,128)(2,1)S(1)}, bf16[8,7296]{1,0:T(8,128)(2,1)S(1)}, u32[]{:S(2)}, u32[]{:S(2)}) collective-permute-start(bf16[8,7296]{1,0:T(8,128)(2,1)S(1)} %get-tuple-element.11), channel_id=1, source_target_pairs={{0,6},{1,7},{2,4},{3,5},{4,2},{5,3},{6,0},{7,1},{8,14},{9,15},{10,... | collective-permute-start | bytes 350216 | tf_op jit(solution)/shard_map/ppermute | solution.py:15
  26.5 0.7 constant_dynamic-update-slice_fusion.5
  27.2 6.1 %collective-permute-done.2 = bf16[8,7296]{1,0:T(8,128)(2,1)S(1)} collective-permute-done((bf16[8,7296]{1,0:T(8,128)(2,1)S(1)}, bf16[8,7296]{1,0:T(8,128)(2,1)S(1)}, u32[]{:S(2)}, u32[]{:S(2)}) %collective-permute-start.2) | collective-permute-done | bytes 116768 | tf_op jit(solution)/shard_map/ppermute | solution.py:15
  33.2 0.7 constant_dynamic-update-slice_fusion.4
  33.9 0.7 constant_dynamic-update-slice_fusion.3
  34.5 0.7 constant_dynamic-update-slice_fusion.2
  35.2 0.7 constant_dynamic-update-slice_fusion.1
  35.9 0.7 constant_dynamic-update-slice_fusion
  36.5 2.7 %collective-permute-done.7 = bf16[64,7296]{1,0:T(8,128)(2,1)S(1)} collective-permute-done((bf16[64,7296]{1,0:T(8,128)(2,1)}, bf16[64,7296]{1,0:T(8,128)(2,1)S(1)}, u32[]{:S(2)}, u32[]{:S(2)}) %collective-permute-start.7) | collective-permute-done | bytes 933920 | tf_op jit(solution)/shard_map/ppermute | solution.py:15
  39.5 11.4 %fusion.2 = f32[128,2048]{1,0:T(8,128)S(1)} fusion(bf16[1,7168,2048]{2,1,0:T(8,128)(2,1)} %param.10, bf16[128,7296]{1,0:T(8,128)(2,1)S(1)} %constant_dynamic-update-slice_fusion.7), kind=kOutput, calls=%fused_computation.2 | convolution fusion | flops 3758096384 | bytes 32243712 | tf_op jit(solution)/shard_map/dot_general | solution.py:84
  51.0 22.1 %fusion = f32[128,7168]{1,0:T(8,128)} fusion(bf16[1,2048,7168]{2,1,0:T(8,128)(2,1)} %param.11, f32[128,2048]{1,0:T(8,128)S(1)} %fusion.2, bf16[1,7168,2048]{2,1,0:T(8,128)(2,1)} %param.9, bf16[128,7296]{1,0:T(8,128)(2,1)S(1)} %constant_dynamic-update-slice_fusion.7, f32[128]{0:T(128)S(1)} %select_reduce_fusion), kind=kOutput, calls=%fused_computation | convolution fusion | flops 7518027776 | bytes 65274368 | tf_op jit(solution)/shard_map/dot_general | solution.py:91
  73.1 1.6 %slice.123 = bf16[64,7168]{1,0:T(8,128)(2,1)S(1)} slice(f32[128,7168]{1,0:T(8,128)} %fusion), slice={[64:128], [0:7168]} | slice | bytes 1835008 | tf_op jit(solution)/shard_map/slice | solution.py:94
  74.9 2.3 %collective-permute-done.8 = bf16[64,7168]{1,0:T(8,128)(2,1)S(1)} collective-permute-done((bf16[64,7168]{1,0:T(8,128)(2,1)S(1)}, bf16[64,7168]{1,0:T(8,128)(2,1)S(1)}, u32[]{:S(2)}, u32[]{:S(2)}) %collective-permute-start.8) | collective-permute-done | bytes 917536 | tf_op jit(solution)/shard_map/ppermute | solution.py:15
  77.2 1.7 %fusion.7 = bf16[64,7168]{1,0:T(8,128)(2,1)S(1)} fusion(f32[128,7168]{1,0:T(8,128)} %fusion, bf16[64,7168]{1,0:T(8,128)(2,1)S(1)} %collective-permute-done.8), kind=kLoop, calls=%fused_computation.11 | loop fusion | flops 1376256 | bytes 3670016 | tf_op jit(solution)/shard_map/convert_element_type | solution.py:96
  79.6 2.2 %collective-permute-start.15 = (bf16[8,7168]{1,0:T(8,128)(2,1)S(1)}, bf16[8,7168]{1,0:T(8,128)(2,1)S(1)}, u32[]{:S(2)}, u32[]{:S(2)}) collective-permute-start(bf16[8,7168]{1,0:T(8,128)(2,1)S(1)} %get-tuple-element.14), channel_id=1, source_target_pairs={{0,14},{1,15},{2,12},{3,13},{4,10},{5,11},{6,8},{7,9},{8,6},{9,7},... | collective-permute-start | bytes 344072 | tf_op jit(solution)/shard_map/ppermute | solution.py:15
  81.7 2.5 %collective-permute-start.14 = (bf16[8,7168]{1,0:T(8,128)(2,1)S(1)}, bf16[8,7168]{1,0:T(8,128)(2,1)S(1)}, u32[]{:S(2)}, u32[]{:S(2)}) collective-permute-start(bf16[8,7168]{1,0:T(8,128)(2,1)S(1)} %get-tuple-element.15), channel_id=1, source_target_pairs={{0,12},{1,13},{2,14},{3,15},{4,8},{5,9},{6,10},{7,11},{8,4},{9,5},... | collective-permute-start | bytes 344072 | tf_op jit(solution)/shard_map/ppermute | solution.py:15
  84.3 2.9 %collective-permute-start.12 = (bf16[8,7168]{1,0:T(8,128)(2,1)S(1)}, bf16[8,7168]{1,0:T(8,128)(2,1)S(1)}, u32[]{:S(2)}, u32[]{:S(2)}) collective-permute-start(bf16[8,7168]{1,0:T(8,128)(2,1)S(1)} %get-tuple-element.17), channel_id=1, source_target_pairs={{0,8},{1,9},{2,10},{3,11},{4,12},{5,13},{6,14},{7,15},{8,0},{9,1},... | collective-permute-start | bytes 344072 | tf_op jit(solution)/shard_map/ppermute | solution.py:15
  87.2 6.8 %collective-permute-done.10 = bf16[8,7168]{1,0:T(8,128)(2,1)S(1)} collective-permute-done((bf16[8,7168]{1,0:T(8,128)(2,1)S(1)}, bf16[8,7168]{1,0:T(8,128)(2,1)S(1)}, u32[]{:S(2)}, u32[]{:S(2)}) %collective-permute-start.10) | collective-permute-done | bytes 114720 | tf_op jit(solution)/shard_map/ppermute | solution.py:15
  94.0 2.7 %collective-permute-start.11 = (bf16[8,7168]{1,0:T(8,128)(2,1)S(1)}, bf16[8,7168]{1,0:T(8,128)(2,1)S(1)}, u32[]{:S(2)}, u32[]{:S(2)}) collective-permute-start(bf16[8,7168]{1,0:T(8,128)(2,1)S(1)} %get-tuple-element.18), channel_id=1, source_target_pairs={{0,6},{1,7},{2,4},{3,5},{4,2},{5,3},{6,0},{7,1},{8,14},{9,15},{10,... | collective-permute-start | bytes 344072 | tf_op jit(solution)/shard_map/ppermute | solution.py:15
  96.7 6.8 %collective-permute-done.11 = bf16[8,7168]{1,0:T(8,128)(2,1)S(1)} collective-permute-done((bf16[8,7168]{1,0:T(8,128)(2,1)S(1)}, bf16[8,7168]{1,0:T(8,128)(2,1)S(1)}, u32[]{:S(2)}, u32[]{:S(2)}) %collective-permute-start.11) | collective-permute-done | bytes 114720 | tf_op jit(solution)/shard_map/ppermute | solution.py:15
  103.6 1.0 fusion.6
  (40 shorter events, 2.3 us)
Async XLA Ops:
  4.3 10.6 %collective-permute-start = (bf16[8,7296]{1,0:T(8,128)(2,1)S(1)}, bf16[8,7296]{1,0:T(8,128)(2,1)S(1)}, u32[]{:S(2)}, u32[]{:S(2)}) collective-permute-start(bf16[8,7296]{1,0:T(8,128)(2,1)S(1)} %get-tuple-element.13), channel_id=1, source_target_pairs={{0,2},{1,3},{2,0},{3,1},{4,6},{5,7},{6,4},{7,5},{8,10},{9,11},{10,... | collective-permute-start | bytes 350216 | tf_op jit(solution)/shard_map/ppermute | solution.py:15
  7.3 28.6 %collective-permute-start.6 = (bf16[8,7296]{1,0:T(8,128)(2,1)S(1)}, bf16[8,7296]{1,0:T(8,128)(2,1)S(1)}, u32[]{:S(2)}, u32[]{:S(2)}) collective-permute-start(bf16[8,7296]{1,0:T(8,128)(2,1)S(1)} %get-tuple-element.7), channel_id=1, source_target_pairs={{0,14},{1,15},{2,12},{3,13},{4,10},{5,11},{6,8},{7,9},{8,6},{9,7},... | collective-permute-start | bytes 350216 | tf_op jit(solution)/shard_map/ppermute | solution.py:15
  10.9 24.4 %collective-permute-start.5 = (bf16[8,7296]{1,0:T(8,128)(2,1)S(1)}, bf16[8,7296]{1,0:T(8,128)(2,1)S(1)}, u32[]{:S(2)}, u32[]{:S(2)}) collective-permute-start(bf16[8,7296]{1,0:T(8,128)(2,1)S(1)} %get-tuple-element.8), channel_id=1, source_target_pairs={{0,12},{1,13},{2,14},{3,15},{4,8},{5,9},{6,10},{7,11},{8,4},{9,5},... | collective-permute-start | bytes 350216 | tf_op jit(solution)/shard_map/ppermute | solution.py:15
  10.9 23.7 %collective-permute-start.4 = (bf16[8,7296]{1,0:T(8,128)(2,1)S(1)}, bf16[8,7296]{1,0:T(8,128)(2,1)S(1)}, u32[]{:S(2)}, u32[]{:S(2)}) collective-permute-start(bf16[8,7296]{1,0:T(8,128)(2,1)S(1)} %get-tuple-element.9), channel_id=1, source_target_pairs={{0,10},{1,11},{2,8},{3,9},{4,14},{5,15},{6,12},{7,13},{8,2},{9,3},... | collective-permute-start | bytes 350216 | tf_op jit(solution)/shard_map/ppermute | solution.py:15
  12.8 21.1 %collective-permute-start.3 = (bf16[8,7296]{1,0:T(8,128)(2,1)S(1)}, bf16[8,7296]{1,0:T(8,128)(2,1)S(1)}, u32[]{:S(2)}, u32[]{:S(2)}) collective-permute-start(bf16[8,7296]{1,0:T(8,128)(2,1)S(1)} %get-tuple-element.10), channel_id=1, source_target_pairs={{0,8},{1,9},{2,10},{3,11},{4,12},{5,13},{6,14},{7,15},{8,0},{9,1},... | collective-permute-start | bytes 350216 | tf_op jit(solution)/shard_map/ppermute | solution.py:15
  14.9 8.1 %collective-permute-start.1 = (bf16[8,7296]{1,0:T(8,128)(2,1)S(1)}, bf16[8,7296]{1,0:T(8,128)(2,1)S(1)}, u32[]{:S(2)}, u32[]{:S(2)}) collective-permute-start(bf16[8,7296]{1,0:T(8,128)(2,1)S(1)} %get-tuple-element.12), channel_id=1, source_target_pairs={{0,4},{1,5},{2,6},{3,7},{4,0},{5,1},{6,2},{7,3},{8,12},{9,13},{10,... | collective-permute-start | bytes 350216 | tf_op jit(solution)/shard_map/ppermute | solution.py:15
  23.1 10.1 %collective-permute-start.2 = (bf16[8,7296]{1,0:T(8,128)(2,1)S(1)}, bf16[8,7296]{1,0:T(8,128)(2,1)S(1)}, u32[]{:S(2)}, u32[]{:S(2)}) collective-permute-start(bf16[8,7296]{1,0:T(8,128)(2,1)S(1)} %get-tuple-element.11), channel_id=1, source_target_pairs={{0,6},{1,7},{2,4},{3,5},{4,2},{5,3},{6,0},{7,1},{8,14},{9,15},{10,... | collective-permute-start | bytes 350216 | tf_op jit(solution)/shard_map/ppermute | solution.py:15
  36.5 2.7 %collective-permute-start.7 = (bf16[64,7296]{1,0:T(8,128)(2,1)}, bf16[64,7296]{1,0:T(8,128)(2,1)S(1)}, u32[]{:S(2)}, u32[]{:S(2)}) collective-permute-start(bf16[64,7296]{1,0:T(8,128)(2,1)} %get-tuple-element.22), channel_id=1, source_target_pairs={{0,1},{1,0},{2,3},{3,2},{4,5},{5,4},{6,7},{7,6},{8,9},{9,8},{10,11... | collective-permute-start | bytes 2801672 | tf_op jit(solution)/shard_map/ppermute | solution.py:15
  74.7 2.5 %collective-permute-start.8 = (bf16[64,7168]{1,0:T(8,128)(2,1)S(1)}, bf16[64,7168]{1,0:T(8,128)(2,1)S(1)}, u32[]{:S(2)}, u32[]{:S(2)}) collective-permute-start(bf16[64,7168]{1,0:T(8,128)(2,1)S(1)} %slice.123), channel_id=1, source_target_pairs={{0,1},{1,0},{2,3},{3,2},{4,5},{5,4},{6,7},{7,6},{8,9},{9,8},{10,11... | collective-permute-start | bytes 2752520 | tf_op jit(solution)/shard_map/ppermute | solution.py:15
  78.9 8.3 %collective-permute-start.9 = (bf16[8,7168]{1,0:T(8,128)(2,1)S(1)}, bf16[8,7168]{1,0:T(8,128)(2,1)S(1)}, u32[]{:S(2)}, u32[]{:S(2)}) collective-permute-start(bf16[8,7168]{1,0:T(8,128)(2,1)S(1)} %get-tuple-element.20), channel_id=1, source_target_pairs={{0,2},{1,3},{2,0},{3,1},{4,6},{5,7},{6,4},{7,5},{8,10},{9,11},{10,... | collective-permute-start | bytes 344072 | tf_op jit(solution)/shard_map/ppermute | solution.py:15
  79.6 24.1 %collective-permute-start.15 = (bf16[8,7168]{1,0:T(8,128)(2,1)S(1)}, bf16[8,7168]{1,0:T(8,128)(2,1)S(1)}, u32[]{:S(2)}, u32[]{:S(2)}) collective-permute-start(bf16[8,7168]{1,0:T(8,128)(2,1)S(1)} %get-tuple-element.14), channel_id=1, source_target_pairs={{0,14},{1,15},{2,12},{3,13},{4,10},{5,11},{6,8},{7,9},{8,6},{9,7},... | collective-permute-start | bytes 344072 | tf_op jit(solution)/shard_map/ppermute | solution.py:15
  81.7 21.9 %collective-permute-start.14 = (bf16[8,7168]{1,0:T(8,128)(2,1)S(1)}, bf16[8,7168]{1,0:T(8,128)(2,1)S(1)}, u32[]{:S(2)}, u32[]{:S(2)}) collective-permute-start(bf16[8,7168]{1,0:T(8,128)(2,1)S(1)} %get-tuple-element.15), channel_id=1, source_target_pairs={{0,12},{1,13},{2,14},{3,15},{4,8},{5,9},{6,10},{7,11},{8,4},{9,5},... | collective-permute-start | bytes 344072 | tf_op jit(solution)/shard_map/ppermute | solution.py:15
  84.3 19.3 %collective-permute-start.13 = (bf16[8,7168]{1,0:T(8,128)(2,1)S(1)}, bf16[8,7168]{1,0:T(8,128)(2,1)S(1)}, u32[]{:S(2)}, u32[]{:S(2)}) collective-permute-start(bf16[8,7168]{1,0:T(8,128)(2,1)S(1)} %get-tuple-element.16), channel_id=1, source_target_pairs={{0,10},{1,11},{2,8},{3,9},{4,14},{5,15},{6,12},{7,13},{8,2},{9,3},... | collective-permute-start | bytes 344072 | tf_op jit(solution)/shard_map/ppermute | solution.py:15
  84.3 19.3 %collective-permute-start.12 = (bf16[8,7168]{1,0:T(8,128)(2,1)S(1)}, bf16[8,7168]{1,0:T(8,128)(2,1)S(1)}, u32[]{:S(2)}, u32[]{:S(2)}) collective-permute-start(bf16[8,7168]{1,0:T(8,128)(2,1)S(1)} %get-tuple-element.17), channel_id=1, source_target_pairs={{0,8},{1,9},{2,10},{3,11},{4,12},{5,13},{6,14},{7,15},{8,0},{9,1},... | collective-permute-start | bytes 344072 | tf_op jit(solution)/shard_map/ppermute | solution.py:15
  87.2 6.8 %collective-permute-start.10 = (bf16[8,7168]{1,0:T(8,128)(2,1)S(1)}, bf16[8,7168]{1,0:T(8,128)(2,1)S(1)}, u32[]{:S(2)}, u32[]{:S(2)}) collective-permute-start(bf16[8,7168]{1,0:T(8,128)(2,1)S(1)} %get-tuple-element.19), channel_id=1, source_target_pairs={{0,4},{1,5},{2,6},{3,7},{4,0},{5,1},{6,2},{7,3},{8,12},{9,13},{10,... | collective-permute-start | bytes 344072 | tf_op jit(solution)/shard_map/ppermute | solution.py:15
  94.0 9.5 %collective-permute-start.11 = (bf16[8,7168]{1,0:T(8,128)(2,1)S(1)}, bf16[8,7168]{1,0:T(8,128)(2,1)S(1)}, u32[]{:S(2)}, u32[]{:S(2)}) collective-permute-start(bf16[8,7168]{1,0:T(8,128)(2,1)S(1)} %get-tuple-element.18), channel_id=1, source_target_pairs={{0,6},{1,7},{2,4},{3,5},{4,2},{5,3},{6,0},{7,1},{8,14},{9,15},{10,... | collective-permute-start | bytes 344072 | tf_op jit(solution)/shard_map/ppermute | solution.py:15

commit v2 on v1

v2 whole, which is shorter than its diff:
```python
import functools

import jax
import jax.numpy as jnp
from jax import lax
from jax.experimental import pallas as pl
from jax.experimental.pallas import tpu as pltpu
from jax.sharding import PartitionSpec as P

GROUPS = 8
EXP_GRP = 2
EXTRA = 128
IN_CUTS = 2
OUT_CUTS = 2
DEPTH = 512
COLUMNS = 512
VMEM = 24 << 20


def exchanged(shard, by, unit):
    size = lax.axis_size("grp")
    return lax.ppermute(
        shard, "grp", [(i, ((i // unit) ^ by) * unit + i % unit) for i in range(size)]
    )


def spans(width, cuts):
    step = width // cuts
    return [(k * step, step) for k in range(cuts)]


def call(kernel, out_shape, cost, **kwargs):
    flops, moved = cost
    return pl.pallas_call(
        kernel,
        out_shape=out_shape,
        compiler_params=pltpu.CompilerParams(vmem_limit_bytes=VMEM),
        cost_estimate=pl.CostEstimate(flops=flops, bytes_accessed=moved, transcendentals=0),
        **kwargs,
    )


def bf16(*shape):
    return jax.ShapeDtypeStruct(shape, jnp.bfloat16)


def f32(*shape):
    return jax.ShapeDtypeStruct(shape, jnp.float32)


def iota(shape, dim):
    return lax.broadcasted_iota(jnp.int32, shape, dim)


def slot_matrix(group_me, ids, batches, rows):
    cap = rows // 2
    count = batches * rows
    block = batches * cap
    eye = (iota((count, count), 0) == iota((count, count), 1)).astype(jnp.float32)
    across = lax.dot_general(ids, eye, (((0,), (0,)), ((), ())), preferred_element_type=jnp.float32)
    across = across.astype(jnp.int32)
    shape = (GROUPS * block, count)
    where = iota(shape, 0)
    lane = iota(shape, 1)
    target = group_me ^ (where // block)
    routed = jnp.zeros(shape, jnp.float32)
    for k in range(ids.shape[1]):
        routed = jnp.where(across[k : k + 1, :] // EXP_GRP == target, 1.0, routed)
    above, here = iota((count, count), 0), iota((count, count), 1)
    before = jnp.where((above < here) & (above // rows == here // rows), 1.0, 0.0)
    slots = jnp.dot(routed, before, preferred_element_type=jnp.float32).astype(jnp.int32)
    taken = (slots == where % cap) & (lane // rows == where % block // cap)
    return jnp.where(taken, routed, 0.0).astype(jnp.bfloat16)


def prep_kernel(cuts, group_ref, tokens_ref, ids_ref, weights_ref, matrix_ref, *out_refs):
    batches, rows, width = tokens_ref.shape
    count = batches * rows
    ids = ids_ref[...].reshape(count, ids_ref.shape[2]).astype(jnp.float32)
    weights = weights_ref[...].astype(jnp.float32).reshape(count, ids_ref.shape[2])
    matrix = slot_matrix(group_ref[0], ids, batches, rows)
    matrix_ref[...] = matrix
    block = matrix.shape[0] // GROUPS
    topk = ids.shape[1]
    for k, (at, step) in enumerate(spans(width, cuts)):
        part = tokens_ref[:, :, at : at + step].reshape(count, step)
        bucket = jnp.dot(matrix, part, preferred_element_type=jnp.float32)
        if k == 0:
            extra = jnp.concatenate(
                [ids, weights, jnp.zeros((count, EXTRA - 2 * topk), jnp.float32)], axis=1
            ).astype(jnp.bfloat16)
            more = jnp.dot(matrix, extra, preferred_element_type=jnp.float32)
        for t in range(GROUPS):
            out = out_refs[k * GROUPS + t]
            out[:, :step] = bucket[t * block : (t + 1) * block].astype(jnp.bfloat16)
            if k == 0:
                out[:, step:] = more[t * block : (t + 1) * block].astype(jnp.bfloat16)


def join_kernel(*refs):
    refs[-1][...] = jnp.concatenate(
        [r[...].astype(jnp.float32) for r in refs[:-1]], axis=0
    ).astype(jnp.bfloat16)


def up_kernel(parts, first, last, topk, expert_ref, *refs):
    x = jnp.concatenate([r[...] for r in refs[:parts]], axis=0)
    refs = refs[parts:]
    extras, refs = refs[:parts], refs[parts:]
    w_gate_ref, w_up_ref, refs = refs[0], refs[1], refs[2:]
    if not first:
        gate_in, up_in, refs = refs[0], refs[1], refs[2:]
    if last:
        hidden_ref, gate_acc, up_acc = refs
    else:
        gate_acc, up_acc = refs
    i = pl.program_id(0)

    @pl.when(i == 0)
    def _():
        gate_acc[...] = jnp.zeros_like(gate_acc) if first else gate_in[...]
        up_acc[...] = jnp.zeros_like(up_acc) if first else up_in[...]

    gate_acc[...] += jnp.dot(x, w_gate_ref[0], preferred_element_type=jnp.float32)
    up_acc[...] += jnp.dot(x, w_up_ref[0], preferred_element_type=jnp.float32)

    if last:

        @pl.when(i == pl.num_programs(0) - 1)
        def _():
            extra = jnp.concatenate([r[...].astype(jnp.float32) for r in extras], axis=0)
            expert = expert_ref[0].astype(jnp.float32)
            column = jnp.zeros((extra.shape[0], 1), jnp.float32)
            for k in range(topk):
                column += jnp.where(
                    extra[:, k : k + 1] == expert, extra[:, topk + k : topk + k + 1], 0.0
                )
            gate = gate_acc[...]
            hidden_ref[...] = (jax.nn.silu(gate) * up_acc[...] * column).astype(jnp.bfloat16)


def down_kernel(hidden_ref, w_ref, kept_ref, away_ref):
    total = jnp.dot(hidden_ref[...], w_ref[0], preferred_element_type=jnp.float32)
    half = kept_ref.shape[0]
    kept_ref[...] = total[:half].astype(jnp.bfloat16)
    away_ref[...] = total[half:].astype(jnp.bfloat16)


def sum_kernel(kept_ref, got_ref, *out_refs):
    total = kept_ref[...].astype(jnp.float32) + got_ref[...].astype(jnp.float32)
    block = out_refs[0].shape[0]
    for t, out in enumerate(out_refs):
        out[...] = total[t * block : (t + 1) * block].astype(jnp.bfloat16)


def mix_kernel(cuts, matrix_ref, *refs):
    out_ref = refs[-1]
    batches, rows, width = out_ref.shape
    for k, (at, step) in enumerate(spans(width, cuts)):
        back = jnp.concatenate(
            [r[...].astype(jnp.float32) for r in refs[k * GROUPS : (k + 1) * GROUPS]], axis=0
        ).astype(jnp.bfloat16)
        mixed = lax.dot_general(
            matrix_ref[...], back, (((0,), (0,)), ((), ())), preferred_element_type=jnp.float32
        )
        for b in range(batches):
            out_ref[b, :, at : at + step] = mixed[b * rows : (b + 1) * rows].astype(jnp.bfloat16)


def body(tokens, expert_ids, gate_weights, w_gate, w_up, w_down):
    devices = lax.axis_size("grp")
    gsize = devices // GROUPS
    in_bits = gsize.bit_length() - 1
    rank = lax.axis_index("grp")
    group_me = (rank // gsize).astype(jnp.int32)
    my_expert = (group_me * EXP_GRP + rank % gsize // (gsize // EXP_GRP)).astype(jnp.int32)
    batches, rows, width = tokens.shape
    cap = rows // 2
    topk = expert_ids.shape[2]
    block = batches * cap
    hid = w_gate.shape[2]
    total_rows = gsize * GROUPS * block
    smem = pl.BlockSpec(memory_space=pltpu.SMEM)
    vmem = pl.BlockSpec(memory_space=pltpu.VMEM)

    in_spans = spans(width, IN_CUTS)
    widths = [step + (EXTRA if k == 0 else 0) for k, (_, step) in enumerate(in_spans)]
    matrix, *buckets = call(
        functools.partial(prep_kernel, IN_CUTS),
        [bf16(GROUPS * block, batches * rows)]
        + [bf16(block, w) for w in widths for _ in range(GROUPS)],
        (2 * GROUPS * block * batches * rows * width, 2 * 5 * batches * rows * width),
        in_specs=[smem, vmem, vmem, vmem],
        out_specs=[vmem] * (1 + GROUPS * IN_CUTS),
    )(group_me.reshape(1), tokens, expert_ids, gate_weights)

    arrived = []
    for k in range(IN_CUTS):
        mine = buckets[k * GROUPS : (k + 1) * GROUPS]
        arrived.append([mine[0]] + [exchanged(mine[by], by, gsize) for by in range(1, GROUPS)])

    first_parts = None
    gate_up = ()
    for k, (at, step) in enumerate(in_spans):
        parts = [
            call(
                join_kernel,
                bf16(GROUPS * block, widths[k]),
                (0, 4 * GROUPS * block * widths[k]),
                in_specs=[vmem] * GROUPS,
                out_specs=vmem,
            )(*arrived[k])
        ]
        for bit in range(in_bits):
            all_rows = parts[0] if bit == 0 else jnp.concatenate(parts)
            parts.append(exchanged(all_rows, 1 << bit, 1))
        if k == 0:
            first_parts = parts
        last = k == IN_CUTS - 1
        depth = DEPTH if step % DEPTH == 0 else step // 7
        acc = pl.BlockSpec((total_rows, hid), lambda i: (0, 0))
        weight = pl.BlockSpec((1, depth, hid), lambda i, at=at, depth=depth: (0, at // depth + i, 0))
        outs = call(
            functools.partial(up_kernel, len(parts), k == 0, last, topk),
            bf16(total_rows, hid) if last else [f32(total_rows, hid)] * 2,
            (4 * total_rows * step * hid, 4 * step * hid),
            grid=(step // depth,),
            in_specs=[smem]
            + [pl.BlockSpec((p.shape[0], depth), lambda i: (0, i)) for p in parts]
            + [
                pl.BlockSpec((p.shape[0], EXTRA), lambda i: (0, in_spans[0][1] // EXTRA))
                for p in first_parts
            ]
            + [weight, weight]
            + ([] if k == 0 else [acc, acc]),
            out_specs=acc if last else [acc, acc],
            scratch_shapes=[pltpu.VMEM((total_rows, hid), jnp.float32)] * 2 if last else [],
        )(my_expert.reshape(1), *parts, *first_parts, w_gate, w_up, *gate_up)
        if last:
            hidden = outs
        else:
            gate_up = outs

    returned = []
    for at, step in spans(width, OUT_CUTS):
        half = total_rows // 2
        kept, away = call(
            down_kernel,
            [bf16(half, step)] * 2,
            (2 * total_rows * step * hid, 2 * step * hid),
            grid=(step // COLUMNS,),
            in_specs=[
                pl.BlockSpec((total_rows, hid), lambda j: (0, 0)),
                pl.BlockSpec((1, hid, COLUMNS), lambda j, at=at: (0, 0, at // COLUMNS + j)),
            ],
            out_specs=[pl.BlockSpec((half, COLUMNS), lambda j: (0, j))] * 2,
        )(hidden, w_down)
        got = exchanged(away, 1 << (in_bits - 1), 1)
        for bit in reversed(range(in_bits - 1)):
            total = kept.astype(jnp.float32) + got.astype(jnp.float32)
            half = total.shape[0] // 2
            kept = total[:half].astype(jnp.bfloat16)
            got = exchanged(total[half:].astype(jnp.bfloat16), 1 << bit, 1)
        results = call(
            sum_kernel,
            [bf16(block, step)] * GROUPS,
            (0, 6 * GROUPS * block * step),
            in_specs=[vmem, vmem],
            out_specs=[vmem] * GROUPS,
        )(kept, got)
        returned += [results[0]] + [exchanged(results[by], by, gsize) for by in range(1, GROUPS)]

    return call(
        functools.partial(mix_kernel, OUT_CUTS),
        bf16(batches, rows, width),
        (2 * GROUPS * block * batches * rows * width, 2 * 5 * batches * rows * width),
        in_specs=[vmem] * (1 + GROUPS * OUT_CUTS),
        out_specs=vmem,
    )(matrix, *returned)


def solution(mesh):
    split = P(None, ("rep", "grp"), None)
    stacked = P("grp", None, None)
    return jax.shard_map(
        body,
        mesh=mesh,
        in_specs=(split, split, split, stacked, stacked, stacked),
        out_specs=split,
        check_vma=False,
    )
```

time: 105 us -> 112 us (1.067)
  the two profiles are of different devices: /device:TPU:0 before, /device:TPU:12 now
where the time goes in v2:
time: 112 us; the launch traced here: 110 us
  starting transfers between devices  40.3 us (36%)
  Pallas kernels  36 us (32%)
  waiting for transfers between devices  22 us (20%)
  local copies, waits for them, and re-layouts  11.8 us (11%)
    ppermute x32, starting transfers between devices, exchanged(): lax.ppermute(shard, 'grp', [(i, (i // unit ^ by) * unit + i % unit) for i...  40.3 us
    pallas_call x2, Pallas kernels, body(): call(functools.partial(up_kernel, len(parts), k == 0, last, topk), bf16(t...  25.6 us
    ppermute x32, waiting for transfers between devices, exchanged(): lax.ppermute(shard, 'grp', [(i, (i // unit ^ by) * unit + i % unit) for i...  22 us
    unnamed x6, local copies, waits for them, and re-layouts  11.8 us
    pallas_call x2, Pallas kernels, body(): call(down_kernel, [bf16(half, step)] * 2, (2 * total_rows * step * hid, 2...  8.53 us
  transfers between devices with their start and end apart: 32, of which 12 were waited for; matrix products, arithmetic and copies ran while one was open for 0% of the time, Pallas kernels for 16%

profile of v2, /device:TPU:12, one launch (start us, length us, event | category | flops | bytes accessed | tf_op | source)
XLA Modules:
  0.0 110.3 jit_solution(8350004128414761001)
XLA Ops:
  3.2 1.6 %collective-permute-start.8 = (bf16[8,3712]{1,0:T(8,128)(2,1)S(1)}, bf16[8,3712]{1,0:T(8,128)(2,1)S(1)}, u32[]{:S(2)}, u32[]{:S(2)}) collective-permute-start(bf16[8,3712]{1,0:T(8,128)(2,1)S(1)} %get-tuple-element.54), channel_id=1, source_target_pairs={{0,2},{1,3},{2,0},{3,1},{4,6},{5,7},{6,4},{7,5},{8,10},{9,11},{10,... | collective-permute-start | bytes 178184 | tf_op jit(solution)/shard_map/ppermute | solution.py:22
  5.2 1.5 %collective-permute-start.10 = (bf16[8,3712]{1,0:T(8,128)(2,1)S(1)}, bf16[8,3712]{1,0:T(8,128)(2,1)S(1)}, u32[]{:S(2)}, u32[]{:S(2)}) collective-permute-start(bf16[8,3712]{1,0:T(8,128)(2,1)S(1)} %get-tuple-element.56), channel_id=1, source_target_pairs={{0,6},{1,7},{2,4},{3,5},{4,2},{5,3},{6,0},{7,1},{8,14},{9,15},{10,... | collective-permute-start | bytes 178184 | tf_op jit(solution)/shard_map/ppermute | solution.py:22
  6.7 2.6 %collective-permute-start.11 = (bf16[8,3712]{1,0:T(8,128)(2,1)S(1)}, bf16[8,3712]{1,0:T(8,128)(2,1)S(1)}, u32[]{:S(2)}, u32[]{:S(2)}) collective-permute-start(bf16[8,3712]{1,0:T(8,128)(2,1)S(1)} %get-tuple-element.57), channel_id=1, source_target_pairs={{0,8},{1,9},{2,10},{3,11},{4,12},{5,13},{6,14},{7,15},{8,0},{9,1},... | collective-permute-start | bytes 178184 | tf_op jit(solution)/shard_map/ppermute | solution.py:22
  9.3 1.3 %collective-permute-start.12 = (bf16[8,3712]{1,0:T(8,128)(2,1)S(1)}, bf16[8,3712]{1,0:T(8,128)(2,1)S(1)}, u32[]{:S(2)}, u32[]{:S(2)}) collective-permute-start(bf16[8,3712]{1,0:T(8,128)(2,1)S(1)} %get-tuple-element.58), channel_id=1, source_target_pairs={{0,10},{1,11},{2,8},{3,9},{4,14},{5,15},{6,12},{7,13},{8,2},{9,3},... | collective-permute-start | bytes 178184 | tf_op jit(solution)/shard_map/ppermute | solution.py:22
  10.6 1.6 %collective-permute-start.13 = (bf16[8,3712]{1,0:T(8,128)(2,1)S(1)}, bf16[8,3712]{1,0:T(8,128)(2,1)S(1)}, u32[]{:S(2)}, u32[]{:S(2)}) collective-permute-start(bf16[8,3712]{1,0:T(8,128)(2,1)S(1)} %get-tuple-element.59), channel_id=1, source_target_pairs={{0,12},{1,13},{2,14},{3,15},{4,8},{5,9},{6,10},{7,11},{8,4},{9,5},... | collective-permute-start | bytes 178184 | tf_op jit(solution)/shard_map/ppermute | solution.py:22
  12.6 1.5 %collective-permute-done.11.refs_4_ = bf16[8,3712]{1,0:T(8,128)(2,1)S(1)} collective-permute-done((bf16[8,3712]{1,0:T(8,128)(2,1)S(1)}, bf16[8,3712]{1,0:T(8,128)(2,1)S(1)}, u32[]{:S(2)}, u32[]{:S(2)}) %collective-permute-start.11) | collective-permute-done | bytes 59424 | tf_op jit(solution)/shard_map/ppermute | solution.py:22
  14.1 1.3 %collective-permute-done.12.refs_5_ = bf16[8,3712]{1,0:T(8,128)(2,1)S(1)} collective-permute-done((bf16[8,3712]{1,0:T(8,128)(2,1)S(1)}, bf16[8,3712]{1,0:T(8,128)(2,1)S(1)}, u32[]{:S(2)}, u32[]{:S(2)}) %collective-permute-start.12) | collective-permute-done | bytes 59424 | tf_op jit(solution)/shard_map/ppermute | solution.py:22
  15.4 2.8 %collective-permute-done.13.refs_6_ = bf16[8,3712]{1,0:T(8,128)(2,1)S(1)} collective-permute-done((bf16[8,3712]{1,0:T(8,128)(2,1)S(1)}, bf16[8,3712]{1,0:T(8,128)(2,1)S(1)}, u32[]{:S(2)}, u32[]{:S(2)}) %collective-permute-start.13) | collective-permute-done | bytes 59424 | tf_op jit(solution)/shard_map/ppermute | solution.py:22
  18.2 2.0 %collective-permute-done.14.refs_7_ = bf16[8,3712]{1,0:T(8,128)(2,1)S(1)} collective-permute-done((bf16[8,3712]{1,0:T(8,128)(2,1)S(1)}, bf16[8,3712]{1,0:T(8,128)(2,1)S(1)}, u32[]{:S(2)}, u32[]{:S(2)}) %collective-permute-start.14) | collective-permute-done | bytes 59424 | tf_op jit(solution)/shard_map/ppermute | solution.py:22
  22.4 1.6 %collective-permute-start.2 = (bf16[8,3584]{1,0:T(8,128)(2,1)S(1)}, bf16[8,3584]{1,0:T(8,128)(2,1)S(1)}, u32[]{:S(2)}, u32[]{:S(2)}) collective-permute-start(bf16[8,3584]{1,0:T(8,128)(2,1)S(1)} %get-tuple-element.48), channel_id=1, source_target_pairs={{0,6},{1,7},{2,4},{3,5},{4,2},{5,3},{6,0},{7,1},{8,14},{9,15},{10,... | collective-permute-start | bytes 172040 | tf_op jit(solution)/shard_map/ppermute | solution.py:22
  25.0 2.2 %collective-permute-start.4 = (bf16[8,3584]{1,0:T(8,128)(2,1)S(1)}, bf16[8,3584]{1,0:T(8,128)(2,1)S(1)}, u32[]{:S(2)}, u32[]{:S(2)}) collective-permute-start(bf16[8,3584]{1,0:T(8,128)(2,1)S(1)} %get-tuple-element.50), channel_id=1, source_target_pairs={{0,10},{1,11},{2,8},{3,9},{4,14},{5,15},{6,12},{7,13},{8,2},{9,3},... | collective-permute-start | bytes 172040 | tf_op jit(solution)/shard_map/ppermute | solution.py:22
  27.2 1.3 %collective-permute-start.5 = (bf16[8,3584]{1,0:T(8,128)(2,1)S(1)}, bf16[8,3584]{1,0:T(8,128)(2,1)S(1)}, u32[]{:S(2)}, u32[]{:S(2)}) collective-permute-start(bf16[8,3584]{1,0:T(8,128)(2,1)S(1)} %get-tuple-element.51), channel_id=1, source_target_pairs={{0,12},{1,13},{2,14},{3,15},{4,8},{5,9},{6,10},{7,11},{8,4},{9,5},... | collective-permute-start | bytes 172040 | tf_op jit(solution)/shard_map/ppermute | solution.py:22
  28.5 1.3 %collective-permute-start.6 = (bf16[8,3584]{1,0:T(8,128)(2,1)S(1)}, bf16[8,3584]{1,0:T(8,128)(2,1)S(1)}, u32[]{:S(2)}, u32[]{:S(2)}) collective-permute-start(bf16[8,3584]{1,0:T(8,128)(2,1)S(1)} %get-tuple-element.52), channel_id=1, source_target_pairs={{0,14},{1,15},{2,12},{3,13},{4,10},{5,11},{6,8},{7,9},{8,6},{9,7},... | collective-permute-start | bytes 172040 | tf_op jit(solution)/shard_map/ppermute | solution.py:22
  30.0 2.5 %collective-permute-done.4.refs_5_ = bf16[8,3584]{1,0:T(8,128)(2,1)S(1)} collective-permute-done((bf16[8,3584]{1,0:T(8,128)(2,1)S(1)}, bf16[8,3584]{1,0:T(8,128)(2,1)S(1)}, u32[]{:S(2)}, u32[]{:S(2)}) %collective-permute-start.4) | collective-permute-done | bytes 57376 | tf_op jit(solution)/shard_map/ppermute | solution.py:22
  32.5 3.7 %collective-permute-done.5.refs_6_ = bf16[8,3584]{1,0:T(8,128)(2,1)S(1)} collective-permute-done((bf16[8,3584]{1,0:T(8,128)(2,1)S(1)}, bf16[8,3584]{1,0:T(8,128)(2,1)S(1)}, u32[]{:S(2)}, u32[]{:S(2)}) %collective-permute-start.5) | collective-permute-done | bytes 57376 | tf_op jit(solution)/shard_map/ppermute | solution.py:22
  37.2 12.7 %shard_map.67 = (f32[128,2048]{1,0:T(8,128)S(1)}, f32[128,2048]{1,0:T(8,128)S(1)}) custom-call(s32[1]{0:T(128)} %bitcast.1.expert_ref, bf16[64,3712]{1,0:T(8,128)(2,1)S(1)} %shard_map.66.refs_0_.refs_2_, bf16[64,3712]{1,0:T(8,128)(2,1)S(1)} %collective-permute-done.15.refs_1_.refs_3_, bf16[64,3712]{1,0:T(8,128)(2,1)S(1)} %shard_map.66.refs_0_.refs_2_, ...), custom_call_target="tpu_custom_call" | custom-call | flops 3758096384 | bytes 29360128 | tf_op jit(solution)/shard_map/pallas_call | solution.py:223
  50.0 12.9 %shard_map.68.hidden_ref = bf16[128,2048]{1,0:T(8,128)(2,1)S(1)} custom-call(s32[1]{0:T(128)} %bitcast.1.expert_ref, bf16[64,3584]{1,0:T(8,128)(2,1)S(1)} %shard_map.65.refs_0_, bf16[64,3584]{1,0:T(8,128)(2,1)S(1)} %collective-permute-done.7.refs_1_, bf16[64,3712]{1,0:T(8,128)(2,1)S(1)} %shard_map.66.refs_0_.refs_2_, ...), custom_call_target="tpu_custom_call" | custom-call | flops 3758096384 | bytes 29360128 | tf_op jit(solution)/shard_map/pallas_call | solution.py:223
  62.8 9.3 %copy-done = bf16[1,2048,7168]{2,1,0:T(8,128)(2,1)S(1)} copy-done((bf16[1,2048,7168]{2,1,0:T(8,128)(2,1)S(1)}, bf16[1,2048,7168]{2,1,0:T(8,128)(2,1)}, u32[]{:S(2)}) %copy-start) | copy-done | bytes 29360152
  72.2 4.3 %shard_map.69 = (bf16[64,3584]{1,0:T(8,128)(2,1)S(1)}, bf16[64,3584]{1,0:T(8,128)(2,1)S(1)}) custom-call(bf16[128,2048]{1,0:T(8,128)(2,1)S(1)} %shard_map.68.hidden_ref, bf16[1,2048,7168]{2,1,0:T(8,128)(2,1)S(1)} %copy-done), custom_call_target="tpu_custom_call" | custom-call | flops 1879048192 | bytes 14680064 | tf_op jit(solution)/shard_map/pallas_call | solution.py:247
  76.9 4.3 %shard_map.71 = (bf16[64,3584]{1,0:T(8,128)(2,1)S(1)}, bf16[64,3584]{1,0:T(8,128)(2,1)S(1)}) custom-call(bf16[128,2048]{1,0:T(8,128)(2,1)S(1)} %shard_map.68.hidden_ref, bf16[1,2048,7168]{2,1,0:T(8,128)(2,1)S(1)} %copy-done), custom_call_target="tpu_custom_call" | custom-call | flops 1879048192 | bytes 14680064 | tf_op jit(solution)/shard_map/pallas_call | solution.py:247
  81.5 1.3 %collective-permute-start.17 = (bf16[8,3584]{1,0:T(8,128)(2,1)S(1)}, bf16[8,3584]{1,0:T(8,128)(2,1)S(1)}, u32[]{:S(2)}, u32[]{:S(2)}) collective-permute-start(bf16[8,3584]{1,0:T(8,128)(2,1)S(1)} %get-tuple-element.66), channel_id=1, source_target_pairs={{0,2},{1,3},{2,0},{3,1},{4,6},{5,7},{6,4},{7,5},{8,10},{9,11},{10,... | collective-permute-start | bytes 172040 | tf_op jit(solution)/shard_map/ppermute | solution.py:22
  82.7 2.3 %collective-permute-start.19 = (bf16[8,3584]{1,0:T(8,128)(2,1)S(1)}, bf16[8,3584]{1,0:T(8,128)(2,1)S(1)}, u32[]{:S(2)}, u32[]{:S(2)}) collective-permute-start(bf16[8,3584]{1,0:T(8,128)(2,1)S(1)} %get-tuple-element.68), channel_id=1, source_target_pairs={{0,6},{1,7},{2,4},{3,5},{4,2},{5,3},{6,0},{7,1},{8,14},{9,15},{10,... | collective-permute-start | bytes 172040 | tf_op jit(solution)/shard_map/ppermute | solution.py:22
  85.5 3.1 %collective-permute-start.21 = (bf16[8,3584]{1,0:T(8,128)(2,1)S(1)}, bf16[8,3584]{1,0:T(8,128)(2,1)S(1)}, u32[]{:S(2)}, u32[]{:S(2)}) collective-permute-start(bf16[8,3584]{1,0:T(8,128)(2,1)S(1)} %get-tuple-element.70), channel_id=1, source_target_pairs={{0,10},{1,11},{2,8},{3,9},{4,14},{5,15},{6,12},{7,13},{8,2},{9,3},... | collective-permute-start | bytes 172040 | tf_op jit(solution)/shard_map/ppermute | solution.py:22
  89.8 1.3 %collective-permute-start.23 = (bf16[8,3584]{1,0:T(8,128)(2,1)S(1)}, bf16[8,3584]{1,0:T(8,128)(2,1)S(1)}, u32[]{:S(2)}, u32[]{:S(2)}) collective-permute-start(bf16[8,3584]{1,0:T(8,128)(2,1)S(1)} %get-tuple-element.72), channel_id=1, source_target_pairs={{0,14},{1,15},{2,12},{3,13},{4,10},{5,11},{6,8},{7,9},{8,6},{9,7},... | collective-permute-start | bytes 172040 | tf_op jit(solution)/shard_map/ppermute | solution.py:22
  91.1 1.2 %collective-permute-start.25 = (bf16[8,3584]{1,0:T(8,128)(2,1)S(1)}, bf16[8,3584]{1,0:T(8,128)(2,1)S(1)}, u32[]{:S(2)}, u32[]{:S(2)}) collective-permute-start(bf16[8,3584]{1,0:T(8,128)(2,1)S(1)} %get-tuple-element.76), channel_id=1, source_target_pairs={{0,2},{1,3},{2,0},{3,1},{4,6},{5,7},{6,4},{7,5},{8,10},{9,11},{10,... | collective-permute-start | bytes 172040 | tf_op jit(solution)/shard_map/ppermute | solution.py:22
  92.3 1.8 %collective-permute-start.26 = (bf16[8,3584]{1,0:T(8,128)(2,1)S(1)}, bf16[8,3584]{1,0:T(8,128)(2,1)S(1)}, u32[]{:S(2)}, u32[]{:S(2)}) collective-permute-start(bf16[8,3584]{1,0:T(8,128)(2,1)S(1)} %get-tuple-element.77), channel_id=1, source_target_pairs={{0,4},{1,5},{2,6},{3,7},{4,0},{5,1},{6,2},{7,3},{8,12},{9,13},{10,... | collective-permute-start | bytes 172040 | tf_op jit(solution)/shard_map/ppermute | solution.py:22
  94.1 2.9 %collective-permute-start.27 = (bf16[8,3584]{1,0:T(8,128)(2,1)S(1)}, bf16[8,3584]{1,0:T(8,128)(2,1)S(1)}, u32[]{:S(2)}, u32[]{:S(2)}) collective-permute-start(bf16[8,3584]{1,0:T(8,128)(2,1)S(1)} %get-tuple-element.78), channel_id=1, source_target_pairs={{0,6},{1,7},{2,4},{3,5},{4,2},{5,3},{6,0},{7,1},{8,14},{9,15},{10,... | collective-permute-start | bytes 172040 | tf_op jit(solution)/shard_map/ppermute | solution.py:22
  97.9 2.6 %collective-permute-start.29 = (bf16[8,3584]{1,0:T(8,128)(2,1)S(1)}, bf16[8,3584]{1,0:T(8,128)(2,1)S(1)}, u32[]{:S(2)}, u32[]{:S(2)}) collective-permute-start(bf16[8,3584]{1,0:T(8,128)(2,1)S(1)} %get-tuple-element.80), channel_id=1, source_target_pairs={{0,10},{1,11},{2,8},{3,9},{4,14},{5,15},{6,12},{7,13},{8,2},{9,3},... | collective-permute-start | bytes 172040 | tf_op jit(solution)/shard_map/ppermute | solution.py:22
  100.5 1.2 %collective-permute-start.30 = (bf16[8,3584]{1,0:T(8,128)(2,1)S(1)}, bf16[8,3584]{1,0:T(8,128)(2,1)S(1)}, u32[]{:S(2)}, u32[]{:S(2)}) collective-permute-start(bf16[8,3584]{1,0:T(8,128)(2,1)S(1)} %get-tuple-element.81), channel_id=1, source_target_pairs={{0,12},{1,13},{2,14},{3,15},{4,8},{5,9},{6,10},{7,11},{8,4},{9,5},... | collective-permute-start | bytes 172040 | tf_op jit(solution)/shard_map/ppermute | solution.py:22
  101.7 1.2 %collective-permute-start.31 = (bf16[8,3584]{1,0:T(8,128)(2,1)S(1)}, bf16[8,3584]{1,0:T(8,128)(2,1)S(1)}, u32[]{:S(2)}, u32[]{:S(2)}) collective-permute-start(bf16[8,3584]{1,0:T(8,128)(2,1)S(1)} %get-tuple-element.82), channel_id=1, source_target_pairs={{0,14},{1,15},{2,12},{3,13},{4,10},{5,11},{6,8},{7,9},{8,6},{9,7},... | collective-permute-start | bytes 172040 | tf_op jit(solution)/shard_map/ppermute | solution.py:22
  102.9 2.2 %collective-permute-done.29.refs_13_ = bf16[8,3584]{1,0:T(8,128)(2,1)S(1)} collective-permute-done((bf16[8,3584]{1,0:T(8,128)(2,1)S(1)}, bf16[8,3584]{1,0:T(8,128)(2,1)S(1)}, u32[]{:S(2)}, u32[]{:S(2)}) %collective-permute-start.29) | collective-permute-done | bytes 57376 | tf_op jit(solution)/shard_map/ppermute | solution.py:22
  105.1 3.1 %collective-permute-done.30.refs_14_ = bf16[8,3584]{1,0:T(8,128)(2,1)S(1)} collective-permute-done((bf16[8,3584]{1,0:T(8,128)(2,1)S(1)}, bf16[8,3584]{1,0:T(8,128)(2,1)S(1)}, u32[]{:S(2)}, u32[]{:S(2)}) %collective-permute-start.30) | collective-permute-done | bytes 57376 | tf_op jit(solution)/shard_map/ppermute | solution.py:22
  (48 shorter events, 13.8 us)
Async XLA Ops:
  3.2 7.4 %collective-permute-start.8 = (bf16[8,3712]{1,0:T(8,128)(2,1)S(1)}, bf16[8,3712]{1,0:T(8,128)(2,1)S(1)}, u32[]{:S(2)}, u32[]{:S(2)}) collective-permute-start(bf16[8,3712]{1,0:T(8,128)(2,1)S(1)} %get-tuple-element.54), channel_id=1, source_target_pairs={{0,2},{1,3},{2,0},{3,1},{4,6},{5,7},{6,4},{7,5},{8,10},{9,11},{10,... | collective-permute-start | bytes 178184 | tf_op jit(solution)/shard_map/ppermute | solution.py:22
  4.7 7.4 %collective-permute-start.9 = (bf16[8,3712]{1,0:T(8,128)(2,1)S(1)}, bf16[8,3712]{1,0:T(8,128)(2,1)S(1)}, u32[]{:S(2)}, u32[]{:S(2)}) collective-permute-start(bf16[8,3712]{1,0:T(8,128)(2,1)S(1)} %get-tuple-element.55), channel_id=1, source_target_pairs={{0,4},{1,5},{2,6},{3,7},{4,0},{5,1},{6,2},{7,3},{8,12},{9,13},{10,... | collective-permute-start | bytes 178184 | tf_op jit(solution)/shard_map/ppermute | solution.py:22
  5.2 7.4 %collective-permute-start.10 = (bf16[8,3712]{1,0:T(8,128)(2,1)S(1)}, bf16[8,3712]{1,0:T(8,128)(2,1)S(1)}, u32[]{:S(2)}, u32[]{:S(2)}) collective-permute-start(bf16[8,3712]{1,0:T(8,128)(2,1)S(1)} %get-tuple-element.56), channel_id=1, source_target_pairs={{0,6},{1,7},{2,4},{3,5},{4,2},{5,3},{6,0},{7,1},{8,14},{9,15},{10,... | collective-permute-start | bytes 178184 | tf_op jit(solution)/shard_map/ppermute | solution.py:22
  6.7 7.4 %collective-permute-start.11 = (bf16[8,3712]{1,0:T(8,128)(2,1)S(1)}, bf16[8,3712]{1,0:T(8,128)(2,1)S(1)}, u32[]{:S(2)}, u32[]{:S(2)}) collective-permute-start(bf16[8,3712]{1,0:T(8,128)(2,1)S(1)} %get-tuple-element.57), channel_id=1, source_target_pairs={{0,8},{1,9},{2,10},{3,11},{4,12},{5,13},{6,14},{7,15},{8,0},{9,1},... | collective-permute-start | bytes 178184 | tf_op jit(solution)/shard_map/ppermute | solution.py:22
  9.3 6.1 %collective-permute-start.12 = (bf16[8,3712]{1,0:T(8,128)(2,1)S(1)}, bf16[8,3712]{1,0:T(8,128)(2,1)S(1)}, u32[]{:S(2)}, u32[]{:S(2)}) collective-permute-start(bf16[8,3712]{1,0:T(8,128)(2,1)S(1)} %get-tuple-element.58), channel_id=1, source_target_pairs={{0,10},{1,11},{2,8},{3,9},{4,14},{5,15},{6,12},{7,13},{8,2},{9,3},... | collective-permute-start | bytes 178184 | tf_op jit(solution)/shard_map/ppermute | solution.py:22
  10.6 7.6 %collective-permute-start.13 = (bf16[8,3712]{1,0:T(8,128)(2,1)S(1)}, bf16[8,3712]{1,0:T(8,128)(2,1)S(1)}, u32[]{:S(2)}, u32[]{:S(2)}) collective-permute-start(bf16[8,3712]{1,0:T(8,128)(2,1)S(1)} %get-tuple-element.59), channel_id=1, source_target_pairs={{0,12},{1,13},{2,14},{3,15},{4,8},{5,9},{6,10},{7,11},{8,4},{9,5},... | collective-permute-start | bytes 178184 | tf_op jit(solution)/shard_map/ppermute | solution.py:22
  12.2 8.1 %collective-permute-start.14 = (bf16[8,3712]{1,0:T(8,128)(2,1)S(1)}, bf16[8,3712]{1,0:T(8,128)(2,1)S(1)}, u32[]{:S(2)}, u32[]{:S(2)}) collective-permute-start(bf16[8,3712]{1,0:T(8,128)(2,1)S(1)} %get-tuple-element.60), channel_id=1, source_target_pairs={{0,14},{1,15},{2,12},{3,13},{4,10},{5,11},{6,8},{7,9},{8,6},{9,7},... | collective-permute-start | bytes 178184 | tf_op jit(solution)/shard_map/ppermute | solution.py:22
  20.3 16.9 %collective-permute-start.15 = (bf16[64,3712]{1,0:T(8,128)(2,1)S(1)}, bf16[64,3712]{1,0:T(8,128)(2,1)S(1)}, u32[]{:S(2)}, u32[]{:S(2)}) collective-permute-start(bf16[64,3712]{1,0:T(8,128)(2,1)S(1)} %shard_map.66.refs_0_.refs_2_), channel_id=1, source_target_pairs={{0,1},{1,0},{2,3},{3,2},{4,5},{5,4},{6,7},{7,6},{8,9},{9,8},{10,11... | collective-permute-start | bytes 1425416 | tf_op jit(solution)/shard_map/ppermute | solution.py:22
  20.4 4.7 %collective-permute-start = (bf16[8,3584]{1,0:T(8,128)(2,1)S(1)}, bf16[8,3584]{1,0:T(8,128)(2,1)S(1)}, u32[]{:S(2)}, u32[]{:S(2)}) collective-permute-start(bf16[8,3584]{1,0:T(8,128)(2,1)S(1)} %get-tuple-element.46), channel_id=1, source_target_pairs={{0,2},{1,3},{2,0},{3,1},{4,6},{5,7},{6,4},{7,5},{8,10},{9,11},{10,... | collective-permute-start | bytes 172040 | tf_op jit(solution)/shard_map/ppermute | solution.py:22
  21.4 5.9 %collective-permute-start.1 = (bf16[8,3584]{1,0:T(8,128)(2,1)S(1)}, bf16[8,3584]{1,0:T(8,128)(2,1)S(1)}, u32[]{:S(2)}, u32[]{:S(2)}) collective-permute-start(bf16[8,3584]{1,0:T(8,128)(2,1)S(1)} %get-tuple-element.47), channel_id=1, source_target_pairs={{0,4},{1,5},{2,6},{3,7},{4,0},{5,1},{6,2},{7,3},{8,12},{9,13},{10,... | collective-permute-start | bytes 172040 | tf_op jit(solution)/shard_map/ppermute | solution.py:22
  22.4 6.2 %collective-permute-start.2 = (bf16[8,3584]{1,0:T(8,128)(2,1)S(1)}, bf16[8,3584]{1,0:T(8,128)(2,1)S(1)}, u32[]{:S(2)}, u32[]{:S(2)}) collective-permute-start(bf16[8,3584]{1,0:T(8,128)(2,1)S(1)} %get-tuple-element.48), channel_id=1, source_target_pairs={{0,6},{1,7},{2,4},{3,5},{4,2},{5,3},{6,0},{7,1},{8,14},{9,15},{10,... | collective-permute-start | bytes 172040 | tf_op jit(solution)/shard_map/ppermute | solution.py:22
  23.9 6.1 %collective-permute-start.3 = (bf16[8,3584]{1,0:T(8,128)(2,1)S(1)}, bf16[8,3584]{1,0:T(8,128)(2,1)S(1)}, u32[]{:S(2)}, u32[]{:S(2)}) collective-permute-start(bf16[8,3584]{1,0:T(8,128)(2,1)S(1)} %get-tuple-element.49), channel_id=1, source_target_pairs={{0,8},{1,9},{2,10},{3,11},{4,12},{5,13},{6,14},{7,15},{8,0},{9,1},... | collective-permute-start | bytes 172040 | tf_op jit(solution)/shard_map/ppermute | solution.py:22
  25.0 7.4 %collective-permute-start.4 = (bf16[8,3584]{1,0:T(8,128)(2,1)S(1)}, bf16[8,3584]{1,0:T(8,128)(2,1)S(1)}, u32[]{:S(2)}, u32[]{:S(2)}) collective-permute-start(bf16[8,3584]{1,0:T(8,128)(2,1)S(1)} %get-tuple-element.50), channel_id=1, source_target_pairs={{0,10},{1,11},{2,8},{3,9},{4,14},{5,15},{6,12},{7,13},{8,2},{9,3},... | collective-permute-start | bytes 172040 | tf_op jit(solution)/shard_map/ppermute | solution.py:22
  27.2 9.0 %collective-permute-start.5 = (bf16[8,3584]{1,0:T(8,128)(2,1)S(1)}, bf16[8,3584]{1,0:T(8,128)(2,1)S(1)}, u32[]{:S(2)}, u32[]{:S(2)}) collective-permute-start(bf16[8,3584]{1,0:T(8,128)(2,1)S(1)} %get-tuple-element.51), channel_id=1, source_target_pairs={{0,12},{1,13},{2,14},{3,15},{4,8},{5,9},{6,10},{7,11},{8,4},{9,5},... | collective-permute-start | bytes 172040 | tf_op jit(solution)/shard_map/ppermute | solution.py:22
  28.5 8.5 %collective-permute-start.6 = (bf16[8,3584]{1,0:T(8,128)(2,1)S(1)}, bf16[8,3584]{1,0:T(8,128)(2,1)S(1)}, u32[]{:S(2)}, u32[]{:S(2)}) collective-permute-start(bf16[8,3584]{1,0:T(8,128)(2,1)S(1)} %get-tuple-element.52), channel_id=1, source_target_pairs={{0,14},{1,15},{2,12},{3,13},{4,10},{5,11},{6,8},{7,9},{8,6},{9,7},... | collective-permute-start | bytes 172040 | tf_op jit(solution)/shard_map/ppermute | solution.py:22
  37.1 12.8 %collective-permute-start.7 = (bf16[64,3584]{1,0:T(8,128)(2,1)S(1)}, bf16[64,3584]{1,0:T(8,128)(2,1)S(1)}, u32[]{:S(2)}, u32[]{:S(2)}) collective-permute-start(bf16[64,3584]{1,0:T(8,128)(2,1)S(1)} %shard_map.65.refs_0_), channel_id=1, source_target_pairs={{0,1},{1,0},{2,3},{3,2},{4,5},{5,4},{6,7},{7,6},{8,9},{9,8},{10,11... | collective-permute-start | bytes 1376264 | tf_op jit(solution)/shard_map/ppermute | solution.py:22
  76.4 4.9 %collective-permute-start.16 = (bf16[64,3584]{1,0:T(8,128)(2,1)S(1)}, bf16[64,3584]{1,0:T(8,128)(2,1)S(1)}, u32[]{:S(2)}, u32[]{:S(2)}) collective-permute-start(bf16[64,3584]{1,0:T(8,128)(2,1)S(1)} %get-tuple-element.64), channel_id=1, source_target_pairs={{0,1},{1,0},{2,3},{3,2},{4,5},{5,4},{6,7},{7,6},{8,9},{9,8},{10,11... | collective-permute-start | bytes 1376264 | tf_op jit(solution)/shard_map/ppermute | solution.py:22
  81.2 4.3 %collective-permute-start.24 = (bf16[64,3584]{1,0:T(8,128)(2,1)S(1)}, bf16[64,3584]{1,0:T(8,128)(2,1)S(1)}, u32[]{:S(2)}, u32[]{:S(2)}) collective-permute-start(bf16[64,3584]{1,0:T(8,128)(2,1)S(1)} %get-tuple-element.74), channel_id=1, source_target_pairs={{0,1},{1,0},{2,3},{3,2},{4,5},{5,4},{6,7},{7,6},{8,9},{9,8},{10,11... | collective-permute-start | bytes 1376264 | tf_op jit(solution)/shard_map/ppermute | solution.py:22
  81.5 7.2 %collective-permute-start.17 = (bf16[8,3584]{1,0:T(8,128)(2,1)S(1)}, bf16[8,3584]{1,0:T(8,128)(2,1)S(1)}, u32[]{:S(2)}, u32[]{:S(2)}) collective-permute-start(bf16[8,3584]{1,0:T(8,128)(2,1)S(1)} %get-tuple-element.66), channel_id=1, source_target_pairs={{0,2},{1,3},{2,0},{3,1},{4,6},{5,7},{6,4},{7,5},{8,10},{9,11},{10,... | collective-permute-start | bytes 172040 | tf_op jit(solution)/shard_map/ppermute | solution.py:22
  82.7 7.0 %collective-permute-start.18 = (bf16[8,3584]{1,0:T(8,128)(2,1)S(1)}, bf16[8,3584]{1,0:T(8,128)(2,1)S(1)}, u32[]{:S(2)}, u32[]{:S(2)}) collective-permute-start(bf16[8,3584]{1,0:T(8,128)(2,1)S(1)} %get-tuple-element.67), channel_id=1, source_target_pairs={{0,4},{1,5},{2,6},{3,7},{4,0},{5,1},{6,2},{7,3},{8,12},{9,13},{10,... | collective-permute-start | bytes 172040 | tf_op jit(solution)/shard_map/ppermute | solution.py:22
  82.7 8.3 %collective-permute-start.19 = (bf16[8,3584]{1,0:T(8,128)(2,1)S(1)}, bf16[8,3584]{1,0:T(8,128)(2,1)S(1)}, u32[]{:S(2)}, u32[]{:S(2)}) collective-permute-start(bf16[8,3584]{1,0:T(8,128)(2,1)S(1)} %get-tuple-element.68), channel_id=1, source_target_pairs={{0,6},{1,7},{2,4},{3,5},{4,2},{5,3},{6,0},{7,1},{8,14},{9,15},{10,... | collective-permute-start | bytes 172040 | tf_op jit(solution)/shard_map/ppermute | solution.py:22
  85.0 7.3 %collective-permute-start.20 = (bf16[8,3584]{1,0:T(8,128)(2,1)S(1)}, bf16[8,3584]{1,0:T(8,128)(2,1)S(1)}, u32[]{:S(2)}, u32[]{:S(2)}) collective-permute-start(bf16[8,3584]{1,0:T(8,128)(2,1)S(1)} %get-tuple-element.69), channel_id=1, source_target_pairs={{0,8},{1,9},{2,10},{3,11},{4,12},{5,13},{6,14},{7,15},{8,0},{9,1},... | collective-permute-start | bytes 172040 | tf_op jit(solution)/shard_map/ppermute | solution.py:22
  85.5 8.6 %collective-permute-start.21 = (bf16[8,3584]{1,0:T(8,128)(2,1)S(1)}, bf16[8,3584]{1,0:T(8,128)(2,1)S(1)}, u32[]{:S(2)}, u32[]{:S(2)}) collective-permute-start(bf16[8,3584]{1,0:T(8,128)(2,1)S(1)} %get-tuple-element.70), channel_id=1, source_target_pairs={{0,10},{1,11},{2,8},{3,9},{4,14},{5,15},{6,12},{7,13},{8,2},{9,3},... | collective-permute-start | bytes 172040 | tf_op jit(solution)/shard_map/ppermute | solution.py:22
  88.7 8.3 %collective-permute-start.22 = (bf16[8,3584]{1,0:T(8,128)(2,1)S(1)}, bf16[8,3584]{1,0:T(8,128)(2,1)S(1)}, u32[]{:S(2)}, u32[]{:S(2)}) collective-permute-start(bf16[8,3584]{1,0:T(8,128)(2,1)S(1)} %get-tuple-element.71), channel_id=1, source_target_pairs={{0,12},{1,13},{2,14},{3,15},{4,8},{5,9},{6,10},{7,11},{8,4},{9,5},... | collective-permute-start | bytes 172040 | tf_op jit(solution)/shard_map/ppermute | solution.py:22
  89.8 8.1 %collective-permute-start.23 = (bf16[8,3584]{1,0:T(8,128)(2,1)S(1)}, bf16[8,3584]{1,0:T(8,128)(2,1)S(1)}, u32[]{:S(2)}, u32[]{:S(2)}) collective-permute-start(bf16[8,3584]{1,0:T(8,128)(2,1)S(1)} %get-tuple-element.72), channel_id=1, source_target_pairs={{0,14},{1,15},{2,12},{3,13},{4,10},{5,11},{6,8},{7,9},{8,6},{9,7},... | collective-permute-start | bytes 172040 | tf_op jit(solution)/shard_map/ppermute | solution.py:22
  91.1 9.5 %collective-permute-start.25 = (bf16[8,3584]{1,0:T(8,128)(2,1)S(1)}, bf16[8,3584]{1,0:T(8,128)(2,1)S(1)}, u32[]{:S(2)}, u32[]{:S(2)}) collective-permute-start(bf16[8,3584]{1,0:T(8,128)(2,1)S(1)} %get-tuple-element.76), channel_id=1, source_target_pairs={{0,2},{1,3},{2,0},{3,1},{4,6},{5,7},{6,4},{7,5},{8,10},{9,11},{10,... | collective-permute-start | bytes 172040 | tf_op jit(solution)/shard_map/ppermute | solution.py:22
  92.3 9.4 %collective-permute-start.26 = (bf16[8,3584]{1,0:T(8,128)(2,1)S(1)}, bf16[8,3584]{1,0:T(8,128)(2,1)S(1)}, u32[]{:S(2)}, u32[]{:S(2)}) collective-permute-start(bf16[8,3584]{1,0:T(8,128)(2,1)S(1)} %get-tuple-element.77), channel_id=1, source_target_pairs={{0,4},{1,5},{2,6},{3,7},{4,0},{5,1},{6,2},{7,3},{8,12},{9,13},{10,... | collective-permute-start | bytes 172040 | tf_op jit(solution)/shard_map/ppermute | solution.py:22
  94.1 8.8 %collective-permute-start.27 = (bf16[8,3584]{1,0:T(8,128)(2,1)S(1)}, bf16[8,3584]{1,0:T(8,128)(2,1)S(1)}, u32[]{:S(2)}, u32[]{:S(2)}) collective-permute-start(bf16[8,3584]{1,0:T(8,128)(2,1)S(1)} %get-tuple-element.78), channel_id=1, source_target_pairs={{0,6},{1,7},{2,4},{3,5},{4,2},{5,3},{6,0},{7,1},{8,14},{9,15},{10,... | collective-permute-start | bytes 172040 | tf_op jit(solution)/shard_map/ppermute | solution.py:22
  97.0 5.9 %collective-permute-start.28 = (bf16[8,3584]{1,0:T(8,128)(2,1)S(1)}, bf16[8,3584]{1,0:T(8,128)(2,1)S(1)}, u32[]{:S(2)}, u32[]{:S(2)}) collective-permute-start(bf16[8,3584]{1,0:T(8,128)(2,1)S(1)} %get-tuple-element.79), channel_id=1, source_target_pairs={{0,8},{1,9},{2,10},{3,11},{4,12},{5,13},{6,14},{7,15},{8,0},{9,1},... | collective-permute-start | bytes 172040 | tf_op jit(solution)/shard_map/ppermute | solution.py:22
  97.9 7.2 %collective-permute-start.29 = (bf16[8,3584]{1,0:T(8,128)(2,1)S(1)}, bf16[8,3584]{1,0:T(8,128)(2,1)S(1)}, u32[]{:S(2)}, u32[]{:S(2)}) collective-permute-start(bf16[8,3584]{1,0:T(8,128)(2,1)S(1)} %get-tuple-element.80), channel_id=1, source_target_pairs={{0,10},{1,11},{2,8},{3,9},{4,14},{5,15},{6,12},{7,13},{8,2},{9,3},... | collective-permute-start | bytes 172040 | tf_op jit(solution)/shard_map/ppermute | solution.py:22
  100.5 7.7 %collective-permute-start.30 = (bf16[8,3584]{1,0:T(8,128)(2,1)S(1)}, bf16[8,3584]{1,0:T(8,128)(2,1)S(1)}, u32[]{:S(2)}, u32[]{:S(2)}) collective-permute-start(bf16[8,3584]{1,0:T(8,128)(2,1)S(1)} %get-tuple-element.81), channel_id=1, source_target_pairs={{0,12},{1,13},{2,14},{3,15},{4,8},{5,9},{6,10},{7,11},{8,4},{9,5},... | collective-permute-start | bytes 172040 | tf_op jit(solution)/shard_map/ppermute | solution.py:22
  101.7 7.6 %collective-permute-start.31 = (bf16[8,3584]{1,0:T(8,128)(2,1)S(1)}, bf16[8,3584]{1,0:T(8,128)(2,1)S(1)}, u32[]{:S(2)}, u32[]{:S(2)}) collective-permute-start(bf16[8,3584]{1,0:T(8,128)(2,1)S(1)} %get-tuple-element.82), channel_id=1, source_target_pairs={{0,14},{1,15},{2,12},{3,13},{4,10},{5,11},{6,8},{7,9},{8,6},{9,7},... | collective-permute-start | bytes 172040 | tf_op jit(solution)/shard_map/ppermute | solution.py:22
  (2 other events, 10.3 us)

commit v3 on v1

v3 whole, which is shorter than its diff:
```python
import functools

import jax
import jax.numpy as jnp
from jax import lax
from jax.experimental import pallas as pl
from jax.experimental.pallas import tpu as pltpu
from jax.sharding import PartitionSpec as P

GROUPS = 8
EXP_GRP = 2
EXTRA = 128
DEPTH = 512
COLUMNS = 512
AHEAD = 4


def exchanged(shard, by, unit):
    size = lax.axis_size("grp")
    return lax.ppermute(
        shard, "grp", [(i, ((i // unit) ^ by) * unit + i % unit) for i in range(size)]
    )


def call(kernel, out_shape, cost, limit=16 << 20, **kwargs):
    flops, moved = cost
    return pl.pallas_call(
        kernel,
        out_shape=out_shape,
        compiler_params=pltpu.CompilerParams(vmem_limit_bytes=limit),
        cost_estimate=pl.CostEstimate(flops=flops, bytes_accessed=moved, transcendentals=0),
        **kwargs,
    )


def bf16(*shape):
    return jax.ShapeDtypeStruct(shape, jnp.bfloat16)


def f32(*shape):
    return jax.ShapeDtypeStruct(shape, jnp.float32)


def iota(shape, dim):
    return lax.broadcasted_iota(jnp.int32, shape, dim)


def slot_matrix(group_me, ids, batches, rows):
    cap = rows // 2
    count = batches * rows
    block = batches * cap
    eye = (iota((count, count), 0) == iota((count, count), 1)).astype(jnp.float32)
    across = lax.dot_general(ids, eye, (((0,), (0,)), ((), ())), preferred_element_type=jnp.float32)
    across = across.astype(jnp.int32)
    shape = (GROUPS * block, count)
    where = iota(shape, 0)
    lane = iota(shape, 1)
    target = group_me ^ (where // block)
    routed = jnp.zeros(shape, jnp.float32)
    for k in range(ids.shape[1]):
        routed = jnp.where(across[k : k + 1, :] // EXP_GRP == target, 1.0, routed)
    above, here = iota((count, count), 0), iota((count, count), 1)
    before = jnp.where((above < here) & (above // rows == here // rows), 1.0, 0.0)
    slots = jnp.dot(routed, before, preferred_element_type=jnp.float32).astype(jnp.int32)
    taken = (slots == where % cap) & (lane // rows == where % block // cap)
    return jnp.where(taken, routed, 0.0).astype(jnp.bfloat16)


def prep_kernel(topk, group_ref, tokens_ref, extra_ref, matrix_ref, *out_refs):
    batches, rows, width = tokens_ref.shape
    extra = extra_ref[...]
    matrix = slot_matrix(group_ref[0], extra[:, :topk].astype(jnp.float32), batches, rows)
    matrix_ref[...] = matrix
    block = matrix.shape[0] // GROUPS
    tokens = tokens_ref[...].reshape(batches * rows, width)
    bucket = jnp.dot(matrix, tokens, preferred_element_type=jnp.float32)
    more = jnp.dot(matrix, extra, preferred_element_type=jnp.float32)
    for t, out in enumerate(out_refs):
        out[:, :width] = bucket[t * block : (t + 1) * block].astype(jnp.bfloat16)
        out[:, width:] = more[t * block : (t + 1) * block].astype(jnp.bfloat16)


def join_kernel(*refs):
    refs[-1][...] = jnp.concatenate(
        [r[...].astype(jnp.float32) for r in refs[:-1]], axis=0
    ).astype(jnp.bfloat16)


def fetch_kernel(after_ref, w_ref, out_ref, sem):
    del after_ref
    copies = [
        pltpu.make_async_copy(
            w_ref.at[0, d : d + DEPTH], out_ref.at[d : d + DEPTH], sem.at[d // DEPTH]
        )
        for d in range(0, out_ref.shape[0], DEPTH)
    ]
    for copy in copies:
        copy.start()
    for copy in copies:
        copy.wait()


def expert_kernel(parts, topk, expert_ref, *refs):
    xs, refs = refs[:parts], refs[parts:]
    w_gate_ref, w_up_ref, w_down_ref, kept_ref, away_ref = refs[:5]
    gate_acc, up_acc, hidden, up_slots, up_sem, down_slots, down_sem = refs[5:]
    half, width = kept_ref.shape
    ups, downs = width // DEPTH, width // COLUMNS
    copies = [
        pltpu.make_async_copy(
            w_up_ref.at[0, i * DEPTH : (i + 1) * DEPTH],
            up_slots.at[i % AHEAD],
            up_sem.at[i % AHEAD],
        )
        for i in range(ups)
    ] + [
        pltpu.make_async_copy(
            w_down_ref.at[0, :, j * COLUMNS : (j + 1) * COLUMNS],
            down_slots.at[j % AHEAD],
            down_sem.at[j % AHEAD],
        )
        for j in range(downs)
    ]
    for copy in copies[:AHEAD]:
        copy.start()

    for i in range(ups):
        here = slice(i * DEPTH, (i + 1) * DEPTH)
        x = jnp.concatenate([r[:, here] for r in xs], axis=0)
        gate = jnp.dot(x, w_gate_ref[here], preferred_element_type=jnp.float32)
        if i == 0:
            gate_acc[...] = gate
        else:
            gate_acc[...] += gate
        copies[i].wait()
        up = jnp.dot(x, up_slots[i % AHEAD], preferred_element_type=jnp.float32)
        if i == 0:
            up_acc[...] = up
        else:
            up_acc[...] += up
        copies[i + AHEAD].start()

    extra = jnp.concatenate([r[:, width:].astype(jnp.float32) for r in xs], axis=0)
    expert = expert_ref[0].astype(jnp.float32)
    column = jnp.zeros((extra.shape[0], 1), jnp.float32)
    for k in range(topk):
        column += jnp.where(
            extra[:, k : k + 1] == expert, extra[:, topk + k : topk + k + 1], 0.0
        )
    hidden[...] = (jax.nn.silu(gate_acc[...]) * up_acc[...] * column).astype(jnp.bfloat16)

    for j in range(downs):
        copies[ups + j].wait()
        total = jnp.dot(hidden[...], down_slots[j % AHEAD], preferred_element_type=jnp.float32)
        here = slice(j * COLUMNS, (j + 1) * COLUMNS)
        kept_ref[:, here] = total[:half].astype(jnp.bfloat16)
        away_ref[:, here] = total[half:].astype(jnp.bfloat16)
        if j + AHEAD < downs:
            copies[ups + j + AHEAD].start()


def sum_kernel(kept_ref, got_ref, *out_refs):
    total = kept_ref[...].astype(jnp.float32) + got_ref[...].astype(jnp.float32)
    block = out_refs[0].shape[0]
    for t, out in enumerate(out_refs):
        out[...] = total[t * block : (t + 1) * block].astype(jnp.bfloat16)


def mix_kernel(matrix_ref, *refs):
    out_ref = refs[-1]
    batches, rows, width = out_ref.shape
    back = jnp.concatenate([r[...].astype(jnp.float32) for r in refs[:-1]], axis=0)
    mixed = lax.dot_general(
        matrix_ref[...],
        back.astype(jnp.bfloat16),
        (((0,), (0,)), ((), ())),
        preferred_element_type=jnp.float32,
    )
    for b in range(batches):
        out_ref[b] = mixed[b * rows : (b + 1) * rows].astype(jnp.bfloat16)


def body(tokens, expert_ids, gate_weights, w_gate, w_up, w_down):
    devices = lax.axis_size("grp")
    gsize = devices // GROUPS
    in_bits = gsize.bit_length() - 1
    rank = lax.axis_index("grp")
    group_me = (rank // gsize).astype(jnp.int32)
    my_expert = (group_me * EXP_GRP + rank % gsize // (gsize // EXP_GRP)).astype(jnp.int32)
    batches, rows, width = tokens.shape
    count = batches * rows
    topk = expert_ids.shape[2]
    block = batches * (rows // 2)
    hid = w_gate.shape[2]
    total_rows = gsize * GROUPS * block
    half = total_rows // 2
    wide = width + EXTRA
    smem = pl.BlockSpec(memory_space=pltpu.SMEM)
    vmem = pl.BlockSpec(memory_space=pltpu.VMEM)
    hbm = pl.BlockSpec(memory_space=pl.ANY)

    def to_all(blocks):
        got = {by: exchanged(blocks[by], by, gsize) for by in reversed(range(1, GROUPS))}
        return [blocks[0]] + [got[by] for by in range(1, GROUPS)]

    extra = jnp.concatenate(
        [
            expert_ids.astype(jnp.bfloat16),
            gate_weights,
            jnp.zeros((batches, rows, EXTRA - 2 * topk), jnp.bfloat16),
        ],
        axis=2,
    ).reshape(count, EXTRA)
    matrix, *buckets = call(
        functools.partial(prep_kernel, topk),
        [bf16(GROUPS * block, count)] + [bf16(block, wide)] * GROUPS,
        (2 * GROUPS * block * count * wide, 10 * count * wide),
        in_specs=[smem, vmem, vmem],
        out_specs=[vmem] * (1 + GROUPS),
    )(group_me.reshape(1), tokens, extra)
    fetched = call(
        fetch_kernel,
        pltpu.VMEM((width, hid), jnp.bfloat16),
        (0, 4 * width * hid),
        in_specs=[hbm, hbm],
        out_specs=vmem,
        scratch_shapes=[pltpu.SemaphoreType.DMA((width // DEPTH,))],
    )(matrix, w_gate)
    fetched = pltpu.with_memory_space_constraint(fetched, pltpu.VMEM)
    parts = [
        call(
            join_kernel,
            bf16(GROUPS * block, wide),
            (0, 4 * GROUPS * block * wide),
            in_specs=[vmem] * GROUPS,
            out_specs=vmem,
        )(*to_all(buckets))
    ]
    for bit in range(in_bits):
        all_rows = parts[0] if bit == 0 else jnp.concatenate(parts)
        parts.append(exchanged(all_rows, 1 << bit, 1))

    slots = 2 * AHEAD * max(DEPTH, COLUMNS) * hid * 2
    kept, away = call(
        functools.partial(expert_kernel, len(parts), topk),
        [bf16(half, width)] * 2,
        (6 * total_rows * width * hid, 4 * width * hid),
        limit=slots + total_rows * (10 * hid + 4 * wide) + (6 << 20),
        in_specs=[smem] + [vmem] * (len(parts) + 1) + [hbm, hbm],
        out_specs=[vmem] * 2,
        scratch_shapes=[
            pltpu.VMEM((total_rows, hid), jnp.float32),
            pltpu.VMEM((total_rows, hid), jnp.float32),
            pltpu.VMEM((total_rows, hid), jnp.bfloat16),
            pltpu.VMEM((AHEAD, DEPTH, hid), jnp.bfloat16),
            pltpu.SemaphoreType.DMA((AHEAD,)),
            pltpu.VMEM((AHEAD, hid, COLUMNS), jnp.bfloat16),
            pltpu.SemaphoreType.DMA((AHEAD,)),
        ],
    )(my_expert.reshape(1), *parts, fetched, w_up, w_down)

    got = exchanged(away, 1 << (in_bits - 1), 1)
    for bit in reversed(range(in_bits - 1)):
        total = kept.astype(jnp.float32) + got.astype(jnp.float32)
        quarter = total.shape[0] // 2
        kept = total[:quarter].astype(jnp.bfloat16)
        got = exchanged(total[quarter:].astype(jnp.bfloat16), 1 << bit, 1)
    results = call(
        sum_kernel,
        [bf16(block, width)] * GROUPS,
        (0, 6 * GROUPS * block * width),
        in_specs=[vmem, vmem],
        out_specs=[vmem] * GROUPS,
    )(kept, got)

    return call(
        mix_kernel,
        bf16(batches, rows, width),
        (2 * GROUPS * block * count * width, 10 * count * width),
        in_specs=[vmem] * (1 + GROUPS),
        out_specs=vmem,
    )(matrix, *to_all(results))


def solution(mesh):
    split = P(None, ("rep", "grp"), None)
    stacked = P("grp", None, None)
    return jax.shard_map(
        body,
        mesh=mesh,
        in_specs=(split, split, split, stacked, stacked, stacked),
        out_specs=split,
        check_vma=False,
    )
```

time: 105 us -> 94.2 us (0.90)
  the two profiles are of different devices: /device:TPU:0 before, /device:TPU:12 now
where the time goes in v3:
time: 94.2 us; the launch traced here: 93.9 us
  waiting for transfers between devices  36.4 us (39%)
  Pallas kernels  33.2 us (35%)
  starting transfers between devices  19.3 us (20%)
  local copies, waits for them, and re-layouts  4.05 us (4%)
    ppermute x16, waiting for transfers between devices, exchanged(): lax.ppermute(shard, 'grp', [(i, (i // unit ^ by) * unit + i % unit) for i...  36.4 us
    pallas_call x1, Pallas kernels, body(): call(functools.partial(expert_kernel, len(parts), topk), [bf16(half, widt...  21.5 us
    ppermute x16, starting transfers between devices, exchanged(): lax.ppermute(shard, 'grp', [(i, (i // unit ^ by) * unit + i % unit) for i...  19.3 us
    pallas_call x1, Pallas kernels, body(): call(fetch_kernel, pltpu.VMEM((width, hid), jnp.bfloat16), (0, 4 * width...  9.8 us
    unnamed x9, local copies, waits for them, and re-layouts  3.86 us
  transfers between devices with their start and end apart: 16, of which 11 were waited for; matrix products, arithmetic and copies ran while one was open for 0% of the time, Pallas kernels for 10%

profile of v3, /device:TPU:12, one launch (start us, length us, event | category | flops | bytes accessed | tf_op | source)
XLA Modules:
  0.0 93.9 jit_solution(17587346636773153418)
XLA Ops:
  0.0 0.7 convert_element_type.3
  0.8 0.8 copy.8
  1.7 0.9 copy-done.2
  2.7 0.7 shard_map.64
  3.4 1.5 %collective-permute-start = (bf16[8,7296]{1,0:T(8,128)(2,1)S(1)}, bf16[8,7296]{1,0:T(8,128)(2,1)S(1)}, u32[]{:S(2)}, u32[]{:S(2)}) collective-permute-start(bf16[8,7296]{1,0:T(8,128)(2,1)S(1)} %get-tuple-element.26), channel_id=1, source_target_pairs={{0,2},{1,3},{2,0},{3,1},{4,6},{5,7},{6,4},{7,5},{8,10},{9,11},{10,... | collective-permute-start | bytes 350216 | tf_op jit(solution)/shard_map/ppermute | solution.py:20
  4.9 0.4 collective-permute-start.1
  5.4 1.6 %collective-permute-start.2 = (bf16[8,7296]{1,0:T(8,128)(2,1)S(1)}, bf16[8,7296]{1,0:T(8,128)(2,1)S(1)}, u32[]{:S(2)}, u32[]{:S(2)}) collective-permute-start(bf16[8,7296]{1,0:T(8,128)(2,1)S(1)} %get-tuple-element.28), channel_id=1, source_target_pairs={{0,6},{1,7},{2,4},{3,5},{4,2},{5,3},{6,0},{7,1},{8,14},{9,15},{10,... | collective-permute-start | bytes 350216 | tf_op jit(solution)/shard_map/ppermute | solution.py:20
  6.9 2.6 %collective-permute-start.3 = (bf16[8,7296]{1,0:T(8,128)(2,1)S(1)}, bf16[8,7296]{1,0:T(8,128)(2,1)S(1)}, u32[]{:S(2)}, u32[]{:S(2)}) collective-permute-start(bf16[8,7296]{1,0:T(8,128)(2,1)S(1)} %get-tuple-element.29), channel_id=1, source_target_pairs={{0,8},{1,9},{2,10},{3,11},{4,12},{5,13},{6,14},{7,15},{8,0},{9,1},... | collective-permute-start | bytes 350216 | tf_op jit(solution)/shard_map/ppermute | solution.py:20
  9.5 1.3 %collective-permute-start.4 = (bf16[8,7296]{1,0:T(8,128)(2,1)S(1)}, bf16[8,7296]{1,0:T(8,128)(2,1)S(1)}, u32[]{:S(2)}, u32[]{:S(2)}) collective-permute-start(bf16[8,7296]{1,0:T(8,128)(2,1)S(1)} %get-tuple-element.30), channel_id=1, source_target_pairs={{0,10},{1,11},{2,8},{3,9},{4,14},{5,15},{6,12},{7,13},{8,2},{9,3},... | collective-permute-start | bytes 350216 | tf_op jit(solution)/shard_map/ppermute | solution.py:20
  10.8 1.6 %collective-permute-start.5 = (bf16[8,7296]{1,0:T(8,128)(2,1)S(1)}, bf16[8,7296]{1,0:T(8,128)(2,1)S(1)}, u32[]{:S(2)}, u32[]{:S(2)}) collective-permute-start(bf16[8,7296]{1,0:T(8,128)(2,1)S(1)} %get-tuple-element.31), channel_id=1, source_target_pairs={{0,12},{1,13},{2,14},{3,15},{4,8},{5,9},{6,10},{7,11},{8,4},{9,5},... | collective-permute-start | bytes 350216 | tf_op jit(solution)/shard_map/ppermute | solution.py:20
  12.8 1.2 %collective-permute-done.2.refs_3_ = bf16[8,7296]{1,0:T(8,128)(2,1)S(1)} collective-permute-done((bf16[8,7296]{1,0:T(8,128)(2,1)S(1)}, bf16[8,7296]{1,0:T(8,128)(2,1)S(1)}, u32[]{:S(2)}, u32[]{:S(2)}) %collective-permute-start.2) | collective-permute-done | bytes 116768 | tf_op jit(solution)/shard_map/ppermute | solution.py:20
  14.0 8.6 %collective-permute-done.3.refs_4_ = bf16[8,7296]{1,0:T(8,128)(2,1)S(1)} collective-permute-done((bf16[8,7296]{1,0:T(8,128)(2,1)S(1)}, bf16[8,7296]{1,0:T(8,128)(2,1)S(1)}, u32[]{:S(2)}, u32[]{:S(2)}) %collective-permute-start.3) | collective-permute-done | bytes 116768 | tf_op jit(solution)/shard_map/ppermute | solution.py:20
  22.7 2.5 %collective-permute-done.4.refs_5_ = bf16[8,7296]{1,0:T(8,128)(2,1)S(1)} collective-permute-done((bf16[8,7296]{1,0:T(8,128)(2,1)S(1)}, bf16[8,7296]{1,0:T(8,128)(2,1)S(1)}, u32[]{:S(2)}, u32[]{:S(2)}) %collective-permute-start.4) | collective-permute-done | bytes 116768 | tf_op jit(solution)/shard_map/ppermute | solution.py:20
  25.2 2.7 %collective-permute-done.5.refs_6_ = bf16[8,7296]{1,0:T(8,128)(2,1)S(1)} collective-permute-done((bf16[8,7296]{1,0:T(8,128)(2,1)S(1)}, bf16[8,7296]{1,0:T(8,128)(2,1)S(1)}, u32[]{:S(2)}, u32[]{:S(2)}) %collective-permute-start.5) | collective-permute-done | bytes 116768 | tf_op jit(solution)/shard_map/ppermute | solution.py:20
  27.9 2.2 %collective-permute-done.6.refs_7_ = bf16[8,7296]{1,0:T(8,128)(2,1)S(1)} collective-permute-done((bf16[8,7296]{1,0:T(8,128)(2,1)S(1)}, bf16[8,7296]{1,0:T(8,128)(2,1)S(1)}, u32[]{:S(2)}, u32[]{:S(2)}) %collective-permute-start.6) | collective-permute-done | bytes 116768 | tf_op jit(solution)/shard_map/ppermute | solution.py:20
  30.2 9.8 %shard_map.66.refs_2_ = bf16[7168,2048]{1,0:T(8,128)(2,1)S(1)} custom-call(bf16[64,16]{1,0:T(8,128)(2,1)S(1)} %get-tuple-element.24.after_ref.matrix_ref, bf16[1,7168,2048]{2,1,0:T(8,128)(2,1)} %w_ref.1), custom_call_target="tpu_custom_call" | custom-call | bytes 58720256 | tf_op jit(solution)/shard_map/pallas_call | solution.py:221
  40.1 1.0 %copy-done.3 = bf16[64,7296]{1,0:T(8,128)(2,1)} copy-done((bf16[64,7296]{1,0:T(8,128)(2,1)}, bf16[64,7296]{1,0:T(8,128)(2,1)S(1)}, u32[]{:S(2)}) %copy-start.3) | copy-done | bytes 933912
  41.0 21.5 %shard_map.67 = (bf16[64,7168]{1,0:T(8,128)(2,1)}, bf16[64,7168]{1,0:T(8,128)(2,1)}) custom-call(s32[1]{0:T(128)} %bitcast.2.expert_ref, bf16[64,7296]{1,0:T(8,128)(2,1)} %copy-done, bf16[64,7296]{1,0:T(8,128)(2,1)} %copy-done.3, bf16[7168,2048]{1,0:T(8,128)(2,1)S(1)} %shard_map.66.refs_2_, bf16[1,7168,2048]{2,1,0:T(8,128)(2,1)} %refs_3_.1, ...), custom_call_target="tpu_custom_call" | custom-call | flops 11274289152 | bytes 58720256 | tf_op jit(solution)/shard_map/pallas_call | solution.py:244
  62.8 2.4 %collective-permute-done.8.got_ref = bf16[64,7168]{1,0:T(8,128)(2,1)S(1)} collective-permute-done((bf16[64,7168]{1,0:T(8,128)(2,1)}, bf16[64,7168]{1,0:T(8,128)(2,1)S(1)}, u32[]{:S(2)}, u32[]{:S(2)}) %collective-permute-start.8) | collective-permute-done | bytes 917536 | tf_op jit(solution)/shard_map/ppermute | solution.py:20
  65.3 1.2 %copy-done.1 = bf16[64,7168]{1,0:T(8,128)(2,1)S(1)} copy-done((bf16[64,7168]{1,0:T(8,128)(2,1)S(1)}, bf16[64,7168]{1,0:T(8,128)(2,1)}, u32[]{:S(2)}) %copy-start.1) | copy-done | bytes 917528
  66.6 0.7 collective-permute-start.9
  67.3 2.9 %collective-permute-start.11 = (bf16[8,7168]{1,0:T(8,128)(2,1)S(1)}, bf16[8,7168]{1,0:T(8,128)(2,1)S(1)}, u32[]{:S(2)}, u32[]{:S(2)}) collective-permute-start(bf16[8,7168]{1,0:T(8,128)(2,1)S(1)} %get-tuple-element.38), channel_id=1, source_target_pairs={{0,6},{1,7},{2,4},{3,5},{4,2},{5,3},{6,0},{7,1},{8,14},{9,15},{10,... | collective-permute-start | bytes 344072 | tf_op jit(solution)/shard_map/ppermute | solution.py:20
  70.2 1.4 %collective-permute-start.12 = (bf16[8,7168]{1,0:T(8,128)(2,1)S(1)}, bf16[8,7168]{1,0:T(8,128)(2,1)S(1)}, u32[]{:S(2)}, u32[]{:S(2)}) collective-permute-start(bf16[8,7168]{1,0:T(8,128)(2,1)S(1)} %get-tuple-element.39), channel_id=1, source_target_pairs={{0,8},{1,9},{2,10},{3,11},{4,12},{5,13},{6,14},{7,15},{8,0},{9,1},... | collective-permute-start | bytes 344072 | tf_op jit(solution)/shard_map/ppermute | solution.py:20
  71.6 1.5 %collective-permute-start.13 = (bf16[8,7168]{1,0:T(8,128)(2,1)S(1)}, bf16[8,7168]{1,0:T(8,128)(2,1)S(1)}, u32[]{:S(2)}, u32[]{:S(2)}) collective-permute-start(bf16[8,7168]{1,0:T(8,128)(2,1)S(1)} %get-tuple-element.40), channel_id=1, source_target_pairs={{0,10},{1,11},{2,8},{3,9},{4,14},{5,15},{6,12},{7,13},{8,2},{9,3},... | collective-permute-start | bytes 344072 | tf_op jit(solution)/shard_map/ppermute | solution.py:20
  73.2 2.0 %collective-permute-start.14 = (bf16[8,7168]{1,0:T(8,128)(2,1)S(1)}, bf16[8,7168]{1,0:T(8,128)(2,1)S(1)}, u32[]{:S(2)}, u32[]{:S(2)}) collective-permute-start(bf16[8,7168]{1,0:T(8,128)(2,1)S(1)} %get-tuple-element.41), channel_id=1, source_target_pairs={{0,12},{1,13},{2,14},{3,15},{4,8},{5,9},{6,10},{7,11},{8,4},{9,5},... | collective-permute-start | bytes 344072 | tf_op jit(solution)/shard_map/ppermute | solution.py:20
  75.1 1.1 %collective-permute-start.15 = (bf16[8,7168]{1,0:T(8,128)(2,1)S(1)}, bf16[8,7168]{1,0:T(8,128)(2,1)S(1)}, u32[]{:S(2)}, u32[]{:S(2)}) collective-permute-start(bf16[8,7168]{1,0:T(8,128)(2,1)S(1)} %get-tuple-element.42), channel_id=1, source_target_pairs={{0,14},{1,15},{2,12},{3,13},{4,10},{5,11},{6,8},{7,9},{8,6},{9,7},... | collective-permute-start | bytes 344072 | tf_op jit(solution)/shard_map/ppermute | solution.py:20
  76.2 0.5 collective-permute-done.11.refs_3_
  76.7 8.4 %collective-permute-done.12.refs_4_ = bf16[8,7168]{1,0:T(8,128)(2,1)S(1)} collective-permute-done((bf16[8,7168]{1,0:T(8,128)(2,1)S(1)}, bf16[8,7168]{1,0:T(8,128)(2,1)S(1)}, u32[]{:S(2)}, u32[]{:S(2)}) %collective-permute-start.12) | collective-permute-done | bytes 114720 | tf_op jit(solution)/shard_map/ppermute | solution.py:20
  85.0 2.5 %collective-permute-done.13.refs_5_ = bf16[8,7168]{1,0:T(8,128)(2,1)S(1)} collective-permute-done((bf16[8,7168]{1,0:T(8,128)(2,1)S(1)}, bf16[8,7168]{1,0:T(8,128)(2,1)S(1)}, u32[]{:S(2)}, u32[]{:S(2)}) %collective-permute-start.13) | collective-permute-done | bytes 114720 | tf_op jit(solution)/shard_map/ppermute | solution.py:20
  87.5 3.2 %collective-permute-done.14.refs_6_ = bf16[8,7168]{1,0:T(8,128)(2,1)S(1)} collective-permute-done((bf16[8,7168]{1,0:T(8,128)(2,1)S(1)}, bf16[8,7168]{1,0:T(8,128)(2,1)S(1)}, u32[]{:S(2)}, u32[]{:S(2)}) %collective-permute-start.14) | collective-permute-done | bytes 114720 | tf_op jit(solution)/shard_map/ppermute | solution.py:20
  90.7 2.2 %collective-permute-done.15.refs_7_ = bf16[8,7168]{1,0:T(8,128)(2,1)S(1)} collective-permute-done((bf16[8,7168]{1,0:T(8,128)(2,1)S(1)}, bf16[8,7168]{1,0:T(8,128)(2,1)S(1)}, u32[]{:S(2)}, u32[]{:S(2)}) %collective-permute-start.15) | collective-permute-done | bytes 114720 | tf_op jit(solution)/shard_map/ppermute | solution.py:20
  92.9 1.0 %shard_map.69 = bf16[2,8,7168]{2,1,0:T(8,128)(2,1)} custom-call(bf16[64,16]{1,0:T(8,128)(2,1)S(1)} %get-tuple-element.24.after_ref.matrix_ref, bf16[8,7168]{1,0:T(8,128)(2,1)S(1)} %get-tuple-element.35.refs_0_, bf16[8,7168]{1,0:T(8,128)(2,1)S(1)} %collective-permute-done.9.refs_1_, bf16[8,7168]{1,0:T(8,128)(2,1)S(1)} %collective-permute-done.10.refs_2_, ...), custom_call_target="tpu_custom_call" | custom-call | flops 14680064 | bytes 1146880 | tf_op jit(solution)/shard_map/pallas_call | solution.py:276
  (20 shorter events, 1.4 us)
Async XLA Ops:
  1.7 0.9 copy-start.2
  3.4 7.4 %collective-permute-start = (bf16[8,7296]{1,0:T(8,128)(2,1)S(1)}, bf16[8,7296]{1,0:T(8,128)(2,1)S(1)}, u32[]{:S(2)}, u32[]{:S(2)}) collective-permute-start(bf16[8,7296]{1,0:T(8,128)(2,1)S(1)} %get-tuple-element.26), channel_id=1, source_target_pairs={{0,2},{1,3},{2,0},{3,1},{4,6},{5,7},{6,4},{7,5},{8,10},{9,11},{10,... | collective-permute-start | bytes 350216 | tf_op jit(solution)/shard_map/ppermute | solution.py:20
  4.9 7.4 %collective-permute-start.1 = (bf16[8,7296]{1,0:T(8,128)(2,1)S(1)}, bf16[8,7296]{1,0:T(8,128)(2,1)S(1)}, u32[]{:S(2)}, u32[]{:S(2)}) collective-permute-start(bf16[8,7296]{1,0:T(8,128)(2,1)S(1)} %get-tuple-element.27), channel_id=1, source_target_pairs={{0,4},{1,5},{2,6},{3,7},{4,0},{5,1},{6,2},{7,3},{8,12},{9,13},{10,... | collective-permute-start | bytes 350216 | tf_op jit(solution)/shard_map/ppermute | solution.py:20
  5.4 8.7 %collective-permute-start.2 = (bf16[8,7296]{1,0:T(8,128)(2,1)S(1)}, bf16[8,7296]{1,0:T(8,128)(2,1)S(1)}, u32[]{:S(2)}, u32[]{:S(2)}) collective-permute-start(bf16[8,7296]{1,0:T(8,128)(2,1)S(1)} %get-tuple-element.28), channel_id=1, source_target_pairs={{0,6},{1,7},{2,4},{3,5},{4,2},{5,3},{6,0},{7,1},{8,14},{9,15},{10,... | collective-permute-start | bytes 350216 | tf_op jit(solution)/shard_map/ppermute | solution.py:20
  6.9 15.7 %collective-permute-start.3 = (bf16[8,7296]{1,0:T(8,128)(2,1)S(1)}, bf16[8,7296]{1,0:T(8,128)(2,1)S(1)}, u32[]{:S(2)}, u32[]{:S(2)}) collective-permute-start(bf16[8,7296]{1,0:T(8,128)(2,1)S(1)} %get-tuple-element.29), channel_id=1, source_target_pairs={{0,8},{1,9},{2,10},{3,11},{4,12},{5,13},{6,14},{7,15},{8,0},{9,1},... | collective-permute-start | bytes 350216 | tf_op jit(solution)/shard_map/ppermute | solution.py:20
  9.5 15.7 %collective-permute-start.4 = (bf16[8,7296]{1,0:T(8,128)(2,1)S(1)}, bf16[8,7296]{1,0:T(8,128)(2,1)S(1)}, u32[]{:S(2)}, u32[]{:S(2)}) collective-permute-start(bf16[8,7296]{1,0:T(8,128)(2,1)S(1)} %get-tuple-element.30), channel_id=1, source_target_pairs={{0,10},{1,11},{2,8},{3,9},{4,14},{5,15},{6,12},{7,13},{8,2},{9,3},... | collective-permute-start | bytes 350216 | tf_op jit(solution)/shard_map/ppermute | solution.py:20
  10.8 17.1 %collective-permute-start.5 = (bf16[8,7296]{1,0:T(8,128)(2,1)S(1)}, bf16[8,7296]{1,0:T(8,128)(2,1)S(1)}, u32[]{:S(2)}, u32[]{:S(2)}) collective-permute-start(bf16[8,7296]{1,0:T(8,128)(2,1)S(1)} %get-tuple-element.31), channel_id=1, source_target_pairs={{0,12},{1,13},{2,14},{3,15},{4,8},{5,9},{6,10},{7,11},{8,4},{9,5},... | collective-permute-start | bytes 350216 | tf_op jit(solution)/shard_map/ppermute | solution.py:20
  12.4 17.7 %collective-permute-start.6 = (bf16[8,7296]{1,0:T(8,128)(2,1)S(1)}, bf16[8,7296]{1,0:T(8,128)(2,1)S(1)}, u32[]{:S(2)}, u32[]{:S(2)}) collective-permute-start(bf16[8,7296]{1,0:T(8,128)(2,1)S(1)} %get-tuple-element.32), channel_id=1, source_target_pairs={{0,14},{1,15},{2,12},{3,13},{4,10},{5,11},{6,8},{7,9},{8,6},{9,7},... | collective-permute-start | bytes 350216 | tf_op jit(solution)/shard_map/ppermute | solution.py:20
  30.1 9.9 %copy-start = (bf16[64,7296]{1,0:T(8,128)(2,1)}, bf16[64,7296]{1,0:T(8,128)(2,1)S(1)}, u32[]{:S(2)}) copy-start(bf16[64,7296]{1,0:T(8,128)(2,1)S(1)} %shard_map.65.refs_0_) | copy-start | bytes 2801668
  30.1 9.9 %collective-permute-start.7 = (bf16[64,7296]{1,0:T(8,128)(2,1)S(1)}, bf16[64,7296]{1,0:T(8,128)(2,1)S(1)}, u32[]{:S(2)}, u32[]{:S(2)}) collective-permute-start(bf16[64,7296]{1,0:T(8,128)(2,1)S(1)} %shard_map.65.refs_0_), channel_id=1, source_target_pairs={{0,1},{1,0},{2,3},{3,2},{4,5},{5,4},{6,7},{7,6},{8,9},{9,8},{10,11... | collective-permute-start | bytes 2801672 | tf_op jit(solution)/shard_map/ppermute | solution.py:20
  40.0 1.0 %copy-start.3 = (bf16[64,7296]{1,0:T(8,128)(2,1)}, bf16[64,7296]{1,0:T(8,128)(2,1)S(1)}, u32[]{:S(2)}) copy-start(bf16[64,7296]{1,0:T(8,128)(2,1)S(1)} %collective-permute-done.7.refs_1_) | copy-start | bytes 2801668
  62.5 2.7 %collective-permute-start.8 = (bf16[64,7168]{1,0:T(8,128)(2,1)}, bf16[64,7168]{1,0:T(8,128)(2,1)S(1)}, u32[]{:S(2)}, u32[]{:S(2)}) collective-permute-start(bf16[64,7168]{1,0:T(8,128)(2,1)} %get-tuple-element.34), channel_id=1, source_target_pairs={{0,1},{1,0},{2,3},{3,2},{4,5},{5,4},{6,7},{7,6},{8,9},{9,8},{10,11... | collective-permute-start | bytes 2752520 | tf_op jit(solution)/shard_map/ppermute | solution.py:20
  65.3 1.2 %copy-start.1 = (bf16[64,7168]{1,0:T(8,128)(2,1)S(1)}, bf16[64,7168]{1,0:T(8,128)(2,1)}, u32[]{:S(2)}) copy-start(bf16[64,7168]{1,0:T(8,128)(2,1)} %get-tuple-element.33.kept_ref) | copy-start | bytes 2752516
  66.6 6.5 %collective-permute-start.9 = (bf16[8,7168]{1,0:T(8,128)(2,1)S(1)}, bf16[8,7168]{1,0:T(8,128)(2,1)S(1)}, u32[]{:S(2)}, u32[]{:S(2)}) collective-permute-start(bf16[8,7168]{1,0:T(8,128)(2,1)S(1)} %get-tuple-element.36), channel_id=1, source_target_pairs={{0,2},{1,3},{2,0},{3,1},{4,6},{5,7},{6,4},{7,5},{8,10},{9,11},{10,... | collective-permute-start | bytes 344072 | tf_op jit(solution)/shard_map/ppermute | solution.py:20
  67.3 7.8 %collective-permute-start.10 = (bf16[8,7168]{1,0:T(8,128)(2,1)S(1)}, bf16[8,7168]{1,0:T(8,128)(2,1)S(1)}, u32[]{:S(2)}, u32[]{:S(2)}) collective-permute-start(bf16[8,7168]{1,0:T(8,128)(2,1)S(1)} %get-tuple-element.37), channel_id=1, source_target_pairs={{0,4},{1,5},{2,6},{3,7},{4,0},{5,1},{6,2},{7,3},{8,12},{9,13},{10,... | collective-permute-start | bytes 344072 | tf_op jit(solution)/shard_map/ppermute | solution.py:20
  67.3 9.3 %collective-permute-start.11 = (bf16[8,7168]{1,0:T(8,128)(2,1)S(1)}, bf16[8,7168]{1,0:T(8,128)(2,1)S(1)}, u32[]{:S(2)}, u32[]{:S(2)}) collective-permute-start(bf16[8,7168]{1,0:T(8,128)(2,1)S(1)} %get-tuple-element.38), channel_id=1, source_target_pairs={{0,6},{1,7},{2,4},{3,5},{4,2},{5,3},{6,0},{7,1},{8,14},{9,15},{10,... | collective-permute-start | bytes 344072 | tf_op jit(solution)/shard_map/ppermute | solution.py:20
  70.2 14.8 %collective-permute-start.12 = (bf16[8,7168]{1,0:T(8,128)(2,1)S(1)}, bf16[8,7168]{1,0:T(8,128)(2,1)S(1)}, u32[]{:S(2)}, u32[]{:S(2)}) collective-permute-start(bf16[8,7168]{1,0:T(8,128)(2,1)S(1)} %get-tuple-element.39), channel_id=1, source_target_pairs={{0,8},{1,9},{2,10},{3,11},{4,12},{5,13},{6,14},{7,15},{8,0},{9,1},... | collective-permute-start | bytes 344072 | tf_op jit(solution)/shard_map/ppermute | solution.py:20
  71.6 15.9 %collective-permute-start.13 = (bf16[8,7168]{1,0:T(8,128)(2,1)S(1)}, bf16[8,7168]{1,0:T(8,128)(2,1)S(1)}, u32[]{:S(2)}, u32[]{:S(2)}) collective-permute-start(bf16[8,7168]{1,0:T(8,128)(2,1)S(1)} %get-tuple-element.40), channel_id=1, source_target_pairs={{0,10},{1,11},{2,8},{3,9},{4,14},{5,15},{6,12},{7,13},{8,2},{9,3},... | collective-permute-start | bytes 344072 | tf_op jit(solution)/shard_map/ppermute | solution.py:20
  73.2 17.6 %collective-permute-start.14 = (bf16[8,7168]{1,0:T(8,128)(2,1)S(1)}, bf16[8,7168]{1,0:T(8,128)(2,1)S(1)}, u32[]{:S(2)}, u32[]{:S(2)}) collective-permute-start(bf16[8,7168]{1,0:T(8,128)(2,1)S(1)} %get-tuple-element.41), channel_id=1, source_target_pairs={{0,12},{1,13},{2,14},{3,15},{4,8},{5,9},{6,10},{7,11},{8,4},{9,5},... | collective-permute-start | bytes 344072 | tf_op jit(solution)/shard_map/ppermute | solution.py:20
  75.1 17.8 %collective-permute-start.15 = (bf16[8,7168]{1,0:T(8,128)(2,1)S(1)}, bf16[8,7168]{1,0:T(8,128)(2,1)S(1)}, u32[]{:S(2)}, u32[]{:S(2)}) collective-permute-start(bf16[8,7168]{1,0:T(8,128)(2,1)S(1)} %get-tuple-element.42), channel_id=1, source_target_pairs={{0,14},{1,15},{2,12},{3,13},{4,10},{5,11},{6,8},{7,9},{8,6},{9,7},... | collective-permute-start | bytes 344072 | tf_op jit(solution)/shard_map/ppermute | solution.py:20

commit v4 on v3

--- a/solution.py
+++ b/solution.py
@@ -13,6 +13,9 @@
 DEPTH = 512
 COLUMNS = 512
 AHEAD = 4
+SMALL = 8 << 20
+SLACK = 1 << 20
+FETCHED = 3
 
 
 def exchanged(shard, by, unit):
@@ -22,7 +25,7 @@
     )
 
 
-def call(kernel, out_shape, cost, limit=16 << 20, **kwargs):
+def call(kernel, out_shape, cost, limit=SMALL, **kwargs):
     flops, moved = cost
     return pl.pallas_call(
         kernel,
@@ -102,17 +105,21 @@
 
 def expert_kernel(parts, topk, expert_ref, *refs):
     xs, refs = refs[:parts], refs[parts:]
-    w_gate_ref, w_up_ref, w_down_ref, kept_ref, away_ref = refs[:5]
-    gate_acc, up_acc, hidden, up_slots, up_sem, down_slots, down_sem = refs[5:]
+    w_gate_ref, w_rest_ref, w_up_ref, w_down_ref, kept_ref, away_ref = refs[:6]
+    gate_acc, up_acc, hidden, up_slots, up_sem, down_slots, down_sem = refs[6:]
     half, width = kept_ref.shape
     ups, downs = width // DEPTH, width // COLUMNS
+    held = w_gate_ref.shape[0] // DEPTH
+    here = [slice(i * DEPTH, (i + 1) * DEPTH) for i in range(ups)]
+    sources = []
+    for i in range(ups):
+        if i >= held:
+            sources.append(w_rest_ref.at[0, here[i]])
+        sources.append(w_up_ref.at[0, here[i]])
+    count = len(sources)
     copies = [
-        pltpu.make_async_copy(
-            w_up_ref.at[0, i * DEPTH : (i + 1) * DEPTH],
-            up_slots.at[i % AHEAD],
-            up_sem.at[i % AHEAD],
-        )
-        for i in range(ups)
+        pltpu.make_async_copy(source, up_slots.at[n % AHEAD], up_sem.at[n % AHEAD])
+        for n, source in enumerate(sources)
     ] + [
         pltpu.make_async_copy(
             w_down_ref.at[0, :, j * COLUMNS : (j + 1) * COLUMNS],
@@ -124,21 +131,23 @@
     for copy in copies[:AHEAD]:
         copy.start()
 
+    def add(acc, i, x, w):
+        product = jnp.dot(x, w, preferred_element_type=jnp.float32)
+        if i == 0:
+            acc[...] = product
+        else:
+            acc[...] += product
+
+    n = 0
     for i in range(ups):
-        here = slice(i * DEPTH, (i + 1) * DEPTH)
-        x = jnp.concatenate([r[:, here] for r in xs], axis=0)
-        gate = jnp.dot(x, w_gate_ref[here], preferred_element_type=jnp.float32)
-        if i == 0:
-            gate_acc[...] = gate
-        else:
-            gate_acc[...] += gate
-        copies[i].wait()
-        up = jnp.dot(x, up_slots[i % AHEAD], preferred_element_type=jnp.float32)
-        if i == 0:
-            up_acc[...] = up
-        else:
-            up_acc[...] += up
-        copies[i + AHEAD].start()
+        x = jnp.concatenate([r[:, here[i]] for r in xs], axis=0)
+        if i < held:
+            add(gate_acc, i, x, w_gate_ref[here[i]])
+        for acc in [up_acc] if i < held else [gate_acc, up_acc]:
+            copies[n].wait()
+            add(acc, i, x, up_slots[n % AHEAD])
+            copies[n + AHEAD].start()
+            n += 1
 
     extra = jnp.concatenate([r[:, width:].astype(jnp.float32) for r in xs], axis=0)
     expert = expert_ref[0].astype(jnp.float32)
@@ -150,13 +159,13 @@
     hidden[...] = (jax.nn.silu(gate_acc[...]) * up_acc[...] * column).astype(jnp.bfloat16)
 
     for j in range(downs):
-        copies[ups + j].wait()
+        copies[count + j].wait()
         total = jnp.dot(hidden[...], down_slots[j % AHEAD], preferred_element_type=jnp.float32)
-        here = slice(j * COLUMNS, (j + 1) * COLUMNS)
-        kept_ref[:, here] = total[:half].astype(jnp.bfloat16)
-        away_ref[:, here] = total[half:].astype(jnp.bfloat16)
+        at = slice(j * COLUMNS, (j + 1) * COLUMNS)
+        kept_ref[:, at] = total[:half].astype(jnp.bfloat16)
+        away_ref[:, at] = total[half:].astype(jnp.bfloat16)
         if j + AHEAD < downs:
-            copies[ups + j + AHEAD].start()
+            copies[count + j + AHEAD].start()
 
 
 def sum_kernel(kept_ref, got_ref, *out_refs):
@@ -218,13 +227,16 @@
         in_specs=[smem, vmem, vmem],
         out_specs=[vmem] * (1 + GROUPS),
     )(group_me.reshape(1), tokens, extra)
+    w_gate, w_up, w_down = (
+        pltpu.with_memory_space_constraint(w, pltpu.HBM) for w in (w_gate, w_up, w_down)
+    )
     fetched = call(
         fetch_kernel,
-        pltpu.VMEM((width, hid), jnp.bfloat16),
-        (0, 4 * width * hid),
+        pltpu.VMEM((FETCHED * DEPTH, hid), jnp.bfloat16),
+        (0, 4 * FETCHED * DEPTH * hid),
         in_specs=[hbm, hbm],
         out_specs=vmem,
-        scratch_shapes=[pltpu.SemaphoreType.DMA((width // DEPTH,))],
+        scratch_shapes=[pltpu.SemaphoreType.DMA((FETCHED,))],
     )(matrix, w_gate)
     fetched = pltpu.with_memory_space_constraint(fetched, pltpu.VMEM)
     parts = [
@@ -245,8 +257,8 @@
         functools.partial(expert_kernel, len(parts), topk),
         [bf16(half, width)] * 2,
         (6 * total_rows * width * hid, 4 * width * hid),
-        limit=slots + total_rows * (10 * hid + 4 * wide) + (6 << 20),
-        in_specs=[smem] + [vmem] * (len(parts) + 1) + [hbm, hbm],
+        limit=slots + total_rows * (10 * hid + 4 * wide) + SLACK,
+        in_specs=[smem] + [vmem] * (len(parts) + 1) + [hbm] * 3,
         out_specs=[vmem] * 2,
         scratch_shapes=[
             pltpu.VMEM((total_rows, hid), jnp.float32),
@@ -257,7 +269,7 @@
             pltpu.VMEM((AHEAD, hid, COLUMNS), jnp.bfloat16),
             pltpu.SemaphoreType.DMA((AHEAD,)),
         ],
-    )(my_expert.reshape(1), *parts, fetched, w_up, w_down)
+    )(my_expert.reshape(1), *parts, fetched, w_gate, w_up, w_down)
 
     got = exchanged(away, 1 << (in_bits - 1), 1)
     for bit in reversed(range(in_bits - 1)):

time: 94.2 us -> 88.8 us (0.943)
  Pallas kernels: 33.2 us -> 30.1 us
  local copies, waits for them, and re-layouts: 4.05 us -> 1.9 us
    pallas_call x1, Pallas kernels: 9.8 us -> 2.89 us  [body(): call(fetch_kernel, pltpu.VMEM((FETCHED * DEPTH, hid), jnp.bfloat16), (0,...]
    pallas_call x1, Pallas kernels: 21.5 us -> 25.3 us  [body(): call(functools.partial(expert_kernel, len(parts), topk), [bf16(half, widt...]
    unnamed x9 -> x3, local copies, waits for them, and re-layouts: 3.86 us -> 1.71 us
  transfers between devices with their start and end apart: 16 -> 16, of which waited for: 11 -> 11; matrix products, arithmetic and copies ran while one was open for 0% -> 0% of each run, Pallas kernels for 10% -> 3%
where the time goes in v4:
time: 88.8 us; the launch traced here: 88.7 us
  waiting for transfers between devices  36.2 us (41%)
  Pallas kernels  30.1 us (34%)
  starting transfers between devices  19.5 us (22%)
  local copies, waits for them, and re-layouts  1.9 us (2%)
    ppermute x16, waiting for transfers between devices, exchanged(): lax.ppermute(shard, 'grp', [(i, (i // unit ^ by) * unit + i % unit) for i...  36.2 us
    pallas_call x1, Pallas kernels, body(): call(functools.partial(expert_kernel, len(parts), topk), [bf16(half, widt...  25.3 us
    ppermute x16, starting transfers between devices, exchanged(): lax.ppermute(shard, 'grp', [(i, (i // unit ^ by) * unit + i % unit) for i...  19.5 us
    pallas_call x1, Pallas kernels, body(): call(fetch_kernel, pltpu.VMEM((FETCHED * DEPTH, hid), jnp.bfloat16), (0,...  2.89 us
  transfers between devices with their start and end apart: 16, of which 11 were waited for; matrix products, arithmetic and copies ran while one was open for 0% of the time, Pallas kernels for 3%

profile of v4, /device:TPU:12, one launch (start us, length us, event | category | flops | bytes accessed | tf_op | source)
XLA Modules:
  0.0 88.7 jit_solution(17527723753574896515)
XLA Ops:
  0.0 0.7 convert_element_type.3
  0.8 0.8 copy.8
  1.7 0.9 %copy-done = bf16[2,8,7168]{2,1,0:T(8,128)(2,1)S(1)} copy-done((bf16[2,8,7168]{2,1,0:T(8,128)(2,1)S(1)}, bf16[2,8,7168]{2,1,0:T(8,128)(2,1)}, u32[]{:S(2)}) %copy-start) | copy-done | bytes 229400
  2.7 0.7 shard_map.64
  3.4 1.5 %collective-permute-start = (bf16[8,7296]{1,0:T(8,128)(2,1)S(1)}, bf16[8,7296]{1,0:T(8,128)(2,1)S(1)}, u32[]{:S(2)}, u32[]{:S(2)}) collective-permute-start(bf16[8,7296]{1,0:T(8,128)(2,1)S(1)} %get-tuple-element.26), channel_id=1, source_target_pairs={{0,2},{1,3},{2,0},{3,1},{4,6},{5,7},{6,4},{7,5},{8,10},{9,11},{10,... | collective-permute-start | bytes 350216 | tf_op jit(solution)/shard_map/ppermute | solution.py:23
  4.9 0.4 collective-permute-start.1
  5.4 1.6 %collective-permute-start.2 = (bf16[8,7296]{1,0:T(8,128)(2,1)S(1)}, bf16[8,7296]{1,0:T(8,128)(2,1)S(1)}, u32[]{:S(2)}, u32[]{:S(2)}) collective-permute-start(bf16[8,7296]{1,0:T(8,128)(2,1)S(1)} %get-tuple-element.28), channel_id=1, source_target_pairs={{0,6},{1,7},{2,4},{3,5},{4,2},{5,3},{6,0},{7,1},{8,14},{9,15},{10,... | collective-permute-start | bytes 350216 | tf_op jit(solution)/shard_map/ppermute | solution.py:23
  6.9 2.6 %collective-permute-start.3 = (bf16[8,7296]{1,0:T(8,128)(2,1)S(1)}, bf16[8,7296]{1,0:T(8,128)(2,1)S(1)}, u32[]{:S(2)}, u32[]{:S(2)}) collective-permute-start(bf16[8,7296]{1,0:T(8,128)(2,1)S(1)} %get-tuple-element.29), channel_id=1, source_target_pairs={{0,8},{1,9},{2,10},{3,11},{4,12},{5,13},{6,14},{7,15},{8,0},{9,1},... | collective-permute-start | bytes 350216 | tf_op jit(solution)/shard_map/ppermute | solution.py:23
  9.5 1.3 %collective-permute-start.4 = (bf16[8,7296]{1,0:T(8,128)(2,1)S(1)}, bf16[8,7296]{1,0:T(8,128)(2,1)S(1)}, u32[]{:S(2)}, u32[]{:S(2)}) collective-permute-start(bf16[8,7296]{1,0:T(8,128)(2,1)S(1)} %get-tuple-element.30), channel_id=1, source_target_pairs={{0,10},{1,11},{2,8},{3,9},{4,14},{5,15},{6,12},{7,13},{8,2},{9,3},... | collective-permute-start | bytes 350216 | tf_op jit(solution)/shard_map/ppermute | solution.py:23
  10.8 1.6 %collective-permute-start.5 = (bf16[8,7296]{1,0:T(8,128)(2,1)S(1)}, bf16[8,7296]{1,0:T(8,128)(2,1)S(1)}, u32[]{:S(2)}, u32[]{:S(2)}) collective-permute-start(bf16[8,7296]{1,0:T(8,128)(2,1)S(1)} %get-tuple-element.31), channel_id=1, source_target_pairs={{0,12},{1,13},{2,14},{3,15},{4,8},{5,9},{6,10},{7,11},{8,4},{9,5},... | collective-permute-start | bytes 350216 | tf_op jit(solution)/shard_map/ppermute | solution.py:23
  12.4 0.4 collective-permute-start.6
  12.8 1.2 %collective-permute-done.2.refs_3_ = bf16[8,7296]{1,0:T(8,128)(2,1)S(1)} collective-permute-done((bf16[8,7296]{1,0:T(8,128)(2,1)S(1)}, bf16[8,7296]{1,0:T(8,128)(2,1)S(1)}, u32[]{:S(2)}, u32[]{:S(2)}) %collective-permute-start.2) | collective-permute-done | bytes 116768 | tf_op jit(solution)/shard_map/ppermute | solution.py:23
  14.0 8.6 %collective-permute-done.3.refs_4_ = bf16[8,7296]{1,0:T(8,128)(2,1)S(1)} collective-permute-done((bf16[8,7296]{1,0:T(8,128)(2,1)S(1)}, bf16[8,7296]{1,0:T(8,128)(2,1)S(1)}, u32[]{:S(2)}, u32[]{:S(2)}) %collective-permute-start.3) | collective-permute-done | bytes 116768 | tf_op jit(solution)/shard_map/ppermute | solution.py:23
  22.7 2.5 %collective-permute-done.4.refs_5_ = bf16[8,7296]{1,0:T(8,128)(2,1)S(1)} collective-permute-done((bf16[8,7296]{1,0:T(8,128)(2,1)S(1)}, bf16[8,7296]{1,0:T(8,128)(2,1)S(1)}, u32[]{:S(2)}, u32[]{:S(2)}) %collective-permute-start.4) | collective-permute-done | bytes 116768 | tf_op jit(solution)/shard_map/ppermute | solution.py:23
  25.2 2.7 %collective-permute-done.5.refs_6_ = bf16[8,7296]{1,0:T(8,128)(2,1)S(1)} collective-permute-done((bf16[8,7296]{1,0:T(8,128)(2,1)S(1)}, bf16[8,7296]{1,0:T(8,128)(2,1)S(1)}, u32[]{:S(2)}, u32[]{:S(2)}) %collective-permute-start.5) | collective-permute-done | bytes 116768 | tf_op jit(solution)/shard_map/ppermute | solution.py:23
  27.9 2.2 %collective-permute-done.6.refs_7_ = bf16[8,7296]{1,0:T(8,128)(2,1)S(1)} collective-permute-done((bf16[8,7296]{1,0:T(8,128)(2,1)S(1)}, bf16[8,7296]{1,0:T(8,128)(2,1)S(1)}, u32[]{:S(2)}, u32[]{:S(2)}) %collective-permute-start.6) | collective-permute-done | bytes 116768 | tf_op jit(solution)/shard_map/ppermute | solution.py:23
  30.2 2.9 %shard_map.66.refs_2_ = bf16[1536,2048]{1,0:T(8,128)(2,1)S(1)} custom-call(bf16[64,16]{1,0:T(8,128)(2,1)S(1)} %get-tuple-element.24.after_ref.matrix_ref, bf16[1,7168,2048]{2,1,0:T(8,128)(2,1)} %refs_3_.1), custom_call_target="tpu_custom_call" | custom-call | bytes 12582912 | tf_op jit(solution)/shard_map/pallas_call | solution.py:233
  33.1 25.3 %shard_map.67 = (bf16[64,7168]{1,0:T(8,128)(2,1)S(1)}, bf16[64,7168]{1,0:T(8,128)(2,1)S(1)}) custom-call(s32[1]{0:T(128)} %bitcast.2.expert_ref, bf16[64,7296]{1,0:T(8,128)(2,1)S(1)} %shard_map.65.refs_0_, bf16[64,7296]{1,0:T(8,128)(2,1)S(1)} %collective-permute-done.7.refs_1_, bf16[1536,2048]{1,0:T(8,128)(2,1)S(1)} %shard_map.66.refs_2_, ...), custom_call_target="tpu_custom_call" | custom-call | flops 11274289152 | bytes 58720256 | tf_op jit(solution)/shard_map/pallas_call | solution.py:256
  58.4 0.5 collective-permute-start.8
  59.0 2.1 %collective-permute-done.8.got_ref = bf16[64,7168]{1,0:T(8,128)(2,1)S(1)} collective-permute-done((bf16[64,7168]{1,0:T(8,128)(2,1)S(1)}, bf16[64,7168]{1,0:T(8,128)(2,1)S(1)}, u32[]{:S(2)}, u32[]{:S(2)}) %collective-permute-start.8) | collective-permute-done | bytes 917536 | tf_op jit(solution)/shard_map/ppermute | solution.py:23
  61.3 0.7 collective-permute-start.9
  62.0 2.9 %collective-permute-start.11 = (bf16[8,7168]{1,0:T(8,128)(2,1)S(1)}, bf16[8,7168]{1,0:T(8,128)(2,1)S(1)}, u32[]{:S(2)}, u32[]{:S(2)}) collective-permute-start(bf16[8,7168]{1,0:T(8,128)(2,1)S(1)} %get-tuple-element.38), channel_id=1, source_target_pairs={{0,6},{1,7},{2,4},{3,5},{4,2},{5,3},{6,0},{7,1},{8,14},{9,15},{10,... | collective-permute-start | bytes 344072 | tf_op jit(solution)/shard_map/ppermute | solution.py:23
  64.9 1.4 %collective-permute-start.12 = (bf16[8,7168]{1,0:T(8,128)(2,1)S(1)}, bf16[8,7168]{1,0:T(8,128)(2,1)S(1)}, u32[]{:S(2)}, u32[]{:S(2)}) collective-permute-start(bf16[8,7168]{1,0:T(8,128)(2,1)S(1)} %get-tuple-element.39), channel_id=1, source_target_pairs={{0,8},{1,9},{2,10},{3,11},{4,12},{5,13},{6,14},{7,15},{8,0},{9,1},... | collective-permute-start | bytes 344072 | tf_op jit(solution)/shard_map/ppermute | solution.py:23
  66.3 1.5 %collective-permute-start.13 = (bf16[8,7168]{1,0:T(8,128)(2,1)S(1)}, bf16[8,7168]{1,0:T(8,128)(2,1)S(1)}, u32[]{:S(2)}, u32[]{:S(2)}) collective-permute-start(bf16[8,7168]{1,0:T(8,128)(2,1)S(1)} %get-tuple-element.40), channel_id=1, source_target_pairs={{0,10},{1,11},{2,8},{3,9},{4,14},{5,15},{6,12},{7,13},{8,2},{9,3},... | collective-permute-start | bytes 344072 | tf_op jit(solution)/shard_map/ppermute | solution.py:23
  67.8 2.0 %collective-permute-start.14 = (bf16[8,7168]{1,0:T(8,128)(2,1)S(1)}, bf16[8,7168]{1,0:T(8,128)(2,1)S(1)}, u32[]{:S(2)}, u32[]{:S(2)}) collective-permute-start(bf16[8,7168]{1,0:T(8,128)(2,1)S(1)} %get-tuple-element.41), channel_id=1, source_target_pairs={{0,12},{1,13},{2,14},{3,15},{4,8},{5,9},{6,10},{7,11},{8,4},{9,5},... | collective-permute-start | bytes 344072 | tf_op jit(solution)/shard_map/ppermute | solution.py:23
  69.8 1.0 %collective-permute-start.15 = (bf16[8,7168]{1,0:T(8,128)(2,1)S(1)}, bf16[8,7168]{1,0:T(8,128)(2,1)S(1)}, u32[]{:S(2)}, u32[]{:S(2)}) collective-permute-start(bf16[8,7168]{1,0:T(8,128)(2,1)S(1)} %get-tuple-element.42), channel_id=1, source_target_pairs={{0,14},{1,15},{2,12},{3,13},{4,10},{5,11},{6,8},{7,9},{8,6},{9,7},... | collective-permute-start | bytes 344072 | tf_op jit(solution)/shard_map/ppermute | solution.py:23
  70.8 0.5 collective-permute-done.11.refs_3_
  71.3 8.4 %collective-permute-done.12.refs_4_ = bf16[8,7168]{1,0:T(8,128)(2,1)S(1)} collective-permute-done((bf16[8,7168]{1,0:T(8,128)(2,1)S(1)}, bf16[8,7168]{1,0:T(8,128)(2,1)S(1)}, u32[]{:S(2)}, u32[]{:S(2)}) %collective-permute-start.12) | collective-permute-done | bytes 114720 | tf_op jit(solution)/shard_map/ppermute | solution.py:23
  79.7 2.5 %collective-permute-done.13.refs_5_ = bf16[8,7168]{1,0:T(8,128)(2,1)S(1)} collective-permute-done((bf16[8,7168]{1,0:T(8,128)(2,1)S(1)}, bf16[8,7168]{1,0:T(8,128)(2,1)S(1)}, u32[]{:S(2)}, u32[]{:S(2)}) %collective-permute-start.13) | collective-permute-done | bytes 114720 | tf_op jit(solution)/shard_map/ppermute | solution.py:23
  82.1 3.4 %collective-permute-done.14.refs_6_ = bf16[8,7168]{1,0:T(8,128)(2,1)S(1)} collective-permute-done((bf16[8,7168]{1,0:T(8,128)(2,1)S(1)}, bf16[8,7168]{1,0:T(8,128)(2,1)S(1)}, u32[]{:S(2)}, u32[]{:S(2)}) %collective-permute-start.14) | collective-permute-done | bytes 114720 | tf_op jit(solution)/shard_map/ppermute | solution.py:23
  85.5 2.2 %collective-permute-done.15.refs_7_ = bf16[8,7168]{1,0:T(8,128)(2,1)S(1)} collective-permute-done((bf16[8,7168]{1,0:T(8,128)(2,1)S(1)}, bf16[8,7168]{1,0:T(8,128)(2,1)S(1)}, u32[]{:S(2)}, u32[]{:S(2)}) %collective-permute-start.15) | collective-permute-done | bytes 114720 | tf_op jit(solution)/shard_map/ppermute | solution.py:23
  87.7 1.0 %shard_map.69 = bf16[2,8,7168]{2,1,0:T(8,128)(2,1)} custom-call(bf16[64,16]{1,0:T(8,128)(2,1)S(1)} %get-tuple-element.24.after_ref.matrix_ref, bf16[8,7168]{1,0:T(8,128)(2,1)S(1)} %get-tuple-element.35.refs_0_, bf16[8,7168]{1,0:T(8,128)(2,1)S(1)} %collective-permute-done.9.refs_1_, bf16[8,7168]{1,0:T(8,128)(2,1)S(1)} %collective-permute-done.10.refs_2_, ...), custom_call_target="tpu_custom_call" | custom-call | flops 14680064 | bytes 1146880 | tf_op jit(solution)/shard_map/pallas_call | solution.py:288
  (14 shorter events, 0.6 us)
Async XLA Ops:
  1.7 0.9 %copy-start = (bf16[2,8,7168]{2,1,0:T(8,128)(2,1)S(1)}, bf16[2,8,7168]{2,1,0:T(8,128)(2,1)}, u32[]{:S(2)}) copy-start(bf16[2,8,7168]{2,1,0:T(8,128)(2,1)} %tokens_ref.1) | copy-start | bytes 688132
  3.4 7.4 %collective-permute-start = (bf16[8,7296]{1,0:T(8,128)(2,1)S(1)}, bf16[8,7296]{1,0:T(8,128)(2,1)S(1)}, u32[]{:S(2)}, u32[]{:S(2)}) collective-permute-start(bf16[8,7296]{1,0:T(8,128)(2,1)S(1)} %get-tuple-element.26), channel_id=1, source_target_pairs={{0,2},{1,3},{2,0},{3,1},{4,6},{5,7},{6,4},{7,5},{8,10},{9,11},{10,... | collective-permute-start | bytes 350216 | tf_op jit(solution)/shard_map/ppermute | solution.py:23
  4.9 7.4 %collective-permute-start.1 = (bf16[8,7296]{1,0:T(8,128)(2,1)S(1)}, bf16[8,7296]{1,0:T(8,128)(2,1)S(1)}, u32[]{:S(2)}, u32[]{:S(2)}) collective-permute-start(bf16[8,7296]{1,0:T(8,128)(2,1)S(1)} %get-tuple-element.27), channel_id=1, source_target_pairs={{0,4},{1,5},{2,6},{3,7},{4,0},{5,1},{6,2},{7,3},{8,12},{9,13},{10,... | collective-permute-start | bytes 350216 | tf_op jit(solution)/shard_map/ppermute | solution.py:23
  5.4 8.7 %collective-permute-start.2 = (bf16[8,7296]{1,0:T(8,128)(2,1)S(1)}, bf16[8,7296]{1,0:T(8,128)(2,1)S(1)}, u32[]{:S(2)}, u32[]{:S(2)}) collective-permute-start(bf16[8,7296]{1,0:T(8,128)(2,1)S(1)} %get-tuple-element.28), channel_id=1, source_target_pairs={{0,6},{1,7},{2,4},{3,5},{4,2},{5,3},{6,0},{7,1},{8,14},{9,15},{10,... | collective-permute-start | bytes 350216 | tf_op jit(solution)/shard_map/ppermute | solution.py:23
  6.9 15.7 %collective-permute-start.3 = (bf16[8,7296]{1,0:T(8,128)(2,1)S(1)}, bf16[8,7296]{1,0:T(8,128)(2,1)S(1)}, u32[]{:S(2)}, u32[]{:S(2)}) collective-permute-start(bf16[8,7296]{1,0:T(8,128)(2,1)S(1)} %get-tuple-element.29), channel_id=1, source_target_pairs={{0,8},{1,9},{2,10},{3,11},{4,12},{5,13},{6,14},{7,15},{8,0},{9,1},... | collective-permute-start | bytes 350216 | tf_op jit(solution)/shard_map/ppermute | solution.py:23
  9.5 15.7 %collective-permute-start.4 = (bf16[8,7296]{1,0:T(8,128)(2,1)S(1)}, bf16[8,7296]{1,0:T(8,128)(2,1)S(1)}, u32[]{:S(2)}, u32[]{:S(2)}) collective-permute-start(bf16[8,7296]{1,0:T(8,128)(2,1)S(1)} %get-tuple-element.30), channel_id=1, source_target_pairs={{0,10},{1,11},{2,8},{3,9},{4,14},{5,15},{6,12},{7,13},{8,2},{9,3},... | collective-permute-start | bytes 350216 | tf_op jit(solution)/shard_map/ppermute | solution.py:23
  10.8 17.1 %collective-permute-start.5 = (bf16[8,7296]{1,0:T(8,128)(2,1)S(1)}, bf16[8,7296]{1,0:T(8,128)(2,1)S(1)}, u32[]{:S(2)}, u32[]{:S(2)}) collective-permute-start(bf16[8,7296]{1,0:T(8,128)(2,1)S(1)} %get-tuple-element.31), channel_id=1, source_target_pairs={{0,12},{1,13},{2,14},{3,15},{4,8},{5,9},{6,10},{7,11},{8,4},{9,5},... | collective-permute-start | bytes 350216 | tf_op jit(solution)/shard_map/ppermute | solution.py:23
  12.4 17.7 %collective-permute-start.6 = (bf16[8,7296]{1,0:T(8,128)(2,1)S(1)}, bf16[8,7296]{1,0:T(8,128)(2,1)S(1)}, u32[]{:S(2)}, u32[]{:S(2)}) collective-permute-start(bf16[8,7296]{1,0:T(8,128)(2,1)S(1)} %get-tuple-element.32), channel_id=1, source_target_pairs={{0,14},{1,15},{2,12},{3,13},{4,10},{5,11},{6,8},{7,9},{8,6},{9,7},... | collective-permute-start | bytes 350216 | tf_op jit(solution)/shard_map/ppermute | solution.py:23
  30.1 3.0 %collective-permute-start.7 = (bf16[64,7296]{1,0:T(8,128)(2,1)S(1)}, bf16[64,7296]{1,0:T(8,128)(2,1)S(1)}, u32[]{:S(2)}, u32[]{:S(2)}) collective-permute-start(bf16[64,7296]{1,0:T(8,128)(2,1)S(1)} %shard_map.65.refs_0_), channel_id=1, source_target_pairs={{0,1},{1,0},{2,3},{3,2},{4,5},{5,4},{6,7},{7,6},{8,9},{9,8},{10,11... | collective-permute-start | bytes 2801672 | tf_op jit(solution)/shard_map/ppermute | solution.py:23
  58.4 2.6 %collective-permute-start.8 = (bf16[64,7168]{1,0:T(8,128)(2,1)S(1)}, bf16[64,7168]{1,0:T(8,128)(2,1)S(1)}, u32[]{:S(2)}, u32[]{:S(2)}) collective-permute-start(bf16[64,7168]{1,0:T(8,128)(2,1)S(1)} %get-tuple-element.34), channel_id=1, source_target_pairs={{0,1},{1,0},{2,3},{3,2},{4,5},{5,4},{6,7},{7,6},{8,9},{9,8},{10,11... | collective-permute-start | bytes 2752520 | tf_op jit(solution)/shard_map/ppermute | solution.py:23
  61.3 6.5 %collective-permute-start.9 = (bf16[8,7168]{1,0:T(8,128)(2,1)S(1)}, bf16[8,7168]{1,0:T(8,128)(2,1)S(1)}, u32[]{:S(2)}, u32[]{:S(2)}) collective-permute-start(bf16[8,7168]{1,0:T(8,128)(2,1)S(1)} %get-tuple-element.36), channel_id=1, source_target_pairs={{0,2},{1,3},{2,0},{3,1},{4,6},{5,7},{6,4},{7,5},{8,10},{9,11},{10,... | collective-permute-start | bytes 344072 | tf_op jit(solution)/shard_map/ppermute | solution.py:23
  62.0 7.8 %collective-permute-start.10 = (bf16[8,7168]{1,0:T(8,128)(2,1)S(1)}, bf16[8,7168]{1,0:T(8,128)(2,1)S(1)}, u32[]{:S(2)}, u32[]{:S(2)}) collective-permute-start(bf16[8,7168]{1,0:T(8,128)(2,1)S(1)} %get-tuple-element.37), channel_id=1, source_target_pairs={{0,4},{1,5},{2,6},{3,7},{4,0},{5,1},{6,2},{7,3},{8,12},{9,13},{10,... | collective-permute-start | bytes 344072 | tf_op jit(solution)/shard_map/ppermute | solution.py:23
  62.0 9.3 %collective-permute-start.11 = (bf16[8,7168]{1,0:T(8,128)(2,1)S(1)}, bf16[8,7168]{1,0:T(8,128)(2,1)S(1)}, u32[]{:S(2)}, u32[]{:S(2)}) collective-permute-start(bf16[8,7168]{1,0:T(8,128)(2,1)S(1)} %get-tuple-element.38), channel_id=1, source_target_pairs={{0,6},{1,7},{2,4},{3,5},{4,2},{5,3},{6,0},{7,1},{8,14},{9,15},{10,... | collective-permute-start | bytes 344072 | tf_op jit(solution)/shard_map/ppermute | solution.py:23
  64.9 14.8 %collective-permute-start.12 = (bf16[8,7168]{1,0:T(8,128)(2,1)S(1)}, bf16[8,7168]{1,0:T(8,128)(2,1)S(1)}, u32[]{:S(2)}, u32[]{:S(2)}) collective-permute-start(bf16[8,7168]{1,0:T(8,128)(2,1)S(1)} %get-tuple-element.39), channel_id=1, source_target_pairs={{0,8},{1,9},{2,10},{3,11},{4,12},{5,13},{6,14},{7,15},{8,0},{9,1},... | collective-permute-start | bytes 344072 | tf_op jit(solution)/shard_map/ppermute | solution.py:23
  66.3 15.8 %collective-permute-start.13 = (bf16[8,7168]{1,0:T(8,128)(2,1)S(1)}, bf16[8,7168]{1,0:T(8,128)(2,1)S(1)}, u32[]{:S(2)}, u32[]{:S(2)}) collective-permute-start(bf16[8,7168]{1,0:T(8,128)(2,1)S(1)} %get-tuple-element.40), channel_id=1, source_target_pairs={{0,10},{1,11},{2,8},{3,9},{4,14},{5,15},{6,12},{7,13},{8,2},{9,3},... | collective-permute-start | bytes 344072 | tf_op jit(solution)/shard_map/ppermute | solution.py:23
  67.8 17.7 %collective-permute-start.14 = (bf16[8,7168]{1,0:T(8,128)(2,1)S(1)}, bf16[8,7168]{1,0:T(8,128)(2,1)S(1)}, u32[]{:S(2)}, u32[]{:S(2)}) collective-permute-start(bf16[8,7168]{1,0:T(8,128)(2,1)S(1)} %get-tuple-element.41), channel_id=1, source_target_pairs={{0,12},{1,13},{2,14},{3,15},{4,8},{5,9},{6,10},{7,11},{8,4},{9,5},... | collective-permute-start | bytes 344072 | tf_op jit(solution)/shard_map/ppermute | solution.py:23
  69.8 17.9 %collective-permute-start.15 = (bf16[8,7168]{1,0:T(8,128)(2,1)S(1)}, bf16[8,7168]{1,0:T(8,128)(2,1)S(1)}, u32[]{:S(2)}, u32[]{:S(2)}) collective-permute-start(bf16[8,7168]{1,0:T(8,128)(2,1)S(1)} %get-tuple-element.42), channel_id=1, source_target_pairs={{0,14},{1,15},{2,12},{3,13},{4,10},{5,11},{6,8},{7,9},{8,6},{9,7},... | collective-permute-start | bytes 344072 | tf_op jit(solution)/shard_map/ppermute | solution.py:23

commit v5 on v4

--- a/solution.py
+++ b/solution.py
@@ -48,19 +48,17 @@
     return lax.broadcasted_iota(jnp.int32, shape, dim)
 
 
-def slot_matrix(group_me, ids, batches, rows):
+def slot_matrix(group_me, across, batches, rows):
     cap = rows // 2
     count = batches * rows
     block = batches * cap
-    eye = (iota((count, count), 0) == iota((count, count), 1)).astype(jnp.float32)
-    across = lax.dot_general(ids, eye, (((0,), (0,)), ((), ())), preferred_element_type=jnp.float32)
     across = across.astype(jnp.int32)
     shape = (GROUPS * block, count)
     where = iota(shape, 0)
     lane = iota(shape, 1)
     target = group_me ^ (where // block)
     routed = jnp.zeros(shape, jnp.float32)
-    for k in range(ids.shape[1]):
+    for k in range(across.shape[0]):
         routed = jnp.where(across[k : k + 1, :] // EXP_GRP == target, 1.0, routed)
     above, here = iota((count, count), 0), iota((count, count), 1)
     before = jnp.where((above < here) & (above // rows == here // rows), 1.0, 0.0)
@@ -69,15 +67,48 @@
     return jnp.where(taken, routed, 0.0).astype(jnp.bfloat16)
 
 
-def prep_kernel(topk, group_ref, tokens_ref, extra_ref, matrix_ref, *out_refs):
+def side_by_side(ref):
+    batches, topk, rows = ref.shape
+    shape = (rows, batches * rows)
+    return sum(
+        jnp.dot(
+            ref[b].astype(jnp.float32),
+            (iota(shape, 0) + b * rows == iota(shape, 1)).astype(jnp.float32),
+            preferred_element_type=jnp.float32,
+        )
+        for b in range(batches)
+    )
+
+
+def prep_kernel(group_ref, *refs):
+    given, (matrix_ref, *out_refs, tokens_ref, ids_ref, weights_ref, sem) = refs[:3], refs[3:]
     batches, rows, width = tokens_ref.shape
-    extra = extra_ref[...]
-    matrix = slot_matrix(group_ref[0], extra[:, :topk].astype(jnp.float32), batches, rows)
+    copies = [
+        pltpu.make_async_copy(source, ref, sem.at[n])
+        for n, (source, ref) in enumerate(zip(given, (tokens_ref, ids_ref, weights_ref)))
+    ]
+    for copy in copies:
+        copy.start()
+    copies[1].wait()
+    copies[2].wait()
+    ids, weights = side_by_side(ids_ref), side_by_side(weights_ref)
+    matrix = slot_matrix(group_ref[0], ids, batches, rows)
     matrix_ref[...] = matrix
     block = matrix.shape[0] // GROUPS
+    copies[0].wait()
     tokens = tokens_ref[...].reshape(batches * rows, width)
     bucket = jnp.dot(matrix, tokens, preferred_element_type=jnp.float32)
-    more = jnp.dot(matrix, extra, preferred_element_type=jnp.float32)
+    more = [
+        lax.dot_general(
+            matrix.astype(jnp.float32),
+            values,
+            (((1,), (1,)), ((), ())),
+            preferred_element_type=jnp.float32,
+        )
+        for values in (ids, weights)
+    ]
+    pad = jnp.zeros((matrix.shape[0], EXTRA - 2 * ids.shape[0]), jnp.float32)
+    more = jnp.concatenate(more + [pad], axis=1)
     for t, out in enumerate(out_refs):
         out[:, :width] = bucket[t * block : (t + 1) * block].astype(jnp.bfloat16)
         out[:, width:] = more[t * block : (t + 1) * block].astype(jnp.bfloat16)
@@ -212,21 +243,25 @@
         got = {by: exchanged(blocks[by], by, gsize) for by in reversed(range(1, GROUPS))}
         return [blocks[0]] + [got[by] for by in range(1, GROUPS)]
 
-    extra = jnp.concatenate(
-        [
-            expert_ids.astype(jnp.bfloat16),
-            gate_weights,
-            jnp.zeros((batches, rows, EXTRA - 2 * topk), jnp.bfloat16),
-        ],
-        axis=2,
-    ).reshape(count, EXTRA)
     matrix, *buckets = call(
-        functools.partial(prep_kernel, topk),
+        prep_kernel,
         [bf16(GROUPS * block, count)] + [bf16(block, wide)] * GROUPS,
         (2 * GROUPS * block * count * wide, 10 * count * wide),
-        in_specs=[smem, vmem, vmem],
+        in_specs=[smem, hbm, hbm, hbm],
         out_specs=[vmem] * (1 + GROUPS),
-    )(group_me.reshape(1), tokens, extra)
+        scratch_shapes=[
+            pltpu.VMEM(tokens.shape, tokens.dtype),
+            pltpu.VMEM((batches, topk, rows), expert_ids.dtype),
+            pltpu.VMEM((batches, topk, rows), gate_weights.dtype),
+            pltpu.SemaphoreType.DMA((3,)),
+        ],
+    )(
+        group_me.reshape(1),
+        *(
+            pltpu.with_memory_space_constraint(v, pltpu.HBM)
+            for v in (tokens, expert_ids.transpose(0, 2, 1), gate_weights.transpose(0, 2, 1))
+        ),
+    )
     w_gate, w_up, w_down = (
         pltpu.with_memory_space_constraint(w, pltpu.HBM) for w in (w_gate, w_up, w_down)
     )

time: 88.8 us -> 87 us (0.980)
  local copies, waits for them, and re-layouts: 1.9 us -> 0 us
  Pallas kernels: 30.1 us -> 31 us
    unnamed x3 -> x0, local copies, waits for them, and re-layouts: 1.71 us -> none
where the time goes in v5:
time: 87 us; the launch traced here: 86.8 us
  waiting for transfers between devices  36.2 us (42%)
  Pallas kernels  31 us (36%)
  starting transfers between devices  19.5 us (22%)
    ppermute x16, waiting for transfers between devices, exchanged(): lax.ppermute(shard, 'grp', [(i, (i // unit ^ by) * unit + i % unit) for i...  36.2 us
    pallas_call x1, Pallas kernels, body(): call(functools.partial(expert_kernel, len(parts), topk), [bf16(half, widt...  25.3 us
    ppermute x16, starting transfers between devices, exchanged(): lax.ppermute(shard, 'grp', [(i, (i // unit ^ by) * unit + i % unit) for i...  19.5 us
    pallas_call x1, Pallas kernels, body(): call(fetch_kernel, pltpu.VMEM((FETCHED * DEPTH, hid), jnp.bfloat16), (0,...  2.89 us
  transfers between devices with their start and end apart: 16, of which 11 were waited for; matrix products, arithmetic and copies ran while one was open for 0% of the time, Pallas kernels for 3%

profile of v5, /device:TPU:12, one launch (start us, length us, event | category | flops | bytes accessed | tf_op | source)
XLA Modules:
  0.0 86.8 jit_solution(5092919737431032816)
XLA Ops:
  0.0 1.5 %shard_map.64 = (bf16[64,16]{1,0:T(8,128)(2,1)S(1)}, bf16[8,7296]{1,0:T(8,128)(2,1)S(1)}, bf16[8,7296]{1,0:T(8,128)(2,1)S(1)}, bf16[8,7296]{1,0:T(8,128)(2,1)S(1...) custom-call(s32[1]{0:T(128)} %bitcast.group_ref, ...), custom_call_target="tpu_custom_call" | custom-call | flops 14942208 | bytes 1167360 | tf_op jit(solution)/shard_map/pallas_call | solution.py:246
  1.6 1.6 %collective-permute-start = (bf16[8,7296]{1,0:T(8,128)(2,1)S(1)}, bf16[8,7296]{1,0:T(8,128)(2,1)S(1)}, u32[]{:S(2)}, u32[]{:S(2)}) collective-permute-start(bf16[8,7296]{1,0:T(8,128)(2,1)S(1)} %get-tuple-element.26), channel_id=1, source_target_pairs={{0,2},{1,3},{2,0},{3,1},{4,6},{5,7},{6,4},{7,5},{8,10},{9,11},{10,... | collective-permute-start | bytes 350216 | tf_op jit(solution)/shard_map/ppermute | solution.py:23
  3.1 0.4 collective-permute-start.1
  3.6 1.5 %collective-permute-start.2 = (bf16[8,7296]{1,0:T(8,128)(2,1)S(1)}, bf16[8,7296]{1,0:T(8,128)(2,1)S(1)}, u32[]{:S(2)}, u32[]{:S(2)}) collective-permute-start(bf16[8,7296]{1,0:T(8,128)(2,1)S(1)} %get-tuple-element.28), channel_id=1, source_target_pairs={{0,6},{1,7},{2,4},{3,5},{4,2},{5,3},{6,0},{7,1},{8,14},{9,15},{10,... | collective-permute-start | bytes 350216 | tf_op jit(solution)/shard_map/ppermute | solution.py:23
  5.1 2.6 %collective-permute-start.3 = (bf16[8,7296]{1,0:T(8,128)(2,1)S(1)}, bf16[8,7296]{1,0:T(8,128)(2,1)S(1)}, u32[]{:S(2)}, u32[]{:S(2)}) collective-permute-start(bf16[8,7296]{1,0:T(8,128)(2,1)S(1)} %get-tuple-element.29), channel_id=1, source_target_pairs={{0,8},{1,9},{2,10},{3,11},{4,12},{5,13},{6,14},{7,15},{8,0},{9,1},... | collective-permute-start | bytes 350216 | tf_op jit(solution)/shard_map/ppermute | solution.py:23
  7.7 1.3 %collective-permute-start.4 = (bf16[8,7296]{1,0:T(8,128)(2,1)S(1)}, bf16[8,7296]{1,0:T(8,128)(2,1)S(1)}, u32[]{:S(2)}, u32[]{:S(2)}) collective-permute-start(bf16[8,7296]{1,0:T(8,128)(2,1)S(1)} %get-tuple-element.30), channel_id=1, source_target_pairs={{0,10},{1,11},{2,8},{3,9},{4,14},{5,15},{6,12},{7,13},{8,2},{9,3},... | collective-permute-start | bytes 350216 | tf_op jit(solution)/shard_map/ppermute | solution.py:23
  9.0 1.6 %collective-permute-start.5 = (bf16[8,7296]{1,0:T(8,128)(2,1)S(1)}, bf16[8,7296]{1,0:T(8,128)(2,1)S(1)}, u32[]{:S(2)}, u32[]{:S(2)}) collective-permute-start(bf16[8,7296]{1,0:T(8,128)(2,1)S(1)} %get-tuple-element.31), channel_id=1, source_target_pairs={{0,12},{1,13},{2,14},{3,15},{4,8},{5,9},{6,10},{7,11},{8,4},{9,5},... | collective-permute-start | bytes 350216 | tf_op jit(solution)/shard_map/ppermute | solution.py:23
  10.5 0.4 collective-permute-start.6
  11.0 1.2 %collective-permute-done.2.refs_3_ = bf16[8,7296]{1,0:T(8,128)(2,1)S(1)} collective-permute-done((bf16[8,7296]{1,0:T(8,128)(2,1)S(1)}, bf16[8,7296]{1,0:T(8,128)(2,1)S(1)}, u32[]{:S(2)}, u32[]{:S(2)}) %collective-permute-start.2) | collective-permute-done | bytes 116768 | tf_op jit(solution)/shard_map/ppermute | solution.py:23
  12.2 8.7 %collective-permute-done.3.refs_4_ = bf16[8,7296]{1,0:T(8,128)(2,1)S(1)} collective-permute-done((bf16[8,7296]{1,0:T(8,128)(2,1)S(1)}, bf16[8,7296]{1,0:T(8,128)(2,1)S(1)}, u32[]{:S(2)}, u32[]{:S(2)}) %collective-permute-start.3) | collective-permute-done | bytes 116768 | tf_op jit(solution)/shard_map/ppermute | solution.py:23
  20.9 2.5 %collective-permute-done.4.refs_5_ = bf16[8,7296]{1,0:T(8,128)(2,1)S(1)} collective-permute-done((bf16[8,7296]{1,0:T(8,128)(2,1)S(1)}, bf16[8,7296]{1,0:T(8,128)(2,1)S(1)}, u32[]{:S(2)}, u32[]{:S(2)}) %collective-permute-start.4) | collective-permute-done | bytes 116768 | tf_op jit(solution)/shard_map/ppermute | solution.py:23
  23.4 2.7 %collective-permute-done.5.refs_6_ = bf16[8,7296]{1,0:T(8,128)(2,1)S(1)} collective-permute-done((bf16[8,7296]{1,0:T(8,128)(2,1)S(1)}, bf16[8,7296]{1,0:T(8,128)(2,1)S(1)}, u32[]{:S(2)}, u32[]{:S(2)}) %collective-permute-start.5) | collective-permute-done | bytes 116768 | tf_op jit(solution)/shard_map/ppermute | solution.py:23
  26.1 2.2 %collective-permute-done.6.refs_7_ = bf16[8,7296]{1,0:T(8,128)(2,1)S(1)} collective-permute-done((bf16[8,7296]{1,0:T(8,128)(2,1)S(1)}, bf16[8,7296]{1,0:T(8,128)(2,1)S(1)}, u32[]{:S(2)}, u32[]{:S(2)}) %collective-permute-start.6) | collective-permute-done | bytes 116768 | tf_op jit(solution)/shard_map/ppermute | solution.py:23
  28.2 0.1 shard_map.65.refs_0_
  28.3 0.1 collective-permute-start.7
  28.4 2.9 %shard_map.66.refs_2_ = bf16[1536,2048]{1,0:T(8,128)(2,1)S(1)} custom-call(bf16[64,16]{1,0:T(8,128)(2,1)S(1)} %get-tuple-element.24.after_ref.matrix_ref, bf16[1,7168,2048]{2,1,0:T(8,128)(2,1)} %refs_3_.1), custom_call_target="tpu_custom_call" | custom-call | bytes 12582912 | tf_op jit(solution)/shard_map/pallas_call | solution.py:268
  31.3 25.3 %shard_map.67 = (bf16[64,7168]{1,0:T(8,128)(2,1)S(1)}, bf16[64,7168]{1,0:T(8,128)(2,1)S(1)}) custom-call(s32[1]{0:T(128)} %bitcast.3.expert_ref, bf16[64,7296]{1,0:T(8,128)(2,1)S(1)} %shard_map.65.refs_0_, bf16[64,7296]{1,0:T(8,128)(2,1)S(1)} %collective-permute-done.7.refs_1_, bf16[1536,2048]{1,0:T(8,128)(2,1)S(1)} %shard_map.66.refs_2_, ...), custom_call_target="tpu_custom_call" | custom-call | flops 11274289152 | bytes 58720256 | tf_op jit(solution)/shard_map/pallas_call | solution.py:291
  56.6 0.5 collective-permute-start.8
  57.2 2.1 %collective-permute-done.8.got_ref = bf16[64,7168]{1,0:T(8,128)(2,1)S(1)} collective-permute-done((bf16[64,7168]{1,0:T(8,128)(2,1)S(1)}, bf16[64,7168]{1,0:T(8,128)(2,1)S(1)}, u32[]{:S(2)}, u32[]{:S(2)}) %collective-permute-start.8) | collective-permute-done | bytes 917536 | tf_op jit(solution)/shard_map/ppermute | solution.py:23
  59.3 0.2 shard_map.68
  59.5 0.7 collective-permute-start.9
  60.1 2.9 %collective-permute-start.11 = (bf16[8,7168]{1,0:T(8,128)(2,1)S(1)}, bf16[8,7168]{1,0:T(8,128)(2,1)S(1)}, u32[]{:S(2)}, u32[]{:S(2)}) collective-permute-start(bf16[8,7168]{1,0:T(8,128)(2,1)S(1)} %get-tuple-element.38), channel_id=1, source_target_pairs={{0,6},{1,7},{2,4},{3,5},{4,2},{5,3},{6,0},{7,1},{8,14},{9,15},{10,... | collective-permute-start | bytes 344072 | tf_op jit(solution)/shard_map/ppermute | solution.py:23
  63.0 1.4 %collective-permute-start.12 = (bf16[8,7168]{1,0:T(8,128)(2,1)S(1)}, bf16[8,7168]{1,0:T(8,128)(2,1)S(1)}, u32[]{:S(2)}, u32[]{:S(2)}) collective-permute-start(bf16[8,7168]{1,0:T(8,128)(2,1)S(1)} %get-tuple-element.39), channel_id=1, source_target_pairs={{0,8},{1,9},{2,10},{3,11},{4,12},{5,13},{6,14},{7,15},{8,0},{9,1},... | collective-permute-start | bytes 344072 | tf_op jit(solution)/shard_map/ppermute | solution.py:23
  64.5 1.5 %collective-permute-start.13 = (bf16[8,7168]{1,0:T(8,128)(2,1)S(1)}, bf16[8,7168]{1,0:T(8,128)(2,1)S(1)}, u32[]{:S(2)}, u32[]{:S(2)}) collective-permute-start(bf16[8,7168]{1,0:T(8,128)(2,1)S(1)} %get-tuple-element.40), channel_id=1, source_target_pairs={{0,10},{1,11},{2,8},{3,9},{4,14},{5,15},{6,12},{7,13},{8,2},{9,3},... | collective-permute-start | bytes 344072 | tf_op jit(solution)/shard_map/ppermute | solution.py:23
  66.0 1.9 %collective-permute-start.14 = (bf16[8,7168]{1,0:T(8,128)(2,1)S(1)}, bf16[8,7168]{1,0:T(8,128)(2,1)S(1)}, u32[]{:S(2)}, u32[]{:S(2)}) collective-permute-start(bf16[8,7168]{1,0:T(8,128)(2,1)S(1)} %get-tuple-element.41), channel_id=1, source_target_pairs={{0,12},{1,13},{2,14},{3,15},{4,8},{5,9},{6,10},{7,11},{8,4},{9,5},... | collective-permute-start | bytes 344072 | tf_op jit(solution)/shard_map/ppermute | solution.py:23
  68.0 1.0 %collective-permute-start.15 = (bf16[8,7168]{1,0:T(8,128)(2,1)S(1)}, bf16[8,7168]{1,0:T(8,128)(2,1)S(1)}, u32[]{:S(2)}, u32[]{:S(2)}) collective-permute-start(bf16[8,7168]{1,0:T(8,128)(2,1)S(1)} %get-tuple-element.42), channel_id=1, source_target_pairs={{0,14},{1,15},{2,12},{3,13},{4,10},{5,11},{6,8},{7,9},{8,6},{9,7},... | collective-permute-start | bytes 344072 | tf_op jit(solution)/shard_map/ppermute | solution.py:23
  69.0 0.5 collective-permute-done.11.refs_3_
  69.5 8.4 %collective-permute-done.12.refs_4_ = bf16[8,7168]{1,0:T(8,128)(2,1)S(1)} collective-permute-done((bf16[8,7168]{1,0:T(8,128)(2,1)S(1)}, bf16[8,7168]{1,0:T(8,128)(2,1)S(1)}, u32[]{:S(2)}, u32[]{:S(2)}) %collective-permute-start.12) | collective-permute-done | bytes 114720 | tf_op jit(solution)/shard_map/ppermute | solution.py:23
  77.9 2.5 %collective-permute-done.13.refs_5_ = bf16[8,7168]{1,0:T(8,128)(2,1)S(1)} collective-permute-done((bf16[8,7168]{1,0:T(8,128)(2,1)S(1)}, bf16[8,7168]{1,0:T(8,128)(2,1)S(1)}, u32[]{:S(2)}, u32[]{:S(2)}) %collective-permute-start.13) | collective-permute-done | bytes 114720 | tf_op jit(solution)/shard_map/ppermute | solution.py:23
  80.3 3.4 %collective-permute-done.14.refs_6_ = bf16[8,7168]{1,0:T(8,128)(2,1)S(1)} collective-permute-done((bf16[8,7168]{1,0:T(8,128)(2,1)S(1)}, bf16[8,7168]{1,0:T(8,128)(2,1)S(1)}, u32[]{:S(2)}, u32[]{:S(2)}) %collective-permute-start.14) | collective-permute-done | bytes 114720 | tf_op jit(solution)/shard_map/ppermute | solution.py:23
  83.7 2.2 %collective-permute-done.15.refs_7_ = bf16[8,7168]{1,0:T(8,128)(2,1)S(1)} collective-permute-done((bf16[8,7168]{1,0:T(8,128)(2,1)S(1)}, bf16[8,7168]{1,0:T(8,128)(2,1)S(1)}, u32[]{:S(2)}, u32[]{:S(2)}) %collective-permute-start.15) | collective-permute-done | bytes 114720 | tf_op jit(solution)/shard_map/ppermute | solution.py:23
  85.9 1.0 %shard_map.69 = bf16[2,8,7168]{2,1,0:T(8,128)(2,1)} custom-call(bf16[64,16]{1,0:T(8,128)(2,1)S(1)} %get-tuple-element.24.after_ref.matrix_ref, bf16[8,7168]{1,0:T(8,128)(2,1)S(1)} %get-tuple-element.35.refs_0_, bf16[8,7168]{1,0:T(8,128)(2,1)S(1)} %collective-permute-done.9.refs_1_, bf16[8,7168]{1,0:T(8,128)(2,1)S(1)} %collective-permute-done.10.refs_2_, ...), custom_call_target="tpu_custom_call" | custom-call | flops 14680064 | bytes 1146880 | tf_op jit(solution)/shard_map/pallas_call | solution.py:323
  (6 shorter events, 0.0 us)
Async XLA Ops:
  1.6 7.4 %collective-permute-start = (bf16[8,7296]{1,0:T(8,128)(2,1)S(1)}, bf16[8,7296]{1,0:T(8,128)(2,1)S(1)}, u32[]{:S(2)}, u32[]{:S(2)}) collective-permute-start(bf16[8,7296]{1,0:T(8,128)(2,1)S(1)} %get-tuple-element.26), channel_id=1, source_target_pairs={{0,2},{1,3},{2,0},{3,1},{4,6},{5,7},{6,4},{7,5},{8,10},{9,11},{10,... | collective-permute-start | bytes 350216 | tf_op jit(solution)/shard_map/ppermute | solution.py:23
  3.1 7.4 %collective-permute-start.1 = (bf16[8,7296]{1,0:T(8,128)(2,1)S(1)}, bf16[8,7296]{1,0:T(8,128)(2,1)S(1)}, u32[]{:S(2)}, u32[]{:S(2)}) collective-permute-start(bf16[8,7296]{1,0:T(8,128)(2,1)S(1)} %get-tuple-element.27), channel_id=1, source_target_pairs={{0,4},{1,5},{2,6},{3,7},{4,0},{5,1},{6,2},{7,3},{8,12},{9,13},{10,... | collective-permute-start | bytes 350216 | tf_op jit(solution)/shard_map/ppermute | solution.py:23
  3.6 8.6 %collective-permute-start.2 = (bf16[8,7296]{1,0:T(8,128)(2,1)S(1)}, bf16[8,7296]{1,0:T(8,128)(2,1)S(1)}, u32[]{:S(2)}, u32[]{:S(2)}) collective-permute-start(bf16[8,7296]{1,0:T(8,128)(2,1)S(1)} %get-tuple-element.28), channel_id=1, source_target_pairs={{0,6},{1,7},{2,4},{3,5},{4,2},{5,3},{6,0},{7,1},{8,14},{9,15},{10,... | collective-permute-start | bytes 350216 | tf_op jit(solution)/shard_map/ppermute | solution.py:23
  5.1 15.7 %collective-permute-start.3 = (bf16[8,7296]{1,0:T(8,128)(2,1)S(1)}, bf16[8,7296]{1,0:T(8,128)(2,1)S(1)}, u32[]{:S(2)}, u32[]{:S(2)}) collective-permute-start(bf16[8,7296]{1,0:T(8,128)(2,1)S(1)} %get-tuple-element.29), channel_id=1, source_target_pairs={{0,8},{1,9},{2,10},{3,11},{4,12},{5,13},{6,14},{7,15},{8,0},{9,1},... | collective-permute-start | bytes 350216 | tf_op jit(solution)/shard_map/ppermute | solution.py:23
  7.7 15.7 %collective-permute-start.4 = (bf16[8,7296]{1,0:T(8,128)(2,1)S(1)}, bf16[8,7296]{1,0:T(8,128)(2,1)S(1)}, u32[]{:S(2)}, u32[]{:S(2)}) collective-permute-start(bf16[8,7296]{1,0:T(8,128)(2,1)S(1)} %get-tuple-element.30), channel_id=1, source_target_pairs={{0,10},{1,11},{2,8},{3,9},{4,14},{5,15},{6,12},{7,13},{8,2},{9,3},... | collective-permute-start | bytes 350216 | tf_op jit(solution)/shard_map/ppermute | solution.py:23
  9.0 17.1 %collective-permute-start.5 = (bf16[8,7296]{1,0:T(8,128)(2,1)S(1)}, bf16[8,7296]{1,0:T(8,128)(2,1)S(1)}, u32[]{:S(2)}, u32[]{:S(2)}) collective-permute-start(bf16[8,7296]{1,0:T(8,128)(2,1)S(1)} %get-tuple-element.31), channel_id=1, source_target_pairs={{0,12},{1,13},{2,14},{3,15},{4,8},{5,9},{6,10},{7,11},{8,4},{9,5},... | collective-permute-start | bytes 350216 | tf_op jit(solution)/shard_map/ppermute | solution.py:23
  10.5 17.7 %collective-permute-start.6 = (bf16[8,7296]{1,0:T(8,128)(2,1)S(1)}, bf16[8,7296]{1,0:T(8,128)(2,1)S(1)}, u32[]{:S(2)}, u32[]{:S(2)}) collective-permute-start(bf16[8,7296]{1,0:T(8,128)(2,1)S(1)} %get-tuple-element.32), channel_id=1, source_target_pairs={{0,14},{1,15},{2,12},{3,13},{4,10},{5,11},{6,8},{7,9},{8,6},{9,7},... | collective-permute-start | bytes 350216 | tf_op jit(solution)/shard_map/ppermute | solution.py:23
  28.3 3.0 %collective-permute-start.7 = (bf16[64,7296]{1,0:T(8,128)(2,1)S(1)}, bf16[64,7296]{1,0:T(8,128)(2,1)S(1)}, u32[]{:S(2)}, u32[]{:S(2)}) collective-permute-start(bf16[64,7296]{1,0:T(8,128)(2,1)S(1)} %shard_map.65.refs_0_), channel_id=1, source_target_pairs={{0,1},{1,0},{2,3},{3,2},{4,5},{5,4},{6,7},{7,6},{8,9},{9,8},{10,11... | collective-permute-start | bytes 2801672 | tf_op jit(solution)/shard_map/ppermute | solution.py:23
  56.6 2.6 %collective-permute-start.8 = (bf16[64,7168]{1,0:T(8,128)(2,1)S(1)}, bf16[64,7168]{1,0:T(8,128)(2,1)S(1)}, u32[]{:S(2)}, u32[]{:S(2)}) collective-permute-start(bf16[64,7168]{1,0:T(8,128)(2,1)S(1)} %get-tuple-element.34), channel_id=1, source_target_pairs={{0,1},{1,0},{2,3},{3,2},{4,5},{5,4},{6,7},{7,6},{8,9},{9,8},{10,11... | collective-permute-start | bytes 2752520 | tf_op jit(solution)/shard_map/ppermute | solution.py:23
  59.5 6.5 %collective-permute-start.9 = (bf16[8,7168]{1,0:T(8,128)(2,1)S(1)}, bf16[8,7168]{1,0:T(8,128)(2,1)S(1)}, u32[]{:S(2)}, u32[]{:S(2)}) collective-permute-start(bf16[8,7168]{1,0:T(8,128)(2,1)S(1)} %get-tuple-element.36), channel_id=1, source_target_pairs={{0,2},{1,3},{2,0},{3,1},{4,6},{5,7},{6,4},{7,5},{8,10},{9,11},{10,... | collective-permute-start | bytes 344072 | tf_op jit(solution)/shard_map/ppermute | solution.py:23
  60.1 7.8 %collective-permute-start.10 = (bf16[8,7168]{1,0:T(8,128)(2,1)S(1)}, bf16[8,7168]{1,0:T(8,128)(2,1)S(1)}, u32[]{:S(2)}, u32[]{:S(2)}) collective-permute-start(bf16[8,7168]{1,0:T(8,128)(2,1)S(1)} %get-tuple-element.37), channel_id=1, source_target_pairs={{0,4},{1,5},{2,6},{3,7},{4,0},{5,1},{6,2},{7,3},{8,12},{9,13},{10,... | collective-permute-start | bytes 344072 | tf_op jit(solution)/shard_map/ppermute | solution.py:23
  60.1 9.3 %collective-permute-start.11 = (bf16[8,7168]{1,0:T(8,128)(2,1)S(1)}, bf16[8,7168]{1,0:T(8,128)(2,1)S(1)}, u32[]{:S(2)}, u32[]{:S(2)}) collective-permute-start(bf16[8,7168]{1,0:T(8,128)(2,1)S(1)} %get-tuple-element.38), channel_id=1, source_target_pairs={{0,6},{1,7},{2,4},{3,5},{4,2},{5,3},{6,0},{7,1},{8,14},{9,15},{10,... | collective-permute-start | bytes 344072 | tf_op jit(solution)/shard_map/ppermute | solution.py:23
  63.0 14.8 %collective-permute-start.12 = (bf16[8,7168]{1,0:T(8,128)(2,1)S(1)}, bf16[8,7168]{1,0:T(8,128)(2,1)S(1)}, u32[]{:S(2)}, u32[]{:S(2)}) collective-permute-start(bf16[8,7168]{1,0:T(8,128)(2,1)S(1)} %get-tuple-element.39), channel_id=1, source_target_pairs={{0,8},{1,9},{2,10},{3,11},{4,12},{5,13},{6,14},{7,15},{8,0},{9,1},... | collective-permute-start | bytes 344072 | tf_op jit(solution)/shard_map/ppermute | solution.py:23
  64.5 15.8 %collective-permute-start.13 = (bf16[8,7168]{1,0:T(8,128)(2,1)S(1)}, bf16[8,7168]{1,0:T(8,128)(2,1)S(1)}, u32[]{:S(2)}, u32[]{:S(2)}) collective-permute-start(bf16[8,7168]{1,0:T(8,128)(2,1)S(1)} %get-tuple-element.40), channel_id=1, source_target_pairs={{0,10},{1,11},{2,8},{3,9},{4,14},{5,15},{6,12},{7,13},{8,2},{9,3},... | collective-permute-start | bytes 344072 | tf_op jit(solution)/shard_map/ppermute | solution.py:23
  66.0 17.7 %collective-permute-start.14 = (bf16[8,7168]{1,0:T(8,128)(2,1)S(1)}, bf16[8,7168]{1,0:T(8,128)(2,1)S(1)}, u32[]{:S(2)}, u32[]{:S(2)}) collective-permute-start(bf16[8,7168]{1,0:T(8,128)(2,1)S(1)} %get-tuple-element.41), channel_id=1, source_target_pairs={{0,12},{1,13},{2,14},{3,15},{4,8},{5,9},{6,10},{7,11},{8,4},{9,5},... | collective-permute-start | bytes 344072 | tf_op jit(solution)/shard_map/ppermute | solution.py:23
  68.0 17.9 %collective-permute-start.15 = (bf16[8,7168]{1,0:T(8,128)(2,1)S(1)}, bf16[8,7168]{1,0:T(8,128)(2,1)S(1)}, u32[]{:S(2)}, u32[]{:S(2)}) collective-permute-start(bf16[8,7168]{1,0:T(8,128)(2,1)S(1)} %get-tuple-element.42), channel_id=1, source_target_pairs={{0,14},{1,15},{2,12},{3,13},{4,10},{5,11},{6,8},{7,9},{8,6},{9,7},... | collective-permute-start | bytes 344072 | tf_op jit(solution)/shard_map/ppermute | solution.py:23

commit v6 on v5

--- a/solution.py
+++ b/solution.py
@@ -15,7 +15,8 @@
 AHEAD = 4
 SMALL = 8 << 20
 SLACK = 1 << 20
-FETCHED = 3
+FETCHED = 2
+ORDER = (7, 6, 5, 4, 3, 2, 1)
 
 
 def exchanged(shard, by, unit):
@@ -240,7 +241,7 @@
     hbm = pl.BlockSpec(memory_space=pl.ANY)
 
     def to_all(blocks):
-        got = {by: exchanged(blocks[by], by, gsize) for by in reversed(range(1, GROUPS))}
+        got = {by: exchanged(blocks[by], by, gsize) for by in ORDER}
         return [blocks[0]] + [got[by] for by in range(1, GROUPS)]
 
     matrix, *buckets = call(
@@ -274,18 +275,23 @@
         scratch_shapes=[pltpu.SemaphoreType.DMA((FETCHED,))],
     )(matrix, w_gate)
     fetched = pltpu.with_memory_space_constraint(fetched, pltpu.VMEM)
-    parts = [
-        call(
-            join_kernel,
-            bf16(GROUPS * block, wide),
-            (0, 4 * GROUPS * block * wide),
-            in_specs=[vmem] * GROUPS,
-            out_specs=vmem,
-        )(*to_all(buckets))
-    ]
+    blocks = to_all(buckets)
+    near, far = blocks[: GROUPS // 2], blocks[GROUPS // 2 :]
+    parts = []
+    for side in (near, far):
+        if parts:
+            side, parts = lax.optimization_barrier((side, parts))
+        parts = parts + [
+            call(
+                join_kernel,
+                bf16(GROUPS // 2 * block, wide),
+                (0, 2 * GROUPS * block * wide),
+                in_specs=[vmem] * (GROUPS // 2),
+                out_specs=vmem,
+            )(*side)
+        ]
     for bit in range(in_bits):
-        all_rows = parts[0] if bit == 0 else jnp.concatenate(parts)
-        parts.append(exchanged(all_rows, 1 << bit, 1))
+        parts += [exchanged(part, 1 << bit, 1) for part in parts]
 
     slots = 2 * AHEAD * max(DEPTH, COLUMNS) * hid * 2
     kept, away = call(

time: 87 us -> 85.2 us (0.979)
  waiting for transfers between devices: 36.2 us -> 34.5 us
    ppermute x16 -> x17, waiting for transfers between devices: 36.2 us -> 34.5 us  [exchanged(): lax.ppermute(shard, 'grp', [(i, (i // unit ^ by) * unit + i % unit) for i...]
    ppermute x16 -> x17, starting transfers between devices: 19.5 us -> 19.5 us  [exchanged(): lax.ppermute(shard, 'grp', [(i, (i // unit ^ by) * unit + i % unit) for i...]
  transfers between devices with their start and end apart: 16 -> 17, of which waited for: 11 -> 10; matrix products, arithmetic and copies ran while one was open for 0% -> 0% of each run, Pallas kernels for 3% -> 3%
where the time goes in v6:
time: 85.2 us; the launch traced here: 85 us
  waiting for transfers between devices  34.5 us (40%)
  Pallas kernels  30.9 us (36%)
  starting transfers between devices  19.5 us (23%)
    ppermute x17, waiting for transfers between devices, exchanged(): lax.ppermute(shard, 'grp', [(i, (i // unit ^ by) * unit + i % unit) for i...  34.5 us
    pallas_call x1, Pallas kernels, body(): call(functools.partial(expert_kernel, len(parts), topk), [bf16(half, widt...  25.9 us
    ppermute x17, starting transfers between devices, exchanged(): lax.ppermute(shard, 'grp', [(i, (i // unit ^ by) * unit + i % unit) for i...  19.5 us
    pallas_call x1, Pallas kernels, body(): call(fetch_kernel, pltpu.VMEM((FETCHED * DEPTH, hid), jnp.bfloat16), (0,...  2.24 us
  transfers between devices with their start and end apart: 17, of which 10 were waited for; matrix products, arithmetic and copies ran while one was open for 0% of the time, Pallas kernels for 3%

profile of v6, /device:TPU:12, one launch (start us, length us, event | category | flops | bytes accessed | tf_op | source)
XLA Modules:
  0.0 85.0 jit_solution(8094739569033958272)
XLA Ops:
  0.0 1.5 %shard_map.64 = (bf16[64,16]{1,0:T(8,128)(2,1)S(1)}, bf16[8,7296]{1,0:T(8,128)(2,1)S(1)}, bf16[8,7296]{1,0:T(8,128)(2,1)S(1)}, bf16[8,7296]{1,0:T(8,128)(2,1)S(1...) custom-call(s32[1]{0:T(128)} %bitcast.group_ref, ...), custom_call_target="tpu_custom_call" | custom-call | flops 14942208 | bytes 1167360 | tf_op jit(solution)/shard_map/pallas_call | solution.py:247
  1.6 1.6 %collective-permute-start.4 = (bf16[8,7296]{1,0:T(8,128)(2,1)S(1)}, bf16[8,7296]{1,0:T(8,128)(2,1)S(1)}, u32[]{:S(2)}, u32[]{:S(2)}) collective-permute-start(bf16[8,7296]{1,0:T(8,128)(2,1)S(1)} %get-tuple-element.35), channel_id=1, source_target_pairs={{0,2},{1,3},{2,0},{3,1},{4,6},{5,7},{6,4},{7,5},{8,10},{9,11},{10,... | collective-permute-start | bytes 350216 | tf_op jit(solution)/shard_map/ppermute | solution.py:24
  3.1 0.4 collective-permute-start.5
  3.6 2.6 %collective-permute-start = (bf16[8,7296]{1,0:T(8,128)(2,1)S(1)}, bf16[8,7296]{1,0:T(8,128)(2,1)S(1)}, u32[]{:S(2)}, u32[]{:S(2)}) collective-permute-start(bf16[8,7296]{1,0:T(8,128)(2,1)S(1)} %get-tuple-element.30), channel_id=1, source_target_pairs={{0,8},{1,9},{2,10},{3,11},{4,12},{5,13},{6,14},{7,15},{8,0},{9,1},... | collective-permute-start | bytes 350216 | tf_op jit(solution)/shard_map/ppermute | solution.py:24
  6.1 0.3 collective-permute-start.1
  6.5 2.5 %collective-permute-start.6 = (bf16[8,7296]{1,0:T(8,128)(2,1)S(1)}, bf16[8,7296]{1,0:T(8,128)(2,1)S(1)}, u32[]{:S(2)}, u32[]{:S(2)}) collective-permute-start(bf16[8,7296]{1,0:T(8,128)(2,1)S(1)} %get-tuple-element.37), channel_id=1, source_target_pairs={{0,6},{1,7},{2,4},{3,5},{4,2},{5,3},{6,0},{7,1},{8,14},{9,15},{10,... | collective-permute-start | bytes 350216 | tf_op jit(solution)/shard_map/ppermute | solution.py:24
  9.0 1.6 %collective-permute-start.2 = (bf16[8,7296]{1,0:T(8,128)(2,1)S(1)}, bf16[8,7296]{1,0:T(8,128)(2,1)S(1)}, u32[]{:S(2)}, u32[]{:S(2)}) collective-permute-start(bf16[8,7296]{1,0:T(8,128)(2,1)S(1)} %get-tuple-element.32), channel_id=1, source_target_pairs={{0,12},{1,13},{2,14},{3,15},{4,8},{5,9},{6,10},{7,11},{8,4},{9,5},... | collective-permute-start | bytes 350216 | tf_op jit(solution)/shard_map/ppermute | solution.py:24
  10.5 0.4 collective-permute-start.3
  11.0 5.8 %collective-permute-done.6.refs_3_ = bf16[8,7296]{1,0:T(8,128)(2,1)S(1)} collective-permute-done((bf16[8,7296]{1,0:T(8,128)(2,1)S(1)}, bf16[8,7296]{1,0:T(8,128)(2,1)S(1)}, u32[]{:S(2)}, u32[]{:S(2)}) %collective-permute-start.6) | collective-permute-done | bytes 116768 | tf_op jit(solution)/shard_map/ppermute | solution.py:24
  16.8 5.1 %collective-permute-done.1.refs_1_ = bf16[8,7296]{1,0:T(8,128)(2,1)S(1)} collective-permute-done((bf16[8,7296]{1,0:T(8,128)(2,1)S(1)}, bf16[8,7296]{1,0:T(8,128)(2,1)S(1)}, u32[]{:S(2)}, u32[]{:S(2)}) %collective-permute-start.1) | collective-permute-done | bytes 116768 | tf_op jit(solution)/shard_map/ppermute | solution.py:24
  22.0 3.0 %collective-permute-done.2.refs_2_ = bf16[8,7296]{1,0:T(8,128)(2,1)S(1)} collective-permute-done((bf16[8,7296]{1,0:T(8,128)(2,1)S(1)}, bf16[8,7296]{1,0:T(8,128)(2,1)S(1)}, u32[]{:S(2)}, u32[]{:S(2)}) %collective-permute-start.2) | collective-permute-done | bytes 116768 | tf_op jit(solution)/shard_map/ppermute | solution.py:24
  25.0 1.5 %collective-permute-done.3.refs_3_ = bf16[8,7296]{1,0:T(8,128)(2,1)S(1)} collective-permute-done((bf16[8,7296]{1,0:T(8,128)(2,1)S(1)}, bf16[8,7296]{1,0:T(8,128)(2,1)S(1)}, u32[]{:S(2)}, u32[]{:S(2)}) %collective-permute-start.3) | collective-permute-done | bytes 116768 | tf_op jit(solution)/shard_map/ppermute | solution.py:24
  26.5 0.1 collective-permute-start.8
  26.6 0.5 collective-permute-start.7
  27.1 2.2 %shard_map.67.refs_4_ = bf16[1024,2048]{1,0:T(8,128)(2,1)S(1)} custom-call(bf16[64,16]{1,0:T(8,128)(2,1)S(1)} %get-tuple-element.29.after_ref.matrix_ref, bf16[1,7168,2048]{2,1,0:T(8,128)(2,1)} %refs_5_.1), custom_call_target="tpu_custom_call" | custom-call | bytes 8388608 | tf_op jit(solution)/shard_map/pallas_call | solution.py:269
  29.3 0.0 collective-permute-done.8.refs_3_
  29.3 25.9 %shard_map.68 = (bf16[64,7168]{1,0:T(8,128)(2,1)S(1)}, bf16[64,7168]{1,0:T(8,128)(2,1)S(1)}) custom-call(s32[1]{0:T(128)} %bitcast.3.expert_ref, bf16[32,7296]{1,0:T(8,128)(2,1)S(1)} %shard_map.65.refs_0_, bf16[32,7296]{1,0:T(8,128)(2,1)S(1)} %shard_map.66.refs_1_, bf16[32,7296]{1,0:T(8,128)(2,1)S(1)} %collective-permute-done.7.refs_2_, ...), custom_call_target="tpu_custom_call" | custom-call | flops 11274289152 | bytes 58720256 | tf_op jit(solution)/shard_map/pallas_call | solution.py:297
  55.2 0.2 collective-permute-start.9
  55.4 2.4 %collective-permute-done.9.got_ref = bf16[64,7168]{1,0:T(8,128)(2,1)S(1)} collective-permute-done((bf16[64,7168]{1,0:T(8,128)(2,1)S(1)}, bf16[64,7168]{1,0:T(8,128)(2,1)S(1)}, u32[]{:S(2)}, u32[]{:S(2)}) %collective-permute-start.9) | collective-permute-done | bytes 917536 | tf_op jit(solution)/shard_map/ppermute | solution.py:24
  57.8 0.2 shard_map.69
  58.0 1.6 %collective-permute-start.10 = (bf16[8,7168]{1,0:T(8,128)(2,1)S(1)}, bf16[8,7168]{1,0:T(8,128)(2,1)S(1)}, u32[]{:S(2)}, u32[]{:S(2)}) collective-permute-start(bf16[8,7168]{1,0:T(8,128)(2,1)S(1)} %get-tuple-element.46), channel_id=1, source_target_pairs={{0,2},{1,3},{2,0},{3,1},{4,6},{5,7},{6,4},{7,5},{8,10},{9,11},{10,... | collective-permute-start | bytes 344072 | tf_op jit(solution)/shard_map/ppermute | solution.py:24
  59.6 2.0 %collective-permute-start.12 = (bf16[8,7168]{1,0:T(8,128)(2,1)S(1)}, bf16[8,7168]{1,0:T(8,128)(2,1)S(1)}, u32[]{:S(2)}, u32[]{:S(2)}) collective-permute-start(bf16[8,7168]{1,0:T(8,128)(2,1)S(1)} %get-tuple-element.48), channel_id=1, source_target_pairs={{0,6},{1,7},{2,4},{3,5},{4,2},{5,3},{6,0},{7,1},{8,14},{9,15},{10,... | collective-permute-start | bytes 344072 | tf_op jit(solution)/shard_map/ppermute | solution.py:24
  61.6 1.1 %collective-permute-start.13 = (bf16[8,7168]{1,0:T(8,128)(2,1)S(1)}, bf16[8,7168]{1,0:T(8,128)(2,1)S(1)}, u32[]{:S(2)}, u32[]{:S(2)}) collective-permute-start(bf16[8,7168]{1,0:T(8,128)(2,1)S(1)} %get-tuple-element.49), channel_id=1, source_target_pairs={{0,8},{1,9},{2,10},{3,11},{4,12},{5,13},{6,14},{7,15},{8,0},{9,1},... | collective-permute-start | bytes 344072 | tf_op jit(solution)/shard_map/ppermute | solution.py:24
  62.6 2.8 %collective-permute-start.14 = (bf16[8,7168]{1,0:T(8,128)(2,1)S(1)}, bf16[8,7168]{1,0:T(8,128)(2,1)S(1)}, u32[]{:S(2)}, u32[]{:S(2)}) collective-permute-start(bf16[8,7168]{1,0:T(8,128)(2,1)S(1)} %get-tuple-element.50), channel_id=1, source_target_pairs={{0,10},{1,11},{2,8},{3,9},{4,14},{5,15},{6,12},{7,13},{8,2},{9,3},... | collective-permute-start | bytes 344072 | tf_op jit(solution)/shard_map/ppermute | solution.py:24
  65.4 1.6 %collective-permute-start.15 = (bf16[8,7168]{1,0:T(8,128)(2,1)S(1)}, bf16[8,7168]{1,0:T(8,128)(2,1)S(1)}, u32[]{:S(2)}, u32[]{:S(2)}) collective-permute-start(bf16[8,7168]{1,0:T(8,128)(2,1)S(1)} %get-tuple-element.51), channel_id=1, source_target_pairs={{0,12},{1,13},{2,14},{3,15},{4,8},{5,9},{6,10},{7,11},{8,4},{9,5},... | collective-permute-start | bytes 344072 | tf_op jit(solution)/shard_map/ppermute | solution.py:24
  67.0 0.4 collective-permute-start.16
  67.4 1.2 %collective-permute-done.12.refs_3_ = bf16[8,7168]{1,0:T(8,128)(2,1)S(1)} collective-permute-done((bf16[8,7168]{1,0:T(8,128)(2,1)S(1)}, bf16[8,7168]{1,0:T(8,128)(2,1)S(1)}, u32[]{:S(2)}, u32[]{:S(2)}) %collective-permute-start.12) | collective-permute-done | bytes 114720 | tf_op jit(solution)/shard_map/ppermute | solution.py:24
  68.6 3.0 %collective-permute-done.13.refs_4_ = bf16[8,7168]{1,0:T(8,128)(2,1)S(1)} collective-permute-done((bf16[8,7168]{1,0:T(8,128)(2,1)S(1)}, bf16[8,7168]{1,0:T(8,128)(2,1)S(1)}, u32[]{:S(2)}, u32[]{:S(2)}) %collective-permute-start.13) | collective-permute-done | bytes 114720 | tf_op jit(solution)/shard_map/ppermute | solution.py:24
  71.6 6.4 %collective-permute-done.14.refs_5_ = bf16[8,7168]{1,0:T(8,128)(2,1)S(1)} collective-permute-done((bf16[8,7168]{1,0:T(8,128)(2,1)S(1)}, bf16[8,7168]{1,0:T(8,128)(2,1)S(1)}, u32[]{:S(2)}, u32[]{:S(2)}) %collective-permute-start.14) | collective-permute-done | bytes 114720 | tf_op jit(solution)/shard_map/ppermute | solution.py:24
  78.0 4.5 %collective-permute-done.15.refs_6_ = bf16[8,7168]{1,0:T(8,128)(2,1)S(1)} collective-permute-done((bf16[8,7168]{1,0:T(8,128)(2,1)S(1)}, bf16[8,7168]{1,0:T(8,128)(2,1)S(1)}, u32[]{:S(2)}, u32[]{:S(2)}) %collective-permute-start.15) | collective-permute-done | bytes 114720 | tf_op jit(solution)/shard_map/ppermute | solution.py:24
  82.5 1.6 %collective-permute-done.16.refs_7_ = bf16[8,7168]{1,0:T(8,128)(2,1)S(1)} collective-permute-done((bf16[8,7168]{1,0:T(8,128)(2,1)S(1)}, bf16[8,7168]{1,0:T(8,128)(2,1)S(1)}, u32[]{:S(2)}, u32[]{:S(2)}) %collective-permute-start.16) | collective-permute-done | bytes 114720 | tf_op jit(solution)/shard_map/ppermute | solution.py:24
  84.1 1.0 %shard_map.70 = bf16[2,8,7168]{2,1,0:T(8,128)(2,1)} custom-call(bf16[64,16]{1,0:T(8,128)(2,1)S(1)} %get-tuple-element.29.after_ref.matrix_ref, bf16[8,7168]{1,0:T(8,128)(2,1)S(1)} %get-tuple-element.45.refs_0_, bf16[8,7168]{1,0:T(8,128)(2,1)S(1)} %collective-permute-done.10.refs_1_, bf16[8,7168]{1,0:T(8,128)(2,1)S(1)} %collective-permute-done.11.refs_2_, ...), custom_call_target="tpu_custom_call" | custom-call | flops 14680064 | bytes 1146880 | tf_op jit(solution)/shard_map/pallas_call | solution.py:329
  (9 shorter events, 0.1 us)
Async XLA Ops:
  1.6 7.4 %collective-permute-start.4 = (bf16[8,7296]{1,0:T(8,128)(2,1)S(1)}, bf16[8,7296]{1,0:T(8,128)(2,1)S(1)}, u32[]{:S(2)}, u32[]{:S(2)}) collective-permute-start(bf16[8,7296]{1,0:T(8,128)(2,1)S(1)} %get-tuple-element.35), channel_id=1, source_target_pairs={{0,2},{1,3},{2,0},{3,1},{4,6},{5,7},{6,4},{7,5},{8,10},{9,11},{10,... | collective-permute-start | bytes 350216 | tf_op jit(solution)/shard_map/ppermute | solution.py:24
  3.1 7.4 %collective-permute-start.5 = (bf16[8,7296]{1,0:T(8,128)(2,1)S(1)}, bf16[8,7296]{1,0:T(8,128)(2,1)S(1)}, u32[]{:S(2)}, u32[]{:S(2)}) collective-permute-start(bf16[8,7296]{1,0:T(8,128)(2,1)S(1)} %get-tuple-element.36), channel_id=1, source_target_pairs={{0,4},{1,5},{2,6},{3,7},{4,0},{5,1},{6,2},{7,3},{8,12},{9,13},{10,... | collective-permute-start | bytes 350216 | tf_op jit(solution)/shard_map/ppermute | solution.py:24
  3.6 13.3 %collective-permute-start = (bf16[8,7296]{1,0:T(8,128)(2,1)S(1)}, bf16[8,7296]{1,0:T(8,128)(2,1)S(1)}, u32[]{:S(2)}, u32[]{:S(2)}) collective-permute-start(bf16[8,7296]{1,0:T(8,128)(2,1)S(1)} %get-tuple-element.30), channel_id=1, source_target_pairs={{0,8},{1,9},{2,10},{3,11},{4,12},{5,13},{6,14},{7,15},{8,0},{9,1},... | collective-permute-start | bytes 350216 | tf_op jit(solution)/shard_map/ppermute | solution.py:24
  6.1 15.8 %collective-permute-start.1 = (bf16[8,7296]{1,0:T(8,128)(2,1)S(1)}, bf16[8,7296]{1,0:T(8,128)(2,1)S(1)}, u32[]{:S(2)}, u32[]{:S(2)}) collective-permute-start(bf16[8,7296]{1,0:T(8,128)(2,1)S(1)} %get-tuple-element.31), channel_id=1, source_target_pairs={{0,10},{1,11},{2,8},{3,9},{4,14},{5,15},{6,12},{7,13},{8,2},{9,3},... | collective-permute-start | bytes 350216 | tf_op jit(solution)/shard_map/ppermute | solution.py:24
  6.5 10.3 %collective-permute-start.6 = (bf16[8,7296]{1,0:T(8,128)(2,1)S(1)}, bf16[8,7296]{1,0:T(8,128)(2,1)S(1)}, u32[]{:S(2)}, u32[]{:S(2)}) collective-permute-start(bf16[8,7296]{1,0:T(8,128)(2,1)S(1)} %get-tuple-element.37), channel_id=1, source_target_pairs={{0,6},{1,7},{2,4},{3,5},{4,2},{5,3},{6,0},{7,1},{8,14},{9,15},{10,... | collective-permute-start | bytes 350216 | tf_op jit(solution)/shard_map/ppermute | solution.py:24
  9.0 16.0 %collective-permute-start.2 = (bf16[8,7296]{1,0:T(8,128)(2,1)S(1)}, bf16[8,7296]{1,0:T(8,128)(2,1)S(1)}, u32[]{:S(2)}, u32[]{:S(2)}) collective-permute-start(bf16[8,7296]{1,0:T(8,128)(2,1)S(1)} %get-tuple-element.32), channel_id=1, source_target_pairs={{0,12},{1,13},{2,14},{3,15},{4,8},{5,9},{6,10},{7,11},{8,4},{9,5},... | collective-permute-start | bytes 350216 | tf_op jit(solution)/shard_map/ppermute | solution.py:24
  10.5 15.9 %collective-permute-start.3 = (bf16[8,7296]{1,0:T(8,128)(2,1)S(1)}, bf16[8,7296]{1,0:T(8,128)(2,1)S(1)}, u32[]{:S(2)}, u32[]{:S(2)}) collective-permute-start(bf16[8,7296]{1,0:T(8,128)(2,1)S(1)} %get-tuple-element.33), channel_id=1, source_target_pairs={{0,14},{1,15},{2,12},{3,13},{4,10},{5,11},{6,8},{7,9},{8,6},{9,7},... | collective-permute-start | bytes 350216 | tf_op jit(solution)/shard_map/ppermute | solution.py:24
  26.5 2.8 %collective-permute-start.8 = (bf16[32,7296]{1,0:T(8,128)(2,1)S(1)}, bf16[32,7296]{1,0:T(8,128)(2,1)S(1)}, u32[]{:S(2)}, u32[]{:S(2)}) collective-permute-start(bf16[32,7296]{1,0:T(8,128)(2,1)S(1)} %shard_map.66.refs_1_), channel_id=1, source_target_pairs={{0,1},{1,0},{2,3},{3,2},{4,5},{5,4},{6,7},{7,6},{8,9},{9,8},{10,11... | collective-permute-start | bytes 1400840 | tf_op jit(solution)/shard_map/ppermute | solution.py:24
  26.6 2.8 %collective-permute-start.7 = (bf16[32,7296]{1,0:T(8,128)(2,1)S(1)}, bf16[32,7296]{1,0:T(8,128)(2,1)S(1)}, u32[]{:S(2)}, u32[]{:S(2)}) collective-permute-start(bf16[32,7296]{1,0:T(8,128)(2,1)S(1)} %shard_map.65.refs_0_), channel_id=1, source_target_pairs={{0,1},{1,0},{2,3},{3,2},{4,5},{5,4},{6,7},{7,6},{8,9},{9,8},{10,11... | collective-permute-start | bytes 1400840 | tf_op jit(solution)/shard_map/ppermute | solution.py:24
  55.2 2.5 %collective-permute-start.9 = (bf16[64,7168]{1,0:T(8,128)(2,1)S(1)}, bf16[64,7168]{1,0:T(8,128)(2,1)S(1)}, u32[]{:S(2)}, u32[]{:S(2)}) collective-permute-start(bf16[64,7168]{1,0:T(8,128)(2,1)S(1)} %get-tuple-element.44), channel_id=1, source_target_pairs={{0,1},{1,0},{2,3},{3,2},{4,5},{5,4},{6,7},{7,6},{8,9},{9,8},{10,11... | collective-permute-start | bytes 2752520 | tf_op jit(solution)/shard_map/ppermute | solution.py:24
  58.0 7.4 %collective-permute-start.10 = (bf16[8,7168]{1,0:T(8,128)(2,1)S(1)}, bf16[8,7168]{1,0:T(8,128)(2,1)S(1)}, u32[]{:S(2)}, u32[]{:S(2)}) collective-permute-start(bf16[8,7168]{1,0:T(8,128)(2,1)S(1)} %get-tuple-element.46), channel_id=1, source_target_pairs={{0,2},{1,3},{2,0},{3,1},{4,6},{5,7},{6,4},{7,5},{8,10},{9,11},{10,... | collective-permute-start | bytes 344072 | tf_op jit(solution)/shard_map/ppermute | solution.py:24
  59.6 7.4 %collective-permute-start.11 = (bf16[8,7168]{1,0:T(8,128)(2,1)S(1)}, bf16[8,7168]{1,0:T(8,128)(2,1)S(1)}, u32[]{:S(2)}, u32[]{:S(2)}) collective-permute-start(bf16[8,7168]{1,0:T(8,128)(2,1)S(1)} %get-tuple-element.47), channel_id=1, source_target_pairs={{0,4},{1,5},{2,6},{3,7},{4,0},{5,1},{6,2},{7,3},{8,12},{9,13},{10,... | collective-permute-start | bytes 344072 | tf_op jit(solution)/shard_map/ppermute | solution.py:24
  59.6 9.0 %collective-permute-start.12 = (bf16[8,7168]{1,0:T(8,128)(2,1)S(1)}, bf16[8,7168]{1,0:T(8,128)(2,1)S(1)}, u32[]{:S(2)}, u32[]{:S(2)}) collective-permute-start(bf16[8,7168]{1,0:T(8,128)(2,1)S(1)} %get-tuple-element.48), channel_id=1, source_target_pairs={{0,6},{1,7},{2,4},{3,5},{4,2},{5,3},{6,0},{7,1},{8,14},{9,15},{10,... | collective-permute-start | bytes 344072 | tf_op jit(solution)/shard_map/ppermute | solution.py:24
  61.6 10.1 %collective-permute-start.13 = (bf16[8,7168]{1,0:T(8,128)(2,1)S(1)}, bf16[8,7168]{1,0:T(8,128)(2,1)S(1)}, u32[]{:S(2)}, u32[]{:S(2)}) collective-permute-start(bf16[8,7168]{1,0:T(8,128)(2,1)S(1)} %get-tuple-element.49), channel_id=1, source_target_pairs={{0,8},{1,9},{2,10},{3,11},{4,12},{5,13},{6,14},{7,15},{8,0},{9,1},... | collective-permute-start | bytes 344072 | tf_op jit(solution)/shard_map/ppermute | solution.py:24
  62.6 15.4 %collective-permute-start.14 = (bf16[8,7168]{1,0:T(8,128)(2,1)S(1)}, bf16[8,7168]{1,0:T(8,128)(2,1)S(1)}, u32[]{:S(2)}, u32[]{:S(2)}) collective-permute-start(bf16[8,7168]{1,0:T(8,128)(2,1)S(1)} %get-tuple-element.50), channel_id=1, source_target_pairs={{0,10},{1,11},{2,8},{3,9},{4,14},{5,15},{6,12},{7,13},{8,2},{9,3},... | collective-permute-start | bytes 344072 | tf_op jit(solution)/shard_map/ppermute | solution.py:24
  65.4 17.1 %collective-permute-start.15 = (bf16[8,7168]{1,0:T(8,128)(2,1)S(1)}, bf16[8,7168]{1,0:T(8,128)(2,1)S(1)}, u32[]{:S(2)}, u32[]{:S(2)}) collective-permute-start(bf16[8,7168]{1,0:T(8,128)(2,1)S(1)} %get-tuple-element.51), channel_id=1, source_target_pairs={{0,12},{1,13},{2,14},{3,15},{4,8},{5,9},{6,10},{7,11},{8,4},{9,5},... | collective-permute-start | bytes 344072 | tf_op jit(solution)/shard_map/ppermute | solution.py:24
  67.0 17.0 %collective-permute-start.16 = (bf16[8,7168]{1,0:T(8,128)(2,1)S(1)}, bf16[8,7168]{1,0:T(8,128)(2,1)S(1)}, u32[]{:S(2)}, u32[]{:S(2)}) collective-permute-start(bf16[8,7168]{1,0:T(8,128)(2,1)S(1)} %get-tuple-element.52), channel_id=1, source_target_pairs={{0,14},{1,15},{2,12},{3,13},{4,10},{5,11},{6,8},{7,9},{8,6},{9,7},... | collective-permute-start | bytes 344072 | tf_op jit(solution)/shard_map/ppermute | solution.py:24

commit v7 on v6

--- a/solution.py
+++ b/solution.py
@@ -15,7 +15,7 @@
 AHEAD = 4
 SMALL = 8 << 20
 SLACK = 1 << 20
-FETCHED = 2
+FETCHED = 1
 ORDER = (7, 6, 5, 4, 3, 2, 1)
 
 

time: 85.2 us -> 85.5 us (level)
  transfers between devices with their start and end apart: 17 -> 17, of which waited for: 10 -> 11; matrix products, arithmetic and copies ran while one was open for 0% -> 0% of each run, Pallas kernels for 3% -> 2%
where the time goes in v7:
time: 85.5 us; the launch traced here: 85.3 us
  waiting for transfers between devices  34.8 us (41%)
  Pallas kernels  30.9 us (36%)
  starting transfers between devices  19.6 us (23%)
    ppermute x17, waiting for transfers between devices, exchanged(): lax.ppermute(shard, 'grp', [(i, (i // unit ^ by) * unit + i % unit) for i...  34.8 us
    pallas_call x1, Pallas kernels, body(): call(functools.partial(expert_kernel, len(parts), topk), [bf16(half, widt...  26.5 us
    ppermute x17, starting transfers between devices, exchanged(): lax.ppermute(shard, 'grp', [(i, (i // unit ^ by) * unit + i % unit) for i...  19.6 us
  transfers between devices with their start and end apart: 17, of which 11 were waited for; matrix products, arithmetic and copies ran while one was open for 0% of the time, Pallas kernels for 2%

profile of v7, /device:TPU:12, one launch (start us, length us, event | category | flops | bytes accessed | tf_op | source)
XLA Modules:
  0.0 85.3 jit_solution(3035560286212563472)
XLA Ops:
  0.0 1.5 %shard_map.64 = (bf16[64,16]{1,0:T(8,128)(2,1)S(1)}, bf16[8,7296]{1,0:T(8,128)(2,1)S(1)}, bf16[8,7296]{1,0:T(8,128)(2,1)S(1)}, bf16[8,7296]{1,0:T(8,128)(2,1)S(1...) custom-call(s32[1]{0:T(128)} %bitcast.group_ref, ...), custom_call_target="tpu_custom_call" | custom-call | flops 14942208 | bytes 1167360 | tf_op jit(solution)/shard_map/pallas_call | solution.py:247
  1.6 1.6 %collective-permute-start.4 = (bf16[8,7296]{1,0:T(8,128)(2,1)S(1)}, bf16[8,7296]{1,0:T(8,128)(2,1)S(1)}, u32[]{:S(2)}, u32[]{:S(2)}) collective-permute-start(bf16[8,7296]{1,0:T(8,128)(2,1)S(1)} %get-tuple-element.35), channel_id=1, source_target_pairs={{0,2},{1,3},{2,0},{3,1},{4,6},{5,7},{6,4},{7,5},{8,10},{9,11},{10,... | collective-permute-start | bytes 350216 | tf_op jit(solution)/shard_map/ppermute | solution.py:24
  3.1 0.4 collective-permute-start.5
  3.6 2.6 %collective-permute-start = (bf16[8,7296]{1,0:T(8,128)(2,1)S(1)}, bf16[8,7296]{1,0:T(8,128)(2,1)S(1)}, u32[]{:S(2)}, u32[]{:S(2)}) collective-permute-start(bf16[8,7296]{1,0:T(8,128)(2,1)S(1)} %get-tuple-element.30), channel_id=1, source_target_pairs={{0,8},{1,9},{2,10},{3,11},{4,12},{5,13},{6,14},{7,15},{8,0},{9,1},... | collective-permute-start | bytes 350216 | tf_op jit(solution)/shard_map/ppermute | solution.py:24
  6.1 0.3 collective-permute-start.1
  6.5 2.5 %collective-permute-start.6 = (bf16[8,7296]{1,0:T(8,128)(2,1)S(1)}, bf16[8,7296]{1,0:T(8,128)(2,1)S(1)}, u32[]{:S(2)}, u32[]{:S(2)}) collective-permute-start(bf16[8,7296]{1,0:T(8,128)(2,1)S(1)} %get-tuple-element.37), channel_id=1, source_target_pairs={{0,6},{1,7},{2,4},{3,5},{4,2},{5,3},{6,0},{7,1},{8,14},{9,15},{10,... | collective-permute-start | bytes 350216 | tf_op jit(solution)/shard_map/ppermute | solution.py:24
  9.0 1.6 %collective-permute-start.2 = (bf16[8,7296]{1,0:T(8,128)(2,1)S(1)}, bf16[8,7296]{1,0:T(8,128)(2,1)S(1)}, u32[]{:S(2)}, u32[]{:S(2)}) collective-permute-start(bf16[8,7296]{1,0:T(8,128)(2,1)S(1)} %get-tuple-element.32), channel_id=1, source_target_pairs={{0,12},{1,13},{2,14},{3,15},{4,8},{5,9},{6,10},{7,11},{8,4},{9,5},... | collective-permute-start | bytes 350216 | tf_op jit(solution)/shard_map/ppermute | solution.py:24
  10.5 0.4 collective-permute-start.3
  11.0 5.8 %collective-permute-done.6.refs_3_ = bf16[8,7296]{1,0:T(8,128)(2,1)S(1)} collective-permute-done((bf16[8,7296]{1,0:T(8,128)(2,1)S(1)}, bf16[8,7296]{1,0:T(8,128)(2,1)S(1)}, u32[]{:S(2)}, u32[]{:S(2)}) %collective-permute-start.6) | collective-permute-done | bytes 116768 | tf_op jit(solution)/shard_map/ppermute | solution.py:24
  16.8 5.1 %collective-permute-done.1.refs_1_ = bf16[8,7296]{1,0:T(8,128)(2,1)S(1)} collective-permute-done((bf16[8,7296]{1,0:T(8,128)(2,1)S(1)}, bf16[8,7296]{1,0:T(8,128)(2,1)S(1)}, u32[]{:S(2)}, u32[]{:S(2)}) %collective-permute-start.1) | collective-permute-done | bytes 116768 | tf_op jit(solution)/shard_map/ppermute | solution.py:24
  22.0 3.0 %collective-permute-done.2.refs_2_ = bf16[8,7296]{1,0:T(8,128)(2,1)S(1)} collective-permute-done((bf16[8,7296]{1,0:T(8,128)(2,1)S(1)}, bf16[8,7296]{1,0:T(8,128)(2,1)S(1)}, u32[]{:S(2)}, u32[]{:S(2)}) %collective-permute-start.2) | collective-permute-done | bytes 116768 | tf_op jit(solution)/shard_map/ppermute | solution.py:24
  25.0 1.5 %collective-permute-done.3.refs_3_ = bf16[8,7296]{1,0:T(8,128)(2,1)S(1)} collective-permute-done((bf16[8,7296]{1,0:T(8,128)(2,1)S(1)}, bf16[8,7296]{1,0:T(8,128)(2,1)S(1)}, u32[]{:S(2)}, u32[]{:S(2)}) %collective-permute-start.3) | collective-permute-done | bytes 116768 | tf_op jit(solution)/shard_map/ppermute | solution.py:24
  26.5 0.1 collective-permute-start.8
  26.6 0.5 collective-permute-start.7
  27.1 1.6 %shard_map.67.refs_4_ = bf16[512,2048]{1,0:T(8,128)(2,1)S(1)} custom-call(bf16[64,16]{1,0:T(8,128)(2,1)S(1)} %get-tuple-element.29.after_ref.matrix_ref, bf16[1,7168,2048]{2,1,0:T(8,128)(2,1)} %refs_5_.1), custom_call_target="tpu_custom_call" | custom-call | bytes 4194304 | tf_op jit(solution)/shard_map/pallas_call | solution.py:269
  28.7 0.4 collective-permute-done.7.refs_2_
  29.1 26.5 %shard_map.68 = (bf16[64,7168]{1,0:T(8,128)(2,1)S(1)}, bf16[64,7168]{1,0:T(8,128)(2,1)S(1)}) custom-call(s32[1]{0:T(128)} %bitcast.3.expert_ref, bf16[32,7296]{1,0:T(8,128)(2,1)S(1)} %shard_map.65.refs_0_, bf16[32,7296]{1,0:T(8,128)(2,1)S(1)} %shard_map.66.refs_1_, bf16[32,7296]{1,0:T(8,128)(2,1)S(1)} %collective-permute-done.7.refs_2_, ...), custom_call_target="tpu_custom_call" | custom-call | flops 11274289152 | bytes 58720256 | tf_op jit(solution)/shard_map/pallas_call | solution.py:297
  55.6 0.2 collective-permute-start.9
  55.8 2.3 %collective-permute-done.9.got_ref = bf16[64,7168]{1,0:T(8,128)(2,1)S(1)} collective-permute-done((bf16[64,7168]{1,0:T(8,128)(2,1)S(1)}, bf16[64,7168]{1,0:T(8,128)(2,1)S(1)}, u32[]{:S(2)}, u32[]{:S(2)}) %collective-permute-start.9) | collective-permute-done | bytes 917536 | tf_op jit(solution)/shard_map/ppermute | solution.py:24
  58.1 0.2 shard_map.69
  58.3 1.6 %collective-permute-start.10 = (bf16[8,7168]{1,0:T(8,128)(2,1)S(1)}, bf16[8,7168]{1,0:T(8,128)(2,1)S(1)}, u32[]{:S(2)}, u32[]{:S(2)}) collective-permute-start(bf16[8,7168]{1,0:T(8,128)(2,1)S(1)} %get-tuple-element.46), channel_id=1, source_target_pairs={{0,2},{1,3},{2,0},{3,1},{4,6},{5,7},{6,4},{7,5},{8,10},{9,11},{10,... | collective-permute-start | bytes 344072 | tf_op jit(solution)/shard_map/ppermute | solution.py:24
  59.9 2.0 %collective-permute-start.12 = (bf16[8,7168]{1,0:T(8,128)(2,1)S(1)}, bf16[8,7168]{1,0:T(8,128)(2,1)S(1)}, u32[]{:S(2)}, u32[]{:S(2)}) collective-permute-start(bf16[8,7168]{1,0:T(8,128)(2,1)S(1)} %get-tuple-element.48), channel_id=1, source_target_pairs={{0,6},{1,7},{2,4},{3,5},{4,2},{5,3},{6,0},{7,1},{8,14},{9,15},{10,... | collective-permute-start | bytes 344072 | tf_op jit(solution)/shard_map/ppermute | solution.py:24
  61.9 1.1 %collective-permute-start.13 = (bf16[8,7168]{1,0:T(8,128)(2,1)S(1)}, bf16[8,7168]{1,0:T(8,128)(2,1)S(1)}, u32[]{:S(2)}, u32[]{:S(2)}) collective-permute-start(bf16[8,7168]{1,0:T(8,128)(2,1)S(1)} %get-tuple-element.49), channel_id=1, source_target_pairs={{0,8},{1,9},{2,10},{3,11},{4,12},{5,13},{6,14},{7,15},{8,0},{9,1},... | collective-permute-start | bytes 344072 | tf_op jit(solution)/shard_map/ppermute | solution.py:24
  62.9 2.8 %collective-permute-start.14 = (bf16[8,7168]{1,0:T(8,128)(2,1)S(1)}, bf16[8,7168]{1,0:T(8,128)(2,1)S(1)}, u32[]{:S(2)}, u32[]{:S(2)}) collective-permute-start(bf16[8,7168]{1,0:T(8,128)(2,1)S(1)} %get-tuple-element.50), channel_id=1, source_target_pairs={{0,10},{1,11},{2,8},{3,9},{4,14},{5,15},{6,12},{7,13},{8,2},{9,3},... | collective-permute-start | bytes 344072 | tf_op jit(solution)/shard_map/ppermute | solution.py:24
  65.7 1.6 %collective-permute-start.15 = (bf16[8,7168]{1,0:T(8,128)(2,1)S(1)}, bf16[8,7168]{1,0:T(8,128)(2,1)S(1)}, u32[]{:S(2)}, u32[]{:S(2)}) collective-permute-start(bf16[8,7168]{1,0:T(8,128)(2,1)S(1)} %get-tuple-element.51), channel_id=1, source_target_pairs={{0,12},{1,13},{2,14},{3,15},{4,8},{5,9},{6,10},{7,11},{8,4},{9,5},... | collective-permute-start | bytes 344072 | tf_op jit(solution)/shard_map/ppermute | solution.py:24
  67.3 0.4 collective-permute-start.16
  67.7 1.2 %collective-permute-done.12.refs_3_ = bf16[8,7168]{1,0:T(8,128)(2,1)S(1)} collective-permute-done((bf16[8,7168]{1,0:T(8,128)(2,1)S(1)}, bf16[8,7168]{1,0:T(8,128)(2,1)S(1)}, u32[]{:S(2)}, u32[]{:S(2)}) %collective-permute-start.12) | collective-permute-done | bytes 114720 | tf_op jit(solution)/shard_map/ppermute | solution.py:24
  68.9 3.0 %collective-permute-done.13.refs_4_ = bf16[8,7168]{1,0:T(8,128)(2,1)S(1)} collective-permute-done((bf16[8,7168]{1,0:T(8,128)(2,1)S(1)}, bf16[8,7168]{1,0:T(8,128)(2,1)S(1)}, u32[]{:S(2)}, u32[]{:S(2)}) %collective-permute-start.13) | collective-permute-done | bytes 114720 | tf_op jit(solution)/shard_map/ppermute | solution.py:24
  71.9 6.4 %collective-permute-done.14.refs_5_ = bf16[8,7168]{1,0:T(8,128)(2,1)S(1)} collective-permute-done((bf16[8,7168]{1,0:T(8,128)(2,1)S(1)}, bf16[8,7168]{1,0:T(8,128)(2,1)S(1)}, u32[]{:S(2)}, u32[]{:S(2)}) %collective-permute-start.14) | collective-permute-done | bytes 114720 | tf_op jit(solution)/shard_map/ppermute | solution.py:24
  78.3 4.5 %collective-permute-done.15.refs_6_ = bf16[8,7168]{1,0:T(8,128)(2,1)S(1)} collective-permute-done((bf16[8,7168]{1,0:T(8,128)(2,1)S(1)}, bf16[8,7168]{1,0:T(8,128)(2,1)S(1)}, u32[]{:S(2)}, u32[]{:S(2)}) %collective-permute-start.15) | collective-permute-done | bytes 114720 | tf_op jit(solution)/shard_map/ppermute | solution.py:24
  82.8 1.6 %collective-permute-done.16.refs_7_ = bf16[8,7168]{1,0:T(8,128)(2,1)S(1)} collective-permute-done((bf16[8,7168]{1,0:T(8,128)(2,1)S(1)}, bf16[8,7168]{1,0:T(8,128)(2,1)S(1)}, u32[]{:S(2)}, u32[]{:S(2)}) %collective-permute-start.16) | collective-permute-done | bytes 114720 | tf_op jit(solution)/shard_map/ppermute | solution.py:24
  84.4 1.0 %shard_map.70 = bf16[2,8,7168]{2,1,0:T(8,128)(2,1)} custom-call(bf16[64,16]{1,0:T(8,128)(2,1)S(1)} %get-tuple-element.29.after_ref.matrix_ref, bf16[8,7168]{1,0:T(8,128)(2,1)S(1)} %get-tuple-element.45.refs_0_, bf16[8,7168]{1,0:T(8,128)(2,1)S(1)} %collective-permute-done.10.refs_1_, bf16[8,7168]{1,0:T(8,128)(2,1)S(1)} %collective-permute-done.11.refs_2_, ...), custom_call_target="tpu_custom_call" | custom-call | flops 14680064 | bytes 1146880 | tf_op jit(solution)/shard_map/pallas_call | solution.py:329
  (9 shorter events, 0.1 us)
Async XLA Ops:
  1.6 7.4 %collective-permute-start.4 = (bf16[8,7296]{1,0:T(8,128)(2,1)S(1)}, bf16[8,7296]{1,0:T(8,128)(2,1)S(1)}, u32[]{:S(2)}, u32[]{:S(2)}) collective-permute-start(bf16[8,7296]{1,0:T(8,128)(2,1)S(1)} %get-tuple-element.35), channel_id=1, source_target_pairs={{0,2},{1,3},{2,0},{3,1},{4,6},{5,7},{6,4},{7,5},{8,10},{9,11},{10,... | collective-permute-start | bytes 350216 | tf_op jit(solution)/shard_map/ppermute | solution.py:24
  3.1 7.4 %collective-permute-start.5 = (bf16[8,7296]{1,0:T(8,128)(2,1)S(1)}, bf16[8,7296]{1,0:T(8,128)(2,1)S(1)}, u32[]{:S(2)}, u32[]{:S(2)}) collective-permute-start(bf16[8,7296]{1,0:T(8,128)(2,1)S(1)} %get-tuple-element.36), channel_id=1, source_target_pairs={{0,4},{1,5},{2,6},{3,7},{4,0},{5,1},{6,2},{7,3},{8,12},{9,13},{10,... | collective-permute-start | bytes 350216 | tf_op jit(solution)/shard_map/ppermute | solution.py:24
  3.6 13.3 %collective-permute-start = (bf16[8,7296]{1,0:T(8,128)(2,1)S(1)}, bf16[8,7296]{1,0:T(8,128)(2,1)S(1)}, u32[]{:S(2)}, u32[]{:S(2)}) collective-permute-start(bf16[8,7296]{1,0:T(8,128)(2,1)S(1)} %get-tuple-element.30), channel_id=1, source_target_pairs={{0,8},{1,9},{2,10},{3,11},{4,12},{5,13},{6,14},{7,15},{8,0},{9,1},... | collective-permute-start | bytes 350216 | tf_op jit(solution)/shard_map/ppermute | solution.py:24
  6.1 15.8 %collective-permute-start.1 = (bf16[8,7296]{1,0:T(8,128)(2,1)S(1)}, bf16[8,7296]{1,0:T(8,128)(2,1)S(1)}, u32[]{:S(2)}, u32[]{:S(2)}) collective-permute-start(bf16[8,7296]{1,0:T(8,128)(2,1)S(1)} %get-tuple-element.31), channel_id=1, source_target_pairs={{0,10},{1,11},{2,8},{3,9},{4,14},{5,15},{6,12},{7,13},{8,2},{9,3},... | collective-permute-start | bytes 350216 | tf_op jit(solution)/shard_map/ppermute | solution.py:24
  6.5 10.3 %collective-permute-start.6 = (bf16[8,7296]{1,0:T(8,128)(2,1)S(1)}, bf16[8,7296]{1,0:T(8,128)(2,1)S(1)}, u32[]{:S(2)}, u32[]{:S(2)}) collective-permute-start(bf16[8,7296]{1,0:T(8,128)(2,1)S(1)} %get-tuple-element.37), channel_id=1, source_target_pairs={{0,6},{1,7},{2,4},{3,5},{4,2},{5,3},{6,0},{7,1},{8,14},{9,15},{10,... | collective-permute-start | bytes 350216 | tf_op jit(solution)/shard_map/ppermute | solution.py:24
  9.0 16.0 %collective-permute-start.2 = (bf16[8,7296]{1,0:T(8,128)(2,1)S(1)}, bf16[8,7296]{1,0:T(8,128)(2,1)S(1)}, u32[]{:S(2)}, u32[]{:S(2)}) collective-permute-start(bf16[8,7296]{1,0:T(8,128)(2,1)S(1)} %get-tuple-element.32), channel_id=1, source_target_pairs={{0,12},{1,13},{2,14},{3,15},{4,8},{5,9},{6,10},{7,11},{8,4},{9,5},... | collective-permute-start | bytes 350216 | tf_op jit(solution)/shard_map/ppermute | solution.py:24
  10.5 15.9 %collective-permute-start.3 = (bf16[8,7296]{1,0:T(8,128)(2,1)S(1)}, bf16[8,7296]{1,0:T(8,128)(2,1)S(1)}, u32[]{:S(2)}, u32[]{:S(2)}) collective-permute-start(bf16[8,7296]{1,0:T(8,128)(2,1)S(1)} %get-tuple-element.33), channel_id=1, source_target_pairs={{0,14},{1,15},{2,12},{3,13},{4,10},{5,11},{6,8},{7,9},{8,6},{9,7},... | collective-permute-start | bytes 350216 | tf_op jit(solution)/shard_map/ppermute | solution.py:24
  26.5 2.2 %collective-permute-start.8 = (bf16[32,7296]{1,0:T(8,128)(2,1)S(1)}, bf16[32,7296]{1,0:T(8,128)(2,1)S(1)}, u32[]{:S(2)}, u32[]{:S(2)}) collective-permute-start(bf16[32,7296]{1,0:T(8,128)(2,1)S(1)} %shard_map.66.refs_1_), channel_id=1, source_target_pairs={{0,1},{1,0},{2,3},{3,2},{4,5},{5,4},{6,7},{7,6},{8,9},{9,8},{10,11... | collective-permute-start | bytes 1400840 | tf_op jit(solution)/shard_map/ppermute | solution.py:24
  26.6 2.5 %collective-permute-start.7 = (bf16[32,7296]{1,0:T(8,128)(2,1)S(1)}, bf16[32,7296]{1,0:T(8,128)(2,1)S(1)}, u32[]{:S(2)}, u32[]{:S(2)}) collective-permute-start(bf16[32,7296]{1,0:T(8,128)(2,1)S(1)} %shard_map.65.refs_0_), channel_id=1, source_target_pairs={{0,1},{1,0},{2,3},{3,2},{4,5},{5,4},{6,7},{7,6},{8,9},{9,8},{10,11... | collective-permute-start | bytes 1400840 | tf_op jit(solution)/shard_map/ppermute | solution.py:24
  55.6 2.5 %collective-permute-start.9 = (bf16[64,7168]{1,0:T(8,128)(2,1)S(1)}, bf16[64,7168]{1,0:T(8,128)(2,1)S(1)}, u32[]{:S(2)}, u32[]{:S(2)}) collective-permute-start(bf16[64,7168]{1,0:T(8,128)(2,1)S(1)} %get-tuple-element.44), channel_id=1, source_target_pairs={{0,1},{1,0},{2,3},{3,2},{4,5},{5,4},{6,7},{7,6},{8,9},{9,8},{10,11... | collective-permute-start | bytes 2752520 | tf_op jit(solution)/shard_map/ppermute | solution.py:24
  58.3 7.4 %collective-permute-start.10 = (bf16[8,7168]{1,0:T(8,128)(2,1)S(1)}, bf16[8,7168]{1,0:T(8,128)(2,1)S(1)}, u32[]{:S(2)}, u32[]{:S(2)}) collective-permute-start(bf16[8,7168]{1,0:T(8,128)(2,1)S(1)} %get-tuple-element.46), channel_id=1, source_target_pairs={{0,2},{1,3},{2,0},{3,1},{4,6},{5,7},{6,4},{7,5},{8,10},{9,11},{10,... | collective-permute-start | bytes 344072 | tf_op jit(solution)/shard_map/ppermute | solution.py:24
  59.9 7.4 %collective-permute-start.11 = (bf16[8,7168]{1,0:T(8,128)(2,1)S(1)}, bf16[8,7168]{1,0:T(8,128)(2,1)S(1)}, u32[]{:S(2)}, u32[]{:S(2)}) collective-permute-start(bf16[8,7168]{1,0:T(8,128)(2,1)S(1)} %get-tuple-element.47), channel_id=1, source_target_pairs={{0,4},{1,5},{2,6},{3,7},{4,0},{5,1},{6,2},{7,3},{8,12},{9,13},{10,... | collective-permute-start | bytes 344072 | tf_op jit(solution)/shard_map/ppermute | solution.py:24
  59.9 9.0 %collective-permute-start.12 = (bf16[8,7168]{1,0:T(8,128)(2,1)S(1)}, bf16[8,7168]{1,0:T(8,128)(2,1)S(1)}, u32[]{:S(2)}, u32[]{:S(2)}) collective-permute-start(bf16[8,7168]{1,0:T(8,128)(2,1)S(1)} %get-tuple-element.48), channel_id=1, source_target_pairs={{0,6},{1,7},{2,4},{3,5},{4,2},{5,3},{6,0},{7,1},{8,14},{9,15},{10,... | collective-permute-start | bytes 344072 | tf_op jit(solution)/shard_map/ppermute | solution.py:24
  61.9 10.1 %collective-permute-start.13 = (bf16[8,7168]{1,0:T(8,128)(2,1)S(1)}, bf16[8,7168]{1,0:T(8,128)(2,1)S(1)}, u32[]{:S(2)}, u32[]{:S(2)}) collective-permute-start(bf16[8,7168]{1,0:T(8,128)(2,1)S(1)} %get-tuple-element.49), channel_id=1, source_target_pairs={{0,8},{1,9},{2,10},{3,11},{4,12},{5,13},{6,14},{7,15},{8,0},{9,1},... | collective-permute-start | bytes 344072 | tf_op jit(solution)/shard_map/ppermute | solution.py:24
  62.9 15.4 %collective-permute-start.14 = (bf16[8,7168]{1,0:T(8,128)(2,1)S(1)}, bf16[8,7168]{1,0:T(8,128)(2,1)S(1)}, u32[]{:S(2)}, u32[]{:S(2)}) collective-permute-start(bf16[8,7168]{1,0:T(8,128)(2,1)S(1)} %get-tuple-element.50), channel_id=1, source_target_pairs={{0,10},{1,11},{2,8},{3,9},{4,14},{5,15},{6,12},{7,13},{8,2},{9,3},... | collective-permute-start | bytes 344072 | tf_op jit(solution)/shard_map/ppermute | solution.py:24
  65.7 17.1 %collective-permute-start.15 = (bf16[8,7168]{1,0:T(8,128)(2,1)S(1)}, bf16[8,7168]{1,0:T(8,128)(2,1)S(1)}, u32[]{:S(2)}, u32[]{:S(2)}) collective-permute-start(bf16[8,7168]{1,0:T(8,128)(2,1)S(1)} %get-tuple-element.51), channel_id=1, source_target_pairs={{0,12},{1,13},{2,14},{3,15},{4,8},{5,9},{6,10},{7,11},{8,4},{9,5},... | collective-permute-start | bytes 344072 | tf_op jit(solution)/shard_map/ppermute | solution.py:24
  67.3 17.0 %collective-permute-start.16 = (bf16[8,7168]{1,0:T(8,128)(2,1)S(1)}, bf16[8,7168]{1,0:T(8,128)(2,1)S(1)}, u32[]{:S(2)}, u32[]{:S(2)}) collective-permute-start(bf16[8,7168]{1,0:T(8,128)(2,1)S(1)} %get-tuple-element.52), channel_id=1, source_target_pairs={{0,14},{1,15},{2,12},{3,13},{4,10},{5,11},{6,8},{7,9},{8,6},{9,7},... | collective-permute-start | bytes 344072 | tf_op jit(solution)/shard_map/ppermute | solution.py:24
